TPU v7x, 512 devices: a whole 4x4x16 slice. The times are simulated.
512 devices in a mesh: bead: 32 (over x, z_hi, y), space: 16 (over z_lo, core).
Axes of the slice: x: 4, y: 4, z: 16 (z_hi: 2, z_lo: 8; z = z_hi * 8 + z_lo), core: 2. Of those that a mesh axis runs over, the one named last changes fastest.
Arguments:
- positions: float32 [32, 3, 8192], P('bead', None, 'space'), may hold values from -3 to 3
- momenta: float32 [32, 3, 8192], P('bead', None, 'space'), may hold values from -6 to 6
- neighbours: int32 [32, 8192], P(None, 'space'), may hold values from 0 to 767, as said below
- ghost_rows: int32 [4096], P('space'), may hold values from 0 to 511
- species: int32 [8192], P('space'), may hold values from 0 to 1
- species_scale: float32 [2], replicated, may hold values from 0.5 to 2
- mass_table: float32 [2], replicated, may hold values from 0.25 to 1
- w_in: float32 [128, 8], replicated, may hold values from -2 to 2
- w_out: float32 [8, 128], replicated, may hold values from -0.5 to 0.5
Outputs:
- new_positions: float32 [32, 3, 8192], P('bead', None, 'space')
- new_momenta: float32 [32, 3, 8192], P('bead', None, 'space')
Inputs may be any that keep to these rules, and one draw needn't show every extreme that they name: `neighbours`: A neighbour entry indexes the window of its atom's domain; slots beyond an atom's live count hold the atom's own position 128 + (atom index mod 512); every atom has at least 8 live slots. `ghost_rows`: domain d's block is entries 2 * 128 * d to 2 * 128 * (d + 1) - 1; entries index atoms within domain d.
All inputs are finite; a program needn't handle non-finite values.
Results may differ from a plain program's by a relative error of at most 0.0003.
Values sent between devices are 32-bit elements; how exact they have to be, the bound alone decides.
No kernel may reach another device: no remote copies, remote signals or barrier semaphores. Data moves between devices by JAX's collectives and lax.ppermute only.
A program may use at most 64 MiB of HBM per device.

v0:
```python
import jax
import jax.numpy as jnp
import numpy as np
from jax import lax
from jax.sharding import PartitionSpec as P

BEADS = 32
CB = 4
NINNER = 3


polymer_freq = 10.0
outer_step = 6.0
pair_width = 1.0
pair_strength = 1.0
highest = lax.Precision.HIGHEST


def with_halo(block, sides, width):
    for axis, dim in sides:
        count = lax.axis_size(axis)
        forward = [(i, i + 1) for i in range(count - 1)]
        forward.append((count - 1, 0))
        backward = [(target, source) for source, target in forward]
        low = lax.ppermute(
            lax.slice_in_dim(block, block.shape[dim] - width, None, axis=dim), axis, forward
        )
        high = lax.ppermute(lax.slice_in_dim(block, 0, width, axis=dim), axis, backward)
        block = jnp.concatenate([low, block, high], axis=dim)
    return block


def from_everyone(shard, axis):
    size = lax.axis_size(axis)
    return lax.all_to_all(
        jnp.broadcast_to(shard[None], (size, *shard.shape)), axis, 0, 0, tiled=True
    )


def of_everyone(shard, axis):
    return from_everyone(shard, axis).sum(axis=0)


def laid_out(blocks, dim):
    blocks = jnp.moveaxis(blocks, 0, dim)
    lengths = blocks.shape
    return blocks.reshape(*lengths[:dim], lengths[dim] * lengths[dim + 1], *lengths[dim + 2 :])


def gather_directly(shard, axis, dim):
    return laid_out(from_everyone(shard, axis), dim)


def mode_matrix(count):
    beadpos = np.arange(count)[None, :]
    modeidx = np.arange(count)[:, None]
    middle = count // 2
    cosine = np.sqrt(2.0 / count) * np.cos(2.0 * np.pi * beadpos * modeidx / count)
    sine_rows = np.sqrt(2.0 / count) * np.sin(2.0 * np.pi * beadpos * modeidx / count)
    matrix = np.where(modeidx < middle, cosine, sine_rows)
    matrix = np.where(modeidx == 0, 1.0 / np.sqrt(count), matrix)
    matrix = np.where(modeidx == middle, np.cos(np.pi * beadpos) / np.sqrt(count), matrix)
    return matrix


def mode_scales(count, inner_step):
    frequency = 2.0 * polymer_freq * np.sin(np.pi * np.arange(count) / count)
    nonzero = np.where(frequency > 0, frequency, 1.0)
    cosine = np.cos(frequency * inner_step)
    drift_gain = np.where(frequency > 0, np.sin(frequency * inner_step) / nonzero, inner_step)
    spring = frequency * np.sin(frequency * inner_step)
    return (cosine, drift_gain, spring)


def polymer_tables(count, inner_step):
    modes = mode_matrix(count)
    cosine, drift_gain, spring = mode_scales(count, inner_step)
    persist = modes.T @ (cosine[:, None] * modes)
    coupling = modes.T @ (drift_gain[:, None] * modes)
    restoring = -(modes.T @ (spring[:, None] * modes))
    return (
        jnp.asarray(persist, jnp.float32),
        jnp.asarray(coupling, jnp.float32),
        jnp.asarray(restoring, jnp.float32),
    )


def contraction(count, fewer):
    full_modes = mode_matrix(count)
    small_modes = mode_matrix(fewer)
    kept = list(range(fewer // 2 + 1)) + list(range(count - fewer // 2 + 1, count))
    contract = np.sqrt(fewer / count) * (small_modes.T @ full_modes[kept])
    expand = count / fewer * contract.T
    return (jnp.asarray(contract, jnp.float32), jnp.asarray(expand, jnp.float32))


def radial_rates(count):
    return 0.2 * 2.0 ** (np.arange(count) / 2.0)


def species_lookup(species, table):
    kinds = jnp.arange(table.shape[0], dtype=jnp.int32)
    return jnp.sum(jnp.where(species[None, :] == kinds[:, None], table[:, None], 0.0), axis=0)


def pair_forces(extended, targets, centres):
    others = extended[:, targets]
    middle = extended[:, centres]
    offsets = others[:3] - middle[:3, None, :]
    squared = jnp.sum(offsets * offsets, axis=0)
    weights = others[3] * jnp.exp(-squared / pair_width)
    return pair_strength * middle[3] * jnp.sum(weights[None] * offsets, axis=1)


def learned_forces(extended, charges, targets, centres, w_in, w_out):
    live = (targets != centres[None, :]).astype(jnp.float32)
    weights = charges[targets] * live
    others = extended[:, targets]
    middle = extended[:, centres]
    offsets = others - middle[:, None, :]
    squared = jnp.sum(offsets * offsets, axis=0)
    rates = jnp.asarray(radial_rates(w_in.shape[1]), jnp.float32)
    basis = jnp.exp(-rates[:, None, None] * squared[None])
    message = jnp.sum(weights[None] * basis, axis=1) / targets.shape[0]
    hidden = jax.nn.silu(
        jnp.dot(w_in, message, precision=highest, preferred_element_type=jnp.float32)
    )
    radial = jnp.dot(w_out, hidden, precision=highest, preferred_element_type=jnp.float32)
    profile = jnp.sum(radial[:, None, :] * basis, axis=0)
    return jnp.sum((weights * profile)[None] * offsets, axis=1)


def body(
    positions, momenta, neighbours, ghost_rows, species, species_scale, mass_table, w_in, w_out
):
    per_device = positions.shape[0]
    atom_count = positions.shape[2]
    ghosts = ghost_rows.shape[0] // 2
    bead_devices = lax.axis_size("bead")
    device = lax.axis_index("bead")
    inner_step = outer_step / NINNER
    persist, coupling, restoring = polymer_tables(BEADS, inner_step)
    contract, expand = contraction(BEADS, CB)
    contract_mine = lax.dynamic_slice_in_dim(contract, device * per_device, per_device, 1)
    expand_mine = lax.dynamic_slice_in_dim(expand, device * per_device, per_device, 0)
    charges = species_lookup(species, species_scale)
    masses = species_lookup(species, mass_table)
    centres = ghosts + jnp.arange(atom_count, dtype=jnp.int32)
    charge_rows = charges[None, None, :]

    def cheap_forces(coords):
        stacked = jnp.concatenate([coords, charge_rows], axis=1)
        sends = stacked[:, :, ghost_rows]
        padded = with_halo(sends, (("space", 2),), ghosts)
        extended = jnp.concatenate(
            [padded[:, :, :ghosts], stacked, padded[:, :, 3 * ghosts :]], axis=2
        )
        forces = lax.map(lambda single: pair_forces(single, neighbours, centres), extended)
        return (forces, extended)

    def expensive_forces(coords, charge_window):
        partial_term = jnp.einsum("cb,bxa->cxa", contract_mine, coords, precision=highest)
        reduced = of_everyone(partial_term, "bead")
        sends = reduced[:, :, ghost_rows]
        padded = with_halo(sends, (("space", 2),), ghosts)
        extended = jnp.concatenate(
            [padded[:, :, :ghosts], reduced, padded[:, :, 3 * ghosts :]], axis=2
        )
        groups = bead_devices // CB
        share = atom_count // groups
        member = device // groups
        offset = device % groups * share
        chosen = lax.dynamic_index_in_dim(extended, member, 0, keepdims=False)
        targets = lax.dynamic_slice_in_dim(neighbours, offset, share, 1)
        middle = ghosts + offset + jnp.arange(share, dtype=jnp.int32)
        piece = learned_forces(chosen, charge_window, targets, middle, w_in, w_out)
        whole = gather_directly(piece, "bead", 1).reshape(3, CB, atom_count)
        result = jnp.einsum("bc,xca->bxa", expand_mine, whole, precision=highest)
        return result

    coords = positions
    cheap_now, bead_window = cheap_forces(coords)
    charge_window = bead_window[0, 3]
    moments = momenta + 0.5 * outer_step * expensive_forces(coords, charge_window)
    for repeat in range(NINNER):
        moments = moments + 0.5 * inner_step * cheap_now
        persist_mine = lax.dynamic_slice_in_dim(persist, device * per_device, per_device, 0)
        coupling_mine = lax.dynamic_slice_in_dim(coupling, device * per_device, per_device, 0)
        restoring_mine = lax.dynamic_slice_in_dim(restoring, device * per_device, per_device, 0)
        empty = jnp.zeros_like(coords)
        pieces = (gather_directly(coords, "bead", 0), gather_directly(moments, "bead", 0))
        number = pieces[0].shape[0]
        block_persist = lax.slice_in_dim(persist_mine, 0, number, axis=1)
        block_coupling = lax.slice_in_dim(coupling_mine, 0, number, axis=1)
        block_restoring = lax.slice_in_dim(restoring_mine, 0, number, axis=1)
        new_coords = (
            empty
            + jnp.einsum("ab,bxn->axn", block_persist, pieces[0], precision=highest)
            + jnp.einsum("ab,bxn->axn", block_coupling, pieces[1], precision=highest) / masses
        )
        new_moments = (
            empty
            + jnp.einsum("ab,bxn->axn", block_persist, pieces[1], precision=highest)
            + jnp.einsum("ab,bxn->axn", block_restoring, pieces[0], precision=highest) * masses
        )
        coords = new_coords
        moments = new_moments
        cheap_now, bead_window = cheap_forces(coords)
        moments = moments + 0.5 * inner_step * cheap_now
    moments = moments + 0.5 * outer_step * expensive_forces(coords, charge_window)
    return (coords, moments)


def solution(mesh):
    in_specs = (
        P("bead", None, "space"),
        P("bead", None, "space"),
        P(None, "space"),
        P("space"),
        P("space"),
        P(),
        P(),
        P(),
        P(),
    )
    out_specs = (P("bead", None, "space"), P("bead", None, "space"))
    return jax.shard_map(body, mesh=mesh, in_specs=in_specs, out_specs=out_specs, check_vma=False)
```

profile of v0, /device:TPU:8, one launch (start us, length us, event | category | flops | bytes accessed | tf_op | source)
XLA Modules:
  0.0 629.3 jit_solution(12027104770591572956)
XLA Ops:
  2.1 1.0 broadcast_in_dim.94
  3.2 20.8 %all-to-all-start.1 = ((f32[32,4,3,512]{3,1,2,0:T(4,128)}), f32[32,4,3,512]{3,1,2,0:T(4,128)S(1)}, u32[]{:S(2)}, u32[]{:S(2)}) async-start(f32[32,4,3,512]{3,1,2,0:T(4,128)} %broadcast_in_dim.94), calls=%async_computation.1 | async-start | bytes 1572864 | tf_op jit(solution)/shard_map/all_to_all | solution.py:35
  27.3 1.9 collective-permute-start
  29.2 10.2 %collective-permute-start.1 = (f32[1,4,128]{1,2,0:T(8,128)S(1)}, f32[1,4,128]{1,2,0:T(8,128)S(1)}, u32[]{:S(2)}, u32[]{:S(2)}) collective-permute-start(f32[1,4,128]{1,2,0:T(8,128)S(1)} %get-tuple-element.87), channel_id=1, source_target_pairs={{1,0},{2,1},{3,2},{4,3},{5,4},{6,5},{7,6},{8,7},{9,8},{10,9},{11,1... | collective-permute-start | bytes 6152 | tf_op jit(solution)/shard_map/ppermute | solution.py:28
  41.4 3.8 collective-permute-done.1
  45.6 8.6 %gather_fusion.1 = f32[2048]{0:T(1024)S(1)} fusion(f32[768]{0:T(1024)S(1)} %slice_reduce_fusion, s32[2048]{0:T(1024)S(1)} %broadcast_clamp_fusion.1), kind=kCustom, calls=%fused_computation.1 | custom fusion | bytes 24576 | tf_op jit(solution)/shard_map/gather | solution.py:117
  54.4 1.0 gather_fusion.5
  55.6 54.4 %gather_fusion.6 = f32[16384,4]{1,0:T(8,128)} fusion(f32[4,768]{0,1:T(8,128)S(1)} %fusion.107, s32[16384]{0:T(1024)S(1)} %broadcast_clamp_fusion), kind=kCustom, calls=%fused_computation.6 | custom fusion | bytes 589824 | tf_op jit(solution)/shard_map/while/body/eval_jaxpr/gather | solution.py:107
  110.0 5.2 copy.192
  116.6 1.0 gather_fusion.2
  117.7 10.7 %collective-permute-start.3 = (f32[4,3,128]{1,0,2:T(4,128)S(1)}, f32[4,3,128]{1,0,2:T(4,128)S(1)}, u32[]{:S(2)}, u32[]{:S(2)}) collective-permute-start(f32[4,3,128]{1,0,2:T(4,128)S(1)} %get-tuple-element.73), channel_id=1, source_target_pairs={{1,0},{2,1},{3,2},{4,3},{5,4},{6,5},{7,6},{8,7},{9,8},{10,9},{11,1... | collective-permute-start | bytes 18440 | tf_op jit(solution)/shard_map/ppermute | solution.py:28
  128.3 8.6 %collective-permute-start.2 = (f32[4,3,128]{1,0,2:T(4,128)S(1)}, f32[4,3,128]{1,0,2:T(4,128)S(1)}, u32[]{:S(2)}, u32[]{:S(2)}) collective-permute-start(f32[4,3,128]{1,0,2:T(4,128)S(1)} %get-tuple-element.74), channel_id=1, source_target_pairs={{0,1},{1,2},{2,3},{3,4},{4,5},{5,6},{6,7},{7,8},{8,9},{9,10},{10,1... | collective-permute-start | bytes 18440 | tf_op jit(solution)/shard_map/ppermute | solution.py:25
  137.0 8.2 %collective-permute-done.2 = f32[4,3,128]{1,0,2:T(4,128)S(1)} collective-permute-done((f32[4,3,128]{1,0,2:T(4,128)S(1)}, f32[4,3,128]{1,0,2:T(4,128)S(1)}, u32[]{:S(2)}, u32[]{:S(2)}) %collective-permute-start.2) | collective-permute-done | bytes 6176 | tf_op jit(solution)/shard_map/ppermute | solution.py:25
  145.6 5.5 gather_fusion.3
  153.9 24.0 %all-to-all-start.2 = ((f32[32,1,192]{2,1,0:T(1,128)}), f32[32,1,192]{2,1,0:T(1,128)S(1)}, u32[]{:S(2)}, u32[]{:S(2)}) async-start(f32[32,1,192]{2,1,0:T(1,128)} %reshape.476), calls=%async_computation.2 | async-start | bytes 65536 | tf_op jit(solution)/shard_map/all_to_all | solution.py:35
  178.2 15.7 %all-to-all-done.2 = f32[32,1,192]{2,1,0:T(1,128)S(1)} async-done(((f32[32,1,192]{2,1,0:T(1,128)}), f32[32,1,192]{2,1,0:T(1,128)S(1)}, u32[]{:S(2)}, u32[]{:S(2)}) %all-to-all-start.2) | async-done | bytes 24608 | tf_op jit(solution)/shard_map/all_to_all | solution.py:35
  194.6 4.9 all-to-all-start
  202.0 14.4 %all-to-all-done = f32[32,1,3,512]{3,1,2,0:T(1,128)S(1)} async-done(((f32[32,1,3,512]{3,1,2,0:T(1,128)}), f32[32,1,3,512]{3,1,2,0:T(1,128)S(1)}, u32[]{:S(2)}, u32[]{:S(2)}) %all-to-all-start) | async-done | bytes 196640 | tf_op jit(solution)/shard_map/all_to_all | solution.py:35
  217.2 6.3 %all-to-all-start.3 = ((f32[32,1,3,512]{3,1,2,0:T(1,128)}), f32[32,1,3,512]{3,1,2,0:T(1,128)S(1)}, u32[]{:S(2)}, u32[]{:S(2)}) async-start(f32[32,1,3,512]{3,1,2,0:T(1,128)} %broadcast_in_dim.102), calls=%async_computation.3 | async-start | bytes 393216 | tf_op jit(solution)/shard_map/all_to_all | solution.py:35
  223.5 0.9 fusion.20
  224.4 0.9 fusion.22
  225.3 14.8 %all-to-all-done.3 = f32[32,1,3,512]{3,1,2,0:T(1,128)S(1)} async-done(((f32[32,1,3,512]{3,1,2,0:T(1,128)}), f32[32,1,3,512]{3,1,2,0:T(1,128)S(1)}, u32[]{:S(2)}, u32[]{:S(2)}) %all-to-all-start.3) | async-done | bytes 196640 | tf_op jit(solution)/shard_map/all_to_all | solution.py:35
  240.2 0.9 fusion.18
  241.9 4.7 all-to-all-start.4
  247.5 1.9 collective-permute-start.4
  249.5 10.2 %collective-permute-start.5 = (f32[1,4,128]{1,2,0:T(8,128)S(1)}, f32[1,4,128]{1,2,0:T(8,128)S(1)}, u32[]{:S(2)}, u32[]{:S(2)}) collective-permute-start(f32[1,4,128]{1,2,0:T(8,128)S(1)} %get-tuple-element.85), channel_id=1, source_target_pairs={{1,0},{2,1},{3,2},{4,3},{5,4},{6,5},{7,6},{8,7},{9,8},{10,9},{11,1... | collective-permute-start | bytes 6152 | tf_op jit(solution)/shard_map/ppermute | solution.py:28
  259.7 0.9 fusion.16
  260.6 1.0 collective-permute-done.5
  261.6 1.0 gather_fusion.8
  262.7 54.4 %gather_fusion.9 = f32[16384,4]{1,0:T(8,128)} fusion(f32[4,768]{0,1:T(8,128)S(1)} %maximum_bitcast_fusion, s32[16384]{0:T(1024)S(1)} %broadcast_clamp_fusion), kind=kCustom, calls=%fused_computation.9 | custom fusion | bytes 589824 | tf_op jit(solution)/shard_map/while/body/eval_jaxpr/gather | solution.py:107
  317.2 5.2 copy.198
  323.6 17.1 %all-to-all-start.5 = ((f32[32,1,3,512]{3,1,2,0:T(1,128)}), f32[32,1,3,512]{3,1,2,0:T(1,128)S(1)}, u32[]{:S(2)}, u32[]{:S(2)}) async-start(f32[32,1,3,512]{3,1,2,0:T(1,128)} %broadcast_in_dim.105), calls=%async_computation.5 | async-start | bytes 393216 | tf_op jit(solution)/shard_map/all_to_all | solution.py:35
  340.7 0.9 fusion.12
  341.7 0.9 fusion.14
  342.6 14.8 %all-to-all-done.5 = f32[32,1,3,512]{3,1,2,0:T(1,128)S(1)} async-done(((f32[32,1,3,512]{3,1,2,0:T(1,128)}), f32[32,1,3,512]{3,1,2,0:T(1,128)S(1)}, u32[]{:S(2)}, u32[]{:S(2)}) %all-to-all-start.5) | async-done | bytes 196640 | tf_op jit(solution)/shard_map/all_to_all | solution.py:35
  359.1 4.9 all-to-all-start.6
  365.0 1.9 collective-permute-start.6
  366.9 10.2 %collective-permute-start.7 = (f32[1,4,128]{1,2,0:T(8,128)S(1)}, f32[1,4,128]{1,2,0:T(8,128)S(1)}, u32[]{:S(2)}, u32[]{:S(2)}) collective-permute-start(f32[1,4,128]{1,2,0:T(8,128)S(1)} %get-tuple-element.83), channel_id=1, source_target_pairs={{1,0},{2,1},{3,2},{4,3},{5,4},{6,5},{7,6},{8,7},{9,8},{10,9},{11,1... | collective-permute-start | bytes 6152 | tf_op jit(solution)/shard_map/ppermute | solution.py:28
  377.1 0.9 fusion.8
  378.1 1.0 collective-permute-done.7
  379.0 1.0 gather_fusion.11
  380.1 54.4 %gather_fusion.12 = f32[16384,4]{1,0:T(8,128)} fusion(f32[4,768]{0,1:T(8,128)S(1)} %maximum_bitcast_fusion.1, s32[16384]{0:T(1024)S(1)} %broadcast_clamp_fusion), kind=kCustom, calls=%fused_computation.12 | custom fusion | bytes 589824 | tf_op jit(solution)/shard_map/while/body/eval_jaxpr/gather | solution.py:107
  434.6 5.2 copy.204
  441.0 17.1 %all-to-all-start.7 = ((f32[32,1,3,512]{3,1,2,0:T(1,128)}), f32[32,1,3,512]{3,1,2,0:T(1,128)S(1)}, u32[]{:S(2)}, u32[]{:S(2)}) async-start(f32[32,1,3,512]{3,1,2,0:T(1,128)} %broadcast_in_dim.107), calls=%async_computation.7 | async-start | bytes 393216 | tf_op jit(solution)/shard_map/all_to_all | solution.py:35
  458.1 0.9 fusion.6
  459.1 16.0 %all-to-all-done.7 = f32[32,1,3,512]{3,1,2,0:T(1,128)S(1)} async-done(((f32[32,1,3,512]{3,1,2,0:T(1,128)}), f32[32,1,3,512]{3,1,2,0:T(1,128)S(1)}, u32[]{:S(2)}, u32[]{:S(2)}) %all-to-all-start.7) | async-done | bytes 196640 | tf_op jit(solution)/shard_map/all_to_all | solution.py:35
  476.1 1.0 broadcast_in_dim.108
  477.1 5.2 all-to-all-start.8
  482.3 0.9 fusion.4
  484.1 1.9 collective-permute-start.8
  486.1 10.2 %collective-permute-start.9 = (f32[1,4,128]{1,2,0:T(8,128)S(1)}, f32[1,4,128]{1,2,0:T(8,128)S(1)}, u32[]{:S(2)}, u32[]{:S(2)}) collective-permute-start(f32[1,4,128]{1,2,0:T(8,128)S(1)} %get-tuple-element.81), channel_id=1, source_target_pairs={{1,0},{2,1},{3,2},{4,3},{5,4},{6,5},{7,6},{8,7},{9,8},{10,9},{11,1... | collective-permute-start | bytes 6152 | tf_op jit(solution)/shard_map/ppermute | solution.py:28
  496.3 0.9 fusion
  497.8 9.4 %collective-permute-done.8 = f32[1,4,128]{1,2,0:T(8,128)S(1)} collective-permute-done((f32[1,4,128]{1,2,0:T(8,128)S(1)}, f32[1,4,128]{1,2,0:T(8,128)S(1)}, u32[]{:S(2)}, u32[]{:S(2)}) %collective-permute-start.8) | collective-permute-done | bytes 2080 | tf_op jit(solution)/shard_map/ppermute | solution.py:25
  507.3 1.0 gather_fusion.14
  508.3 54.4 %gather_fusion.15 = f32[16384,4]{1,0:T(8,128)} fusion(f32[4,768]{0,1:T(8,128)S(1)} %maximum_bitcast_fusion.2, s32[16384]{0:T(1024)S(1)} %broadcast_clamp_fusion), kind=kCustom, calls=%fused_computation.15 | custom fusion | bytes 589824 | tf_op jit(solution)/shard_map/while/body/eval_jaxpr/gather | solution.py:107
  562.8 5.2 copy.209
  568.7 1.0 gather_fusion.16
  569.8 5.1 collective-permute-start.11
  574.9 1.9 collective-permute-start.10
  576.9 3.2 collective-permute-done.11
  580.2 9.0 %collective-permute-done.10 = f32[4,3,128]{1,0,2:T(4,128)S(1)} collective-permute-done((f32[4,3,128]{1,0,2:T(4,128)S(1)}, f32[4,3,128]{1,0,2:T(4,128)S(1)}, u32[]{:S(2)}, u32[]{:S(2)}) %collective-permute-start.10) | collective-permute-done | bytes 6176 | tf_op jit(solution)/shard_map/ppermute | solution.py:25
  590.1 5.5 gather_fusion.17
  597.8 13.1 %all-to-all-start.9 = ((f32[32,1,192]{2,1,0:T(1,128)}), f32[32,1,192]{2,1,0:T(1,128)S(1)}, u32[]{:S(2)}, u32[]{:S(2)}) async-start(f32[32,1,192]{2,1,0:T(1,128)} %reshape.478), calls=%async_computation.9 | async-start | bytes 65536 | tf_op jit(solution)/shard_map/all_to_all | solution.py:35
  611.2 15.7 %all-to-all-done.9 = f32[32,1,192]{2,1,0:T(1,128)S(1)} async-done(((f32[32,1,192]{2,1,0:T(1,128)}), f32[32,1,192]{2,1,0:T(1,128)S(1)}, u32[]{:S(2)}, u32[]{:S(2)}) %all-to-all-start.9) | async-done | bytes 24608 | tf_op jit(solution)/shard_map/all_to_all | solution.py:35
  (144 shorter events, 32.1 us)
Async XLA Ops:
  0.6 151.5 %copy-start = (f32[128,8]{0,1:T(8,128)S(1)}, f32[128,8]{0,1:T(8,128)}, u32[]{:S(2)}) copy-start(f32[128,8]{0,1:T(8,128)} %param.23) | copy-start | bytes 12292
  3.2 112.9 %all-to-all-start.1 = ((f32[32,4,3,512]{3,1,2,0:T(4,128)}), f32[32,4,3,512]{3,1,2,0:T(4,128)S(1)}, u32[]{:S(2)}, u32[]{:S(2)}) async-start(f32[32,4,3,512]{3,1,2,0:T(4,128)} %broadcast_in_dim.94), calls=%async_computation.1 | async-start | bytes 1572864 | tf_op jit(solution)/shard_map/all_to_all | solution.py:35
  27.3 14.1 %collective-permute-start = (f32[1,4,128]{1,2,0:T(8,128)S(1)}, f32[1,4,128]{1,2,0:T(8,128)S(1)}, u32[]{:S(2)}, u32[]{:S(2)}) collective-permute-start(f32[1,4,128]{1,2,0:T(8,128)S(1)} %get-tuple-element.86), channel_id=1, source_target_pairs={{0,1},{1,2},{2,3},{3,4},{4,5},{5,6},{6,7},{7,8},{8,9},{9,10},{10,1... | collective-permute-start | bytes 6152 | tf_op jit(solution)/shard_map/ppermute | solution.py:25
  29.2 15.9 %collective-permute-start.1 = (f32[1,4,128]{1,2,0:T(8,128)S(1)}, f32[1,4,128]{1,2,0:T(8,128)S(1)}, u32[]{:S(2)}, u32[]{:S(2)}) collective-permute-start(f32[1,4,128]{1,2,0:T(8,128)S(1)} %get-tuple-element.87), channel_id=1, source_target_pairs={{1,0},{2,1},{3,2},{4,3},{5,4},{6,5},{7,6},{8,7},{9,8},{10,9},{11,1... | collective-permute-start | bytes 6152 | tf_op jit(solution)/shard_map/ppermute | solution.py:28
  55.6 96.5 %copy-start.1 = (f32[8]{0:T(128)S(1)}, f32[8]{0:T(128)}, u32[]{:S(2)}) copy-start(f32[8]{0:T(128)} %constant.158) | copy-start | bytes 100
  55.6 96.8 %copy-start.3 = (f32[8,128]{1,0:T(8,128)S(1)}, f32[8,128]{1,0:T(8,128)}, u32[]{:S(2)}) copy-start(f32[8,128]{1,0:T(8,128)} %param.24) | copy-start | bytes 12292
  110.0 92.0 %copy-start.2 = (f32[1,3,512]{2,0,1:T(1,128)S(1)}, f32[1,3,512]{2,0,1:T(1,128)}, u32[]{:S(2)}) copy-start(f32[1,3,512]{2,0,1:T(1,128)} %param.17) | copy-start | bytes 18436
  117.7 19.3 %collective-permute-start.3 = (f32[4,3,128]{1,0,2:T(4,128)S(1)}, f32[4,3,128]{1,0,2:T(4,128)S(1)}, u32[]{:S(2)}, u32[]{:S(2)}) collective-permute-start(f32[4,3,128]{1,0,2:T(4,128)S(1)} %get-tuple-element.73), channel_id=1, source_target_pairs={{1,0},{2,1},{3,2},{4,3},{5,4},{6,5},{7,6},{8,7},{9,8},{10,9},{11,1... | collective-permute-start | bytes 18440 | tf_op jit(solution)/shard_map/ppermute | solution.py:28
  128.3 16.9 %collective-permute-start.2 = (f32[4,3,128]{1,0,2:T(4,128)S(1)}, f32[4,3,128]{1,0,2:T(4,128)S(1)}, u32[]{:S(2)}, u32[]{:S(2)}) collective-permute-start(f32[4,3,128]{1,0,2:T(4,128)S(1)} %get-tuple-element.74), channel_id=1, source_target_pairs={{0,1},{1,2},{2,3},{3,4},{4,5},{5,6},{6,7},{7,8},{8,9},{9,10},{10,1... | collective-permute-start | bytes 18440 | tf_op jit(solution)/shard_map/ppermute | solution.py:25
  153.9 39.9 %all-to-all-start.2 = ((f32[32,1,192]{2,1,0:T(1,128)}), f32[32,1,192]{2,1,0:T(1,128)S(1)}, u32[]{:S(2)}, u32[]{:S(2)}) async-start(f32[32,1,192]{2,1,0:T(1,128)} %reshape.476), calls=%async_computation.2 | async-start | bytes 65536 | tf_op jit(solution)/shard_map/all_to_all | solution.py:35
  194.6 21.8 %all-to-all-start = ((f32[32,1,3,512]{3,1,2,0:T(1,128)}), f32[32,1,3,512]{3,1,2,0:T(1,128)S(1)}, u32[]{:S(2)}, u32[]{:S(2)}) async-start(f32[32,1,3,512]{3,1,2,0:T(1,128)} %broadcast_in_dim.88), calls=%async_computation | async-start | bytes 393216 | tf_op jit(solution)/shard_map/all_to_all | solution.py:35
  217.2 23.0 %all-to-all-start.3 = ((f32[32,1,3,512]{3,1,2,0:T(1,128)}), f32[32,1,3,512]{3,1,2,0:T(1,128)S(1)}, u32[]{:S(2)}, u32[]{:S(2)}) async-start(f32[32,1,3,512]{3,1,2,0:T(1,128)} %broadcast_in_dim.102), calls=%async_computation.3 | async-start | bytes 393216 | tf_op jit(solution)/shard_map/all_to_all | solution.py:35
  241.9 81.0 %all-to-all-start.4 = ((f32[32,1,3,512]{3,1,2,0:T(1,128)}), f32[32,1,3,512]{3,1,2,0:T(1,128)S(1)}, u32[]{:S(2)}, u32[]{:S(2)}) async-start(f32[32,1,3,512]{3,1,2,0:T(1,128)} %broadcast_in_dim.104), calls=%async_computation.4 | async-start | bytes 393216 | tf_op jit(solution)/shard_map/all_to_all | solution.py:35
  247.5 13.1 %collective-permute-start.4 = (f32[1,4,128]{1,2,0:T(8,128)S(1)}, f32[1,4,128]{1,2,0:T(8,128)S(1)}, u32[]{:S(2)}, u32[]{:S(2)}) collective-permute-start(f32[1,4,128]{1,2,0:T(8,128)S(1)} %get-tuple-element.84), channel_id=1, source_target_pairs={{0,1},{1,2},{2,3},{3,4},{4,5},{5,6},{6,7},{7,8},{8,9},{9,10},{10,1... | collective-permute-start | bytes 6152 | tf_op jit(solution)/shard_map/ppermute | solution.py:25
  249.5 12.1 %collective-permute-start.5 = (f32[1,4,128]{1,2,0:T(8,128)S(1)}, f32[1,4,128]{1,2,0:T(8,128)S(1)}, u32[]{:S(2)}, u32[]{:S(2)}) collective-permute-start(f32[1,4,128]{1,2,0:T(8,128)S(1)} %get-tuple-element.85), channel_id=1, source_target_pairs={{1,0},{2,1},{3,2},{4,3},{5,4},{6,5},{7,6},{8,7},{9,8},{10,9},{11,1... | collective-permute-start | bytes 6152 | tf_op jit(solution)/shard_map/ppermute | solution.py:28
  323.6 33.8 %all-to-all-start.5 = ((f32[32,1,3,512]{3,1,2,0:T(1,128)}), f32[32,1,3,512]{3,1,2,0:T(1,128)S(1)}, u32[]{:S(2)}, u32[]{:S(2)}) async-start(f32[32,1,3,512]{3,1,2,0:T(1,128)} %broadcast_in_dim.105), calls=%async_computation.5 | async-start | bytes 393216 | tf_op jit(solution)/shard_map/all_to_all | solution.py:35
  359.1 81.1 %all-to-all-start.6 = ((f32[32,1,3,512]{3,1,2,0:T(1,128)}), f32[32,1,3,512]{3,1,2,0:T(1,128)S(1)}, u32[]{:S(2)}, u32[]{:S(2)}) async-start(f32[32,1,3,512]{3,1,2,0:T(1,128)} %broadcast_in_dim.106), calls=%async_computation.6 | async-start | bytes 393216 | tf_op jit(solution)/shard_map/all_to_all | solution.py:35
  365.0 13.1 %collective-permute-start.6 = (f32[1,4,128]{1,2,0:T(8,128)S(1)}, f32[1,4,128]{1,2,0:T(8,128)S(1)}, u32[]{:S(2)}, u32[]{:S(2)}) collective-permute-start(f32[1,4,128]{1,2,0:T(8,128)S(1)} %get-tuple-element.82), channel_id=1, source_target_pairs={{0,1},{1,2},{2,3},{3,4},{4,5},{5,6},{6,7},{7,8},{8,9},{9,10},{10,1... | collective-permute-start | bytes 6152 | tf_op jit(solution)/shard_map/ppermute | solution.py:25
  366.9 12.1 %collective-permute-start.7 = (f32[1,4,128]{1,2,0:T(8,128)S(1)}, f32[1,4,128]{1,2,0:T(8,128)S(1)}, u32[]{:S(2)}, u32[]{:S(2)}) collective-permute-start(f32[1,4,128]{1,2,0:T(8,128)S(1)} %get-tuple-element.83), channel_id=1, source_target_pairs={{1,0},{2,1},{3,2},{4,3},{5,4},{6,5},{7,6},{8,7},{9,8},{10,9},{11,1... | collective-permute-start | bytes 6152 | tf_op jit(solution)/shard_map/ppermute | solution.py:28
  441.0 34.1 %all-to-all-start.7 = ((f32[32,1,3,512]{3,1,2,0:T(1,128)}), f32[32,1,3,512]{3,1,2,0:T(1,128)S(1)}, u32[]{:S(2)}, u32[]{:S(2)}) async-start(f32[32,1,3,512]{3,1,2,0:T(1,128)} %broadcast_in_dim.107), calls=%async_computation.7 | async-start | bytes 393216 | tf_op jit(solution)/shard_map/all_to_all | solution.py:35
  477.1 91.1 %all-to-all-start.8 = ((f32[32,4,3,512]{3,1,2,0:T(4,128)}), f32[32,4,3,512]{3,1,2,0:T(4,128)S(1)}, u32[]{:S(2)}, u32[]{:S(2)}) async-start(f32[32,4,3,512]{3,1,2,0:T(4,128)} %broadcast_in_dim.108), calls=%async_computation.8 | async-start | bytes 1572864 | tf_op jit(solution)/shard_map/all_to_all | solution.py:35
  484.1 23.1 %collective-permute-start.8 = (f32[1,4,128]{1,2,0:T(8,128)S(1)}, f32[1,4,128]{1,2,0:T(8,128)S(1)}, u32[]{:S(2)}, u32[]{:S(2)}) collective-permute-start(f32[1,4,128]{1,2,0:T(8,128)S(1)} %get-tuple-element.80), channel_id=1, source_target_pairs={{0,1},{1,2},{2,3},{3,4},{4,5},{5,6},{6,7},{7,8},{8,9},{9,10},{10,1... | collective-permute-start | bytes 6152 | tf_op jit(solution)/shard_map/ppermute | solution.py:25
  486.1 21.2 %collective-permute-start.9 = (f32[1,4,128]{1,2,0:T(8,128)S(1)}, f32[1,4,128]{1,2,0:T(8,128)S(1)}, u32[]{:S(2)}, u32[]{:S(2)}) collective-permute-start(f32[1,4,128]{1,2,0:T(8,128)S(1)} %get-tuple-element.81), channel_id=1, source_target_pairs={{1,0},{2,1},{3,2},{4,3},{5,4},{6,5},{7,6},{8,7},{9,8},{10,9},{11,1... | collective-permute-start | bytes 6152 | tf_op jit(solution)/shard_map/ppermute | solution.py:28
  569.8 10.3 %collective-permute-start.11 = (f32[4,3,128]{1,0,2:T(4,128)S(1)}, f32[4,3,128]{1,0,2:T(4,128)S(1)}, u32[]{:S(2)}, u32[]{:S(2)}) collective-permute-start(f32[4,3,128]{1,0,2:T(4,128)S(1)} %get-tuple-element.71), channel_id=1, source_target_pairs={{1,0},{2,1},{3,2},{4,3},{5,4},{6,5},{7,6},{8,7},{9,8},{10,9},{11,1... | collective-permute-start | bytes 18440 | tf_op jit(solution)/shard_map/ppermute | solution.py:28
  574.9 14.3 %collective-permute-start.10 = (f32[4,3,128]{1,0,2:T(4,128)S(1)}, f32[4,3,128]{1,0,2:T(4,128)S(1)}, u32[]{:S(2)}, u32[]{:S(2)}) collective-permute-start(f32[4,3,128]{1,0,2:T(4,128)S(1)} %get-tuple-element.72), channel_id=1, source_target_pairs={{0,1},{1,2},{2,3},{3,4},{4,5},{5,6},{6,7},{7,8},{8,9},{9,10},{10,1... | collective-permute-start | bytes 18440 | tf_op jit(solution)/shard_map/ppermute | solution.py:25
  597.8 29.0 %all-to-all-start.9 = ((f32[32,1,192]{2,1,0:T(1,128)}), f32[32,1,192]{2,1,0:T(1,128)S(1)}, u32[]{:S(2)}, u32[]{:S(2)}) async-start(f32[32,1,192]{2,1,0:T(1,128)} %reshape.478), calls=%async_computation.9 | async-start | bytes 65536 | tf_op jit(solution)/shard_map/all_to_all | solution.py:35
where the time goes:
time: 631 us; the launch traced here: 629 us
  local copies, waits for them, and re-layouts  285 us (45%)
  starting transfers between devices  193 us (31%)
  waiting for transfers between devices  127 us (20%)
  matrix products  13.4 us (2%)
  other arithmetic  8.93 us (1%)
    gather x8, local copies, waits for them, and re-layouts, pair_forces(): others = extended[:, targets]  239 us
    all_to_all x10, starting transfers between devices, from_everyone(): lax.all_to_all(jnp.broadcast_to(shard[None], (size, *shard.shape)), axis,...  118 us
    all_to_all x10, waiting for transfers between devices, from_everyone(): lax.all_to_all(jnp.broadcast_to(shard[None], (size, *shard.shape)), axis,...  91.4 us
    ppermute x6, starting transfers between devices, with_halo(): lax.ppermute(lax.slice_in_dim(block, 0, width, axis=dim), axis, backward)  56.8 us
    ppermute x6, waiting for transfers between devices, with_halo(): lax.ppermute(lax.slice_in_dim(block, block.shape[dim] - width, None, axis...  26.6 us
    ppermute x6, starting transfers between devices, with_halo(): lax.ppermute(lax.slice_in_dim(block, block.shape[dim] - width, None, axis...  18.2 us
  transfers between devices with their start and end apart: 22, of which 13 were waited for; matrix products, arithmetic and copies ran while one was open for 43% of the time, Pallas kernels for 0%

commit v1 on v0

v1 whole, which is shorter than its diff:
```python
import functools

import jax
import jax.numpy as jnp
import numpy as np
from jax import lax
from jax.experimental import pallas as pl
from jax.experimental.pallas import tpu as pltpu
from jax.sharding import PartitionSpec as P

BEADS = 32
CB = 4
NINNER = 3
NRBF = 8
H = 128
SLOTS = 32
ATOMS = 512
CHUNKS = 4
WINDOW = 6
N_SPACE = 16

polymer_freq = 10.0
outer_step = 6.0
inner_step = outer_step / NINNER
f32 = jnp.float32
bf16 = jnp.bfloat16
VMEM_LIMIT = 56 * 1024 * 1024


def mode_matrix(count):
    beadpos = np.arange(count)[None, :]
    modeidx = np.arange(count)[:, None]
    middle = count // 2
    cosine = np.sqrt(2.0 / count) * np.cos(2.0 * np.pi * beadpos * modeidx / count)
    sine_rows = np.sqrt(2.0 / count) * np.sin(2.0 * np.pi * beadpos * modeidx / count)
    matrix = np.where(modeidx < middle, cosine, sine_rows)
    matrix = np.where(modeidx == 0, 1.0 / np.sqrt(count), matrix)
    matrix = np.where(modeidx == middle, np.cos(np.pi * beadpos) / np.sqrt(count), matrix)
    return matrix


def polymer_tables(count):
    modes = mode_matrix(count)
    frequency = 2.0 * polymer_freq * np.sin(np.pi * np.arange(count) / count)
    nonzero = np.where(frequency > 0, frequency, 1.0)
    cosine = np.cos(frequency * inner_step)
    drift_gain = np.where(frequency > 0, np.sin(frequency * inner_step) / nonzero, inner_step)
    spring = frequency * np.sin(frequency * inner_step)
    persist = modes.T @ (cosine[:, None] * modes)
    coupling = modes.T @ (drift_gain[:, None] * modes)
    restoring = -(modes.T @ (spring[:, None] * modes))
    return persist, coupling, restoring


def contraction(count, fewer):
    full_modes = mode_matrix(count)
    small_modes = mode_matrix(fewer)
    kept = list(range(fewer // 2 + 1)) + list(range(count - fewer // 2 + 1, count))
    contract = np.sqrt(fewer / count) * (small_modes.T @ full_modes[kept])
    expand = count / fewer * contract.T
    return contract, expand


def three_terms(matrix):
    high = matrix.astype(np.float32).astype(jnp.bfloat16)
    low = (matrix - high.astype(np.float64)).astype(np.float32).astype(jnp.bfloat16)
    return np.concatenate([high, low, high], axis=1)


BEAD_OF_ROW = np.array([x * 8 + z * 4 + y for z in range(2) for x in range(4) for y in range(4)])


def tables():
    persist, coupling, restoring = polymer_tables(BEADS)
    contract, expand = contraction(BEADS, CB)
    order = BEAD_OF_ROW
    persist, coupling, restoring = (m[np.ix_(order, order)] for m in (persist, coupling, restoring))
    contract, expand = contract[:, order], expand[order]
    step = np.block([[persist, coupling], [restoring, persist]])
    padded_expand = np.concatenate([expand, np.zeros((BEADS, 16 - CB))], axis=1)
    kick = np.concatenate([coupling @ padded_expand, persist @ padded_expand], axis=0)
    first = three_terms(np.concatenate([step, 0.5 * outer_step * kick], axis=1))
    later = three_terms(step)
    reduce_ = three_terms(np.concatenate([contract, np.zeros((16 - CB, BEADS))], axis=0))
    return first, later, reduce_, (0.5 * outer_step * expand).astype(np.float32)


def lanes(source, index):
    return jnp.take_along_axis(source, index, axis=1)


def row8(row):
    return jnp.broadcast_to(row, (8, 128))


def split_rows(value):
    high = value.astype(bf16)
    low = (value - high.astype(f32)).astype(bf16)
    return jnp.concatenate([high, high, low], axis=0)


def dot3(matrix, value):
    return jnp.dot(matrix, split_rows(value), preferred_element_type=f32)


def by_species(species, table):
    return jnp.where(species == 0, table[0], table[1])


def ghosts_of(chunk, index):
    first = chunk(0)
    rows = first.shape[0]
    lane = jnp.broadcast_to(index & 127, (rows, 128))
    part = jnp.broadcast_to(index >> 7, (rows, 128))
    out = lanes(first, lane)
    for k in range(1, CHUNKS):
        out = jnp.where(part == k, lanes(chunk(k), lane), out)
    return out


def tile_index(neighbours, g, a):
    index = neighbours[8 * g : 8 * g + 8, 128 * a : 128 * a + 128]
    return index & 127, [(index >> 7) == k for k in range(1, WINDOW)], index


def looked_up(rows, lane, masks):
    out = lanes(rows[0], lane)
    for k in range(1, WINDOW):
        out = jnp.where(masks[k - 1], lanes(rows[k], lane), out)
    return out


def cheap_by_lanes(table, neighbours, weights, a):
    rows = [[row8(table(x, k)) for k in range(WINDOW)] for x in range(3)]
    total = [jnp.zeros((8, 128), f32) for _ in range(3)]
    for g in range(SLOTS // 8):
        lane, masks, _ = tile_index(neighbours, g, a)
        offset = [looked_up(rows[x], lane, masks) - rows[x][1 + a] for x in range(3)]
        squared = offset[0] * offset[0] + offset[1] * offset[1] + offset[2] * offset[2]
        w = weights[8 * g : 8 * g + 8, 128 * a : 128 * a + 128] * jnp.exp(-squared)
        for x in range(3):
            total[x] = total[x] + w * offset[x]
    return [jnp.sum(t, axis=0, keepdims=True) for t in total]


def powers(squared):
    even = jnp.exp(-0.2 * squared)
    odd = jnp.exp(-(0.2 * 2.0**0.5) * squared)
    out = [even, odd]
    for _ in range(3):
        even, odd = even * even, odd * odd
        out += [even, odd]
    return out


def learned_by_lanes(table, neighbours, weights, w_in, w_out, offsets, messages, radials, store):
    for c in range(CB):
        for a in range(CHUNKS):
            rows = [[row8(table(c, x, k)) for k in range(WINDOW)] for x in range(3)]
            total = [jnp.zeros((8, 128), f32) for _ in range(NRBF)]
            for g in range(SLOTS // 8):
                lane, masks, _ = tile_index(neighbours, g, a)
                offset = [looked_up(rows[x], lane, masks) - rows[x][1 + a] for x in range(3)]
                squared = offset[0] * offset[0] + offset[1] * offset[1] + offset[2] * offset[2]
                for x in range(3):
                    offsets[c, a, g, x] = offset[x]
                w = weights[8 * g : 8 * g + 8, 128 * a : 128 * a + 128]
                for r, basis in enumerate(powers(squared)):
                    total[r] = total[r] + w * basis
            at = c * ATOMS + a * 128
            for r in range(NRBF):
                messages[r : r + 1, at : at + 128] = jnp.sum(total[r], axis=0, keepdims=True) * (1.0 / SLOTS)
    highest = lax.Precision.HIGHEST
    hidden = jnp.dot(w_in[...], messages[...], precision=highest, preferred_element_type=f32)
    hidden = hidden * (1.0 / (1.0 + jnp.exp(-hidden)))
    radials[...] = jnp.dot(w_out[...], hidden, precision=highest, preferred_element_type=f32)
    for c in range(CB):
        for a in range(CHUNKS):
            at = c * ATOMS + a * 128
            radial = [row8(radials[r : r + 1, at : at + 128]) for r in range(NRBF)]
            total = [jnp.zeros((8, 128), f32) for _ in range(3)]
            for g in range(SLOTS // 8):
                offset = [offsets[c, a, g, x] for x in range(3)]
                squared = offset[0] * offset[0] + offset[1] * offset[1] + offset[2] * offset[2]
                basis = powers(squared)
                profile = radial[0] * basis[0]
                for r in range(1, NRBF):
                    profile = profile + radial[r] * basis[r]
                w = weights[8 * g : 8 * g + 8, 128 * a : 128 * a + 128] * profile
                for x in range(3):
                    total[x] = total[x] + w * offset[x]
            for x in range(3):
                store(c, x, a, jnp.sum(total[x], axis=0, keepdims=True))


def cheap_by_matmul(coords, below, above, neighbours, weights, stacked, total):
    rows = 3 * BEADS
    parts = (
        jnp.concatenate([below[...], coords[:, 0:128]], axis=1),
        coords[:, 128:384],
        jnp.concatenate([coords[:, 384:512], above[...]], axis=1),
    )
    for k, part in enumerate(parts):
        high = part.astype(bf16)
        stacked[k * rows : (k + 1) * rows, 0:256] = high
        stacked[k * rows : (k + 1) * rows, 256:512] = (part - high.astype(f32)).astype(bf16)
    rounded = coords[...].astype(bf16).astype(f32)
    rounded = rounded + (coords[...] - rounded).astype(bf16).astype(f32)
    total[...] = jnp.zeros_like(total)
    unroll = 4

    def group(i, _):
        for j in range(unroll):
            slot = i * unroll + j
            index = neighbours[pl.ds(slot, 1), :]
            place = lax.broadcasted_iota(jnp.int32, (256, ATOMS), 0)
            chosen = jnp.where(place == (index & 255), 1.0, 0.0).astype(bf16)
            picked = jnp.dot(
                stacked[...], jnp.concatenate([chosen, chosen], axis=0), preferred_element_type=f32
            )
            part = index >> 8
            other = jnp.where(
                part == 0,
                picked[0:rows],
                jnp.where(part == 1, picked[rows : 2 * rows], picked[2 * rows : 3 * rows]),
            )
            offset = other - rounded
            x, y, z = offset[0:BEADS], offset[BEADS : 2 * BEADS], offset[2 * BEADS :]
            w = weights[pl.ds(slot, 1), :] * jnp.exp(-(x * x + y * y + z * z))
            total[0:BEADS] += w * x
            total[BEADS : 2 * BEADS] += w * y
            total[2 * BEADS :] += w * z
        return 0

    lax.fori_loop(0, SLOTS // unroll, group, 0)


def propagated(coords, veloc, table, extra=None):
    wide = []
    for x in range(3):
        at = slice(x * BEADS, (x + 1) * BEADS)
        pieces = [coords[at], veloc[at]]
        if extra is not None:
            pieces.append(extra[x])
        wide.append(jnp.concatenate(pieces, axis=0))
    return dot3(table[...], jnp.concatenate(wide, axis=1))


def first_kernel(pos, mom, species, mass_table, out):
    mass = by_species(species[...], mass_table)
    out[0:12] = pos[...]
    for x in range(3):
        out[12 + 4 * x : 16 + 4 * x] = mom[4 * x : 4 * x + 4] / mass


def send_kernel(place, own, peer, species, scale, ghost_rows, down, up, rows):
    upper = place[0] == 0
    low = jnp.where(upper, own[...], peer[...])
    high = jnp.where(upper, peer[...], own[...])
    charge = by_species(species[...], scale)
    for k in range(CHUNKS):
        for x in range(3):
            rows[k, x : x + 1] = low[4 * x + k : 4 * x + k + 1]
            rows[k, 3 + x : 4 + x] = high[4 * x + k : 4 * x + k + 1]
        rows[k, 6:7] = charge[k : k + 1]
        rows[k, 7:8] = charge[k : k + 1]
    down[...] = ghosts_of(lambda k: rows[k], ghost_rows[0:1])
    up[...] = ghosts_of(lambda k: rows[k], ghost_rows[1:2])


def pack_kernel(
    place, own, peer, below, above, species, scale, mass_table, neighbours, out, weights, block, charges
):
    upper = place[0] == 0
    low = jnp.where(upper, own[...], peer[...])
    high = jnp.where(upper, peer[...], own[...])
    charge = by_species(species[...], scale)
    inverse = by_species(species[...], [1.0 / mass_table[0], 1.0 / mass_table[1]])
    charges[0:1] = below[6:7]
    charges[1:5] = charge
    charges[5:6] = above[6:7]
    for k, state in enumerate((low, high)):
        base = 32 * k
        for x in range(3):
            at = base + 6 * x
            block[at : at + 1] = below[3 * k + x : 3 * k + x + 1]
            block[at + 1 : at + 5] = state[4 * x : 4 * x + 4]
            block[at + 5 : at + 6] = above[3 * k + x : 3 * k + x + 1]
        block[base + 18 : base + 30] = state[12:24]
        block[base + 30 : base + 32] = jnp.zeros((2, 128), f32)
    for a in range(CHUNKS):
        itself = 128 + 128 * a + lax.broadcasted_iota(jnp.int32, (8, 128), 1)
        rows = [row8(charges[k : k + 1]) for k in range(WINDOW)]
        for g in range(SLOTS // 8):
            lane, masks, index = tile_index(neighbours, g, a)
            q = looked_up(rows, lane, masks)
            weights[8 * g : 8 * g + 8, 128 * a : 128 * a + 128] = jnp.where(index == itself, 0.0, q)
    for k in range(2):
        base = 32 * k
        for a in range(CHUNKS):
            force = cheap_by_lanes(
                lambda x, w: block[base + 6 * x + w : base + 6 * x + w + 1], neighbours, weights, a
            )
            gain = charge[a : a + 1] * inverse[a : a + 1]
            for x in range(3):
                at = base + 18 + 4 * x + a
                block[at : at + 1] = block[at : at + 1] + gain * force[x]
    for i in range(16):
        out[i] = block[...]


def begin_kernel(
    gathered, neighbours, weights, species, mass_table, ghost_rows, w_in, w_out, first, reduce_,
    coords, veloc, down, up,
    window, start, contracted, offsets, messages, radials, slow,
):
    inverse = by_species(species[...], [1.0 / mass_table[0], 1.0 / mass_table[1]])
    for z in range(2):
        for x in range(3):
            at = slice(x * BEADS + 16 * z, x * BEADS + 16 * z + 16)
            for k in range(WINDOW):
                window[at, 128 * k : 128 * k + 128] = gathered[:, 32 * z + 6 * x + k, :]
            for k in range(CHUNKS):
                start[at, 128 * k : 128 * k + 128] = gathered[:, 32 * z + 18 + 4 * x + k, :]
    for x in range(3):
        contracted[x] = dot3(reduce_[...], window[x * BEADS : (x + 1) * BEADS, :])
    slow[...] = jnp.zeros_like(slow)

    def store(c, x, a, value):
        slow[x, c : c + 1, 128 * a : 128 * a + 128] = value

    learned_by_lanes(
        lambda c, x, k: contracted[x, c : c + 1, 128 * k : 128 * k + 128],
        neighbours, weights, w_in, w_out, offsets, messages, radials, store,
    )
    moved = propagated(
        window[:, 128:640], start[...], first, [slow[x] * inverse for x in range(3)]
    )
    finish_step(moved, coords, veloc, ghost_rows, down, up)


def finish_step(moved, coords, veloc, ghost_rows, down, up):
    for x in range(3):
        at = slice(x * BEADS, (x + 1) * BEADS)
        coords[at] = moved[0:BEADS, ATOMS * x : ATOMS * (x + 1)]
        veloc[at] = moved[BEADS : 2 * BEADS, ATOMS * x : ATOMS * (x + 1)]
    for i in range(3 * BEADS // 8):
        chunk = lambda k: coords[8 * i : 8 * i + 8, 128 * k : 128 * k + 128]
        down[8 * i : 8 * i + 8] = ghosts_of(chunk, ghost_rows[0:1])
        up[8 * i : 8 * i + 8] = ghosts_of(chunk, ghost_rows[1:2])


def kicked(coords, veloc, below, above, neighbours, weights, species, scale, mass_table, stacked, total):
    cheap_by_matmul(coords, below, above, neighbours, weights, stacked, total)
    gain = by_species(species[...], [scale[0] / mass_table[0], scale[1] / mass_table[1]]) * inner_step
    return veloc[...] + gain * total[...]


def middle_kernel(
    coords, veloc, below, above, neighbours, weights, species, scale, mass_table, ghost_rows, later,
    new_coords, new_veloc, down, up, stacked, total,
):
    velocities = kicked(
        coords, veloc, below, above, neighbours, weights, species, scale, mass_table, stacked, total
    )
    moved = propagated(coords[...], velocities, later)
    finish_step(moved, new_coords, new_veloc, ghost_rows, down, up)


def last_kernel(
    place, coords, veloc, below, above, neighbours, weights, species, scale, mass_table, ghost_rows, later,
    reduce_, own, contracted, down, up, stacked, total, moved, rows,
):
    velocities = kicked(
        coords, veloc, below, above, neighbours, weights, species, scale, mass_table, stacked, total
    )
    moved[...] = propagated(coords[...], velocities, later)
    small = dot3(reduce_[...], moved[0:BEADS, :])
    for x in range(3):
        at = slice(ATOMS * x, ATOMS * (x + 1))
        own[x : x + 1] = moved[pl.ds(place[1], 1), at]
        own[3 + x : 4 + x] = moved[pl.ds(BEADS + place[1], 1), at]
        contracted[4 * x : 4 * x + 4] = small[0:4, at]
    own[6:8] = jnp.zeros((2, ATOMS), f32)
    contracted[12:16] = jnp.zeros((4, ATOMS), f32)
    rows[0:12] = contracted[0:12]
    for which, out in ((2, down), (3, up)):
        for x in range(3):
            rows[12 + x : 13 + x] = moved[pl.ds(place[which], 1), ATOMS * x : ATOMS * (x + 1)]
        rows[15:16] = contracted[12:13]
        index = ghost_rows[which - 2 : which - 1]
        for i in range(2):
            out[8 * i : 8 * i + 8] = ghosts_of(
                lambda k: rows[8 * i : 8 * i + 8, 128 * k : 128 * k + 128], index
            )


def end_kernel(
    place, expand, own, contracted, below, above, neighbours, weights, species, scale, mass_table, w_in, w_out,
    new_pos, new_mom,
    window, offsets, messages, radials, slow,
):
    charge = by_species(species[...], scale)
    mass = by_species(species[...], mass_table)
    window[0:16, 0:128] = below[...]
    window[0:16, 640:768] = above[...]
    window[0:12, 128:640] = contracted[0:12]
    window[12:15, 128:640] = own[0:3]

    def store(c, x, a, value):
        slow[c, x, a : a + 1] = value

    learned_by_lanes(
        lambda c, x, k: window[4 * x + c : 4 * x + c + 1, 128 * k : 128 * k + 128],
        neighbours, weights, w_in, w_out, offsets, messages, radials, store,
    )
    for a in range(CHUNKS):
        force = cheap_by_lanes(
            lambda x, k: window[12 + x : 13 + x, 128 * k : 128 * k + 128], neighbours, weights, a
        )
        at = slice(128 * a, 128 * a + 128)
        for x in range(3):
            value = mass[a : a + 1] * own[3 + x : 4 + x, at] + (0.5 * inner_step) * charge[a : a + 1] * force[x]
            for c in range(CB):
                value = value + expand[place[1], c] * slow[c, x, a : a + 1]
            new_mom[4 * x + a : 4 * x + a + 1] = value
            new_pos[4 * x + a : 4 * x + a + 1] = own[x : x + 1, at]


def call(kernel, outs, scratch, args, scalars):
    specs = [
        pl.BlockSpec(memory_space=pltpu.SMEM if i in scalars else pltpu.VMEM) for i in range(len(args))
    ]
    shapes = [jax.ShapeDtypeStruct(s, f32) for s in outs]
    return pl.pallas_call(
        kernel,
        out_shape=shapes,
        in_specs=specs,
        out_specs=[pl.BlockSpec(memory_space=pltpu.VMEM)] * len(outs),
        scratch_shapes=[pltpu.VMEM(s, d) for s, d in scratch],
        compiler_params=pltpu.CompilerParams(vmem_limit_bytes=VMEM_LIMIT),
    )(*args)


RING = ("bead", "space")


def ring(step):
    pairs = []
    for bead in range(BEADS):
        for domain in range(N_SPACE):
            to = domain + step
            other = bead if 0 <= to < N_SPACE else bead ^ 4
            pairs.append((bead * N_SPACE + domain, other * N_SPACE + to % N_SPACE))
    return pairs


def exchange(down, up):
    below = lax.ppermute(up, RING, ring(1))
    above = lax.ppermute(down, RING, ring(-1))
    return below, above


def body(
    positions, momenta, neighbours, ghost_rows, species, species_scale, mass_table, w_in, w_out
):
    first, later, reduce_, expand = tables()
    first, later, reduce_ = (jnp.asarray(t) for t in (first, later, reduce_))
    expand = jnp.asarray(expand)
    bead = lax.axis_index("bead")
    domain = lax.axis_index("space")
    half = (bead // 4) % 2
    row = half * 16 + (bead // 8) * 4 + bead % 4
    other = (1 - half) * 16 + (bead // 8) * 4 + bead % 4
    row_below = jnp.where(domain == 0, other, row)
    row_above = jnp.where(domain == N_SPACE - 1, other, row)
    place = jnp.stack([half, row, row_below, row_above]).astype(jnp.int32)

    pos = positions.reshape(12, 128)
    mom = momenta.reshape(12, 128)
    sp4 = species.reshape(4, 128)
    sp1 = species.reshape(1, ATOMS)
    ghosts = ghost_rows.reshape(2, 128)

    (own,) = call(first_kernel, [(24, 128)], [], (pos, mom, sp4, mass_table), (3,))
    peer = lax.ppermute(own, "bead", [(b, b ^ 4) for b in range(BEADS)])
    down, up = call(
        send_kernel, [(8, 128)] * 2, [((4, 8, 128), f32)], (place, own, peer, sp4, species_scale, ghosts), (0, 4)
    )
    below, above = exchange(down, up)
    block, weights = call(
        pack_kernel,
        [(16, 64, 128), (SLOTS, ATOMS)],
        [((64, 128), f32), ((8, 128), f32)],
        (place, own, peer, below, above, sp4, species_scale, mass_table, neighbours),
        (0, 6, 7),
    )
    groups = [[x * 8 + z * 4 + y for x in range(4) for y in range(4)] for z in range(2)]
    gathered = lax.all_to_all(block, "bead", 0, 0, axis_index_groups=groups, tiled=True)
    offsets = ((CB, CHUNKS, SLOTS // 8, 3, 8, 128), f32)
    coords, veloc, down, up = call(
        begin_kernel,
        [(96, ATOMS), (96, ATOMS), (96, 128), (96, 128)],
        [
            ((96, 768), f32), ((96, ATOMS), f32), ((3, 16, 768), f32), offsets, ((NRBF, CB * ATOMS), f32),
            ((NRBF, CB * ATOMS), f32), ((3, 16, ATOMS), f32),
        ],
        (gathered, neighbours, weights, sp1, mass_table, ghosts, w_in, w_out, first, reduce_),
        (4,),
    )
    big = [((3 * 96, 512), bf16), ((96, ATOMS), f32)]
    below, above = exchange(down, up)
    coords, veloc, down, up = call(
        middle_kernel,
        [(96, ATOMS), (96, ATOMS), (96, 128), (96, 128)],
        big,
        (coords, veloc, below, above, neighbours, weights, sp1, species_scale, mass_table, ghosts, later),
        (7, 8),
    )
    below, above = exchange(down, up)
    mine, contracted, down, up = call(
        last_kernel,
        [(8, ATOMS), (16, ATOMS), (16, 128), (16, 128)],
        big + [((2 * BEADS, 3 * ATOMS), f32), ((16, ATOMS), f32)],
        (place, coords, veloc, below, above, neighbours, weights, sp1, species_scale, mass_table, ghosts, later, reduce_),
        (0, 8, 9),
    )
    below, above = exchange(down, up)
    new_pos, new_mom = call(
        end_kernel,
        [(12, 128), (12, 128)],
        [
            ((16, 768), f32), offsets, ((NRBF, CB * ATOMS), f32), ((NRBF, CB * ATOMS), f32),
            ((CB, 3, CHUNKS, 128), f32),
        ],
        (place, expand, mine, contracted, below, above, neighbours, weights, sp4, species_scale, mass_table, w_in, w_out),
        (0, 1, 9, 10),
    )
    return new_pos.reshape(1, 3, ATOMS), new_mom.reshape(1, 3, ATOMS)


def solution(mesh):
    in_specs = (
        P("bead", None, "space"),
        P("bead", None, "space"),
        P(None, "space"),
        P("space"),
        P("space"),
        P(),
        P(),
        P(),
        P(),
    )
    out_specs = (P("bead", None, "space"), P("bead", None, "space"))
    return jax.shard_map(body, mesh=mesh, in_specs=in_specs, out_specs=out_specs, check_vma=False)
```

time: 631 us -> 103 us (0.16)
  the two profiles are of different devices: /device:TPU:8 before, /device:TPU:97 now
where the time goes in v1:
time: 103 us; the launch traced here: 102 us
  Pallas kernels  37.1 us (36%)
  starting transfers between devices  27.7 us (27%)
  waiting for transfers between devices  27.5 us (27%)
  local copies, waits for them, and re-layouts  7.77 us (8%)
  other arithmetic  1.33 us (1%)
    pallas_call x7, Pallas kernels, call(): pl.pallas_call(kernel, out_shape=shapes, in_specs=specs, out_specs=[pl.Bl...  37.1 us
    ppermute x4, waiting for transfers between devices, exchange(): above = lax.ppermute(down, RING, ring(-1))  13.6 us
    ppermute x1, starting transfers between devices, body(): peer = lax.ppermute(own, 'bead', [(b, b ^ 4) for b in range(BEADS)])  12.7 us
    all_to_all x1, waiting for transfers between devices, body(): lax.all_to_all(block, 'bead', 0, 0, axis_index_groups=groups, tiled=True)  8.79 us
    ppermute x4, starting transfers between devices, exchange(): below = lax.ppermute(up, RING, ring(1))  7.22 us
    all_to_all x1, starting transfers between devices, body(): lax.all_to_all(block, 'bead', 0, 0, axis_index_groups=groups, tiled=True)  6.89 us
    unnamed x27, local copies, waits for them, and re-layouts  4.65 us
    ppermute x4, waiting for transfers between devices, exchange(): below = lax.ppermute(up, RING, ring(1))  4.39 us
  transfers between devices with their start and end apart: 10, of which 10 were waited for; matrix products, arithmetic and copies ran while one was open for 1% of the time, Pallas kernels for 0%

profile of v1, /device:TPU:97, one launch (start us, length us, event | category | flops | bytes accessed | tf_op | source)
XLA Modules:
  0.0 102.1 jit_solution(14613738462796063197)
XLA Ops:
  0.6 0.7 reduce
  1.3 0.0 copy-start.9
  1.4 0.6 reshape.25.pos
  2.0 0.1 copy-done.9
  2.1 0.6 reshape.26.mom
  2.7 1.4 %shard_map.140.own = f32[24,128]{1,0:T(8,128)} custom-call(f32[12,128]{1,0:T(8,128)} %reshape.25.pos, f32[12,128]{1,0:T(8,128)} %reshape.26.mom, s32[4,128]{1,0:T(4,128)} %bitcast.7, f32[2]{0:T(128)} %mass_table.11), custom_call_target="tpu_custom_call" | custom-call | tf_op jit(solution)/shard_map/pallas_call | solution.py:435
  4.1 12.7 %collective-permute-start = (f32[24,128]{1,0:T(8,128)}, f32[24,128]{1,0:T(8,128)S(1)}, u32[]{:S(2)}, u32[]{:S(2)}) collective-permute-start(f32[24,128]{1,0:T(8,128)} %shard_map.140.own), channel_id=1, source_target_pairs={{0,64},{16,80},{32,96},{48,112},{64,0},{80,16},{96,32},{112,48},{1... | collective-permute-start | bytes 36872 | tf_op jit(solution)/shard_map/ppermute | solution.py:486
  16.9 0.6 pad_add_fusion.place
  17.5 0.7 collective-permute-done.peer
  18.2 0.0 copy-start.5
  18.2 0.6 copy-done.5
  18.8 1.5 %shard_map.141 = (f32[8,128]{1,0:T(8,128)}, f32[8,128]{1,0:T(8,128)}) custom-call(s32[4]{0:T(128)} %pad_add_fusion.place, f32[24,128]{1,0:T(8,128)} %shard_map.140.own, f32[24,128]{1,0:T(8,128)} %copy-done.5, s32[4,128]{1,0:T(4,128)} %bitcast.8, f32[2]{0:T(128)} %scale.9, s32[2,128]{1,0:T(2,128)} %bitcast.14), custom_call_target="tpu_custom_call" | custom-call | tf_op jit(solution)/shard_map/pallas_call | solution.py:435
  20.3 3.8 %collective-permute-start.1 = (f32[8,128]{1,0:T(8,128)}, f32[8,128]{1,0:T(8,128)S(1)}, u32[]{:S(2)}, u32[]{:S(2)}) collective-permute-start(f32[8,128]{1,0:T(8,128)} %get-tuple-element.20), channel_id=1, source_target_pairs={{0,1},{1,2},{2,3},{3,4},{4,5},{5,6},{6,7},{7,8},{8,9},{9,10},{10,1... | collective-permute-start | bytes 12296 | tf_op jit(solution)/shard_map/ppermute | solution.py:459
  24.1 0.0 collective-permute-start.2
  24.1 1.0 collective-permute-done.1.below
  25.1 0.0 copy-start.11
  25.1 3.5 %collective-permute-done.2.above = f32[8,128]{1,0:T(8,128)S(1)} collective-permute-done((f32[8,128]{1,0:T(8,128)}, f32[8,128]{1,0:T(8,128)S(1)}, u32[]{:S(2)}, u32[]{:S(2)}) %collective-permute-start.2) | collective-permute-done | bytes 4128 | tf_op jit(solution)/shard_map/ppermute | solution.py:460
  28.5 0.0 copy-done.11
  28.6 0.0 copy-start.12
  28.6 0.6 copy-done.12
  29.1 2.8 %shard_map.142 = (f32[16,64,128]{2,1,0:T(8,128)}, f32[32,512]{1,0:T(8,128)}) custom-call(s32[4]{0:T(128)} %pad_add_fusion.place, f32[24,128]{1,0:T(8,128)} %shard_map.140.own, f32[24,128]{1,0:T(8,128)} %copy-done.5, f32[8,128]{1,0:T(8,128)} %copy-done.11, f32[8,128]{1,0:T(8,128)} %copy-done.12, s32[4,128]{1,0:T(4,128)} %bitcast.9, f32[2]{0:T(128)} %scale.9, ...), custom_call_target="tpu_custom_call" | custom-call | tf_op jit(solution)/shard_map/pallas_call | solution.py:435
  31.9 0.0 copy-start.10
  31.9 6.9 %all-to-all-start = ((f32[16,64,128]{2,1,0:T(8,128)}), f32[16,64,128]{2,1,0:T(8,128)S(1)}, u32[]{:S(2)}, u32[]{:S(2)}) async-start(f32[16,64,128]{2,1,0:T(8,128)} %get-tuple-element.22), calls=%async_computation | async-start | bytes 1048576 | tf_op jit(solution)/shard_map/all_to_all | solution.py:499
  38.8 0.0 copy-done.10
  38.8 0.7 copy.19.w_in
  39.5 8.8 %all-to-all-done.gathered = f32[16,64,128]{2,1,0:T(8,128)S(1)} async-done(((f32[16,64,128]{2,1,0:T(8,128)}), f32[16,64,128]{2,1,0:T(8,128)S(1)}, u32[]{:S(2)}, u32[]{:S(2)}) %all-to-all-start) | async-done | bytes 524320 | tf_op jit(solution)/shard_map/all_to_all | solution.py:499
  48.3 0.0 copy-start
  48.3 0.8 copy-done
  49.1 5.5 %shard_map.143 = (f32[96,512]{1,0:T(8,128)}, f32[96,512]{1,0:T(8,128)}, f32[96,128]{1,0:T(8,128)}, f32[96,128]{1,0:T(8,128)}) custom-call(f32[16,64,128]{2,1,0:T(8,128)} %copy-done, s32[32,512]{1,0:T(8,128)} %neighbours.9, f32[32,512]{1,0:T(8,128)} %get-tuple-element.23.weights, s32[1,512]{1,0:T(1,128)} %bitcast.10, f32[2]{0:T(128)} %mass_table.11, ...), custom_call_target="tpu_custom_call" | custom-call | tf_op jit(solution)/shard_map/pallas_call | solution.py:435
  54.6 3.2 %collective-permute-start.3 = (f32[96,128]{1,0:T(8,128)}, f32[96,128]{1,0:T(8,128)S(1)}, u32[]{:S(2)}, u32[]{:S(2)}) collective-permute-start(f32[96,128]{1,0:T(8,128)} %get-tuple-element.26), channel_id=1, source_target_pairs={{0,1},{1,2},{2,3},{3,4},{4,5},{5,6},{6,7},{7,8},{8,9},{9,10},{10,1... | collective-permute-start | bytes 147464 | tf_op jit(solution)/shard_map/ppermute | solution.py:459
  57.8 0.0 collective-permute-start.4
  57.8 1.5 %collective-permute-done.3.below = f32[96,128]{1,0:T(8,128)S(1)} collective-permute-done((f32[96,128]{1,0:T(8,128)}, f32[96,128]{1,0:T(8,128)S(1)}, u32[]{:S(2)}, u32[]{:S(2)}) %collective-permute-start.3) | collective-permute-done | bytes 49184 | tf_op jit(solution)/shard_map/ppermute | solution.py:459
  59.3 0.0 copy-start.2
  59.3 3.4 %collective-permute-done.4.above = f32[96,128]{1,0:T(8,128)S(1)} collective-permute-done((f32[96,128]{1,0:T(8,128)}, f32[96,128]{1,0:T(8,128)S(1)}, u32[]{:S(2)}, u32[]{:S(2)}) %collective-permute-start.4) | collective-permute-done | bytes 49184 | tf_op jit(solution)/shard_map/ppermute | solution.py:460
  62.8 0.0 copy-start.4
  62.8 0.0 copy-done.2
  62.8 0.6 copy-done.4
  63.4 10.9 %shard_map.144 = (f32[96,512]{1,0:T(8,128)}, f32[96,512]{1,0:T(8,128)}, f32[96,128]{1,0:T(8,128)}, f32[96,128]{1,0:T(8,128)}) custom-call(f32[96,512]{1,0:T(8,128)} %get-tuple-element.24.coords, f32[96,512]{1,0:T(8,128)} %get-tuple-element.25.veloc, f32[96,128]{1,0:T(8,128)} %copy-done.2, f32[96,128]{1,0:T(8,128)} %copy-done.4, s32[32,512]{1,0:T(8,128)} %neighbours.9, ...), custom_call_target="tpu_custom_call" | custom-call | tf_op jit(solution)/shard_map/pallas_call | solution.py:435
  74.3 0.1 collective-permute-start.5
  74.4 0.4 collective-permute-start.6
  74.8 1.1 %collective-permute-done.5.below = f32[96,128]{1,0:T(8,128)S(1)} collective-permute-done((f32[96,128]{1,0:T(8,128)}, f32[96,128]{1,0:T(8,128)S(1)}, u32[]{:S(2)}, u32[]{:S(2)}) %collective-permute-start.5) | collective-permute-done | bytes 49184 | tf_op jit(solution)/shard_map/ppermute | solution.py:459
  75.8 0.0 copy-start.1
  75.9 3.4 %collective-permute-done.6.above = f32[96,128]{1,0:T(8,128)S(1)} collective-permute-done((f32[96,128]{1,0:T(8,128)}, f32[96,128]{1,0:T(8,128)S(1)}, u32[]{:S(2)}, u32[]{:S(2)}) %collective-permute-start.6) | collective-permute-done | bytes 49184 | tf_op jit(solution)/shard_map/ppermute | solution.py:460
  79.3 0.0 copy-start.3
  79.3 0.0 copy-done.1
  79.3 0.6 copy-done.3
  79.9 10.9 %shard_map.145 = (f32[8,512]{1,0:T(8,128)}, f32[16,512]{1,0:T(8,128)}, f32[16,128]{1,0:T(8,128)}, f32[16,128]{1,0:T(8,128)}) custom-call(s32[4]{0:T(128)} %pad_add_fusion.place, f32[96,512]{1,0:T(8,128)} %get-tuple-element.28.coords, f32[96,512]{1,0:T(8,128)} %get-tuple-element.29.veloc, f32[96,128]{1,0:T(8,128)} %copy-done.1, f32[96,128]{1,0:T(8,128)} %copy-done.3, ...), custom_call_target="tpu_custom_call" | custom-call | tf_op jit(solution)/shard_map/pallas_call | solution.py:435
  90.8 0.1 collective-permute-start.7
  90.9 0.4 collective-permute-start.8
  91.3 0.9 collective-permute-done.7.below
  92.2 0.0 copy-start.6
  92.2 3.2 %collective-permute-done.8.above = f32[16,128]{1,0:T(8,128)S(1)} collective-permute-done((f32[16,128]{1,0:T(8,128)}, f32[16,128]{1,0:T(8,128)S(1)}, u32[]{:S(2)}, u32[]{:S(2)}) %collective-permute-start.8) | collective-permute-done | bytes 8224 | tf_op jit(solution)/shard_map/ppermute | solution.py:460
  95.4 0.0 copy-start.7
  95.4 0.0 copy-done.6
  95.4 0.6 copy-done.7
  96.0 4.2 %shard_map.146 = (f32[12,128]{1,0:T(8,128)}, f32[12,128]{1,0:T(8,128)}) custom-call(s32[4]{0:T(128)} %pad_add_fusion.place, f32[32,4]{1,0:T(8,128)} %constant.74.clone.expand, f32[8,512]{1,0:T(8,128)} %get-tuple-element.32.own, f32[16,512]{1,0:T(8,128)} %get-tuple-element.33.contracted, f32[16,128]{1,0:T(8,128)} %copy-done.6, f32[16,128]{1,0:T(8,128)} %copy-done.7, ...), custom_call_target="tpu_custom_call" | custom-call | tf_op jit(solution)/shard_map/pallas_call | solution.py:435
  100.2 0.0 copy-start.8
  100.2 1.3 %reshape.32 = f32[1,3,512]{2,0,1:T(1,128)} reshape(f32[12,128]{1,0:T(8,128)} %get-tuple-element.36) | data formatting | bytes 12288 | tf_op jit(solution)/shard_map/reshape | solution.py:539
  101.5 0.0 copy-done.8
  101.5 0.6 reshape.33
  (1 shorter events, 0.0 us)
Async XLA Ops:
  1.3 0.7 copy-start.9
  4.1 14.1 %collective-permute-start = (f32[24,128]{1,0:T(8,128)}, f32[24,128]{1,0:T(8,128)S(1)}, u32[]{:S(2)}, u32[]{:S(2)}) collective-permute-start(f32[24,128]{1,0:T(8,128)} %shard_map.140.own), channel_id=1, source_target_pairs={{0,64},{16,80},{32,96},{48,112},{64,0},{80,16},{96,32},{112,48},{1... | collective-permute-start | bytes 36872 | tf_op jit(solution)/shard_map/ppermute | solution.py:486
  18.2 0.6 copy-start.5
  20.3 4.8 %collective-permute-start.1 = (f32[8,128]{1,0:T(8,128)}, f32[8,128]{1,0:T(8,128)S(1)}, u32[]{:S(2)}, u32[]{:S(2)}) collective-permute-start(f32[8,128]{1,0:T(8,128)} %get-tuple-element.20), channel_id=1, source_target_pairs={{0,1},{1,2},{2,3},{3,4},{4,5},{5,6},{6,7},{7,8},{8,9},{9,10},{10,1... | collective-permute-start | bytes 12296 | tf_op jit(solution)/shard_map/ppermute | solution.py:459
  24.1 4.5 %collective-permute-start.2 = (f32[8,128]{1,0:T(8,128)}, f32[8,128]{1,0:T(8,128)S(1)}, u32[]{:S(2)}, u32[]{:S(2)}) collective-permute-start(f32[8,128]{1,0:T(8,128)} %get-tuple-element.21), channel_id=1, source_target_pairs={{0,79},{1,0},{2,1},{3,2},{4,3},{5,4},{6,5},{7,6},{8,7},{9,8},{10,9... | collective-permute-start | bytes 12296 | tf_op jit(solution)/shard_map/ppermute | solution.py:460
  25.1 3.5 %copy-start.11 = (f32[8,128]{1,0:T(8,128)}, f32[8,128]{1,0:T(8,128)S(1)}, u32[]{:S(2)}) copy-start(f32[8,128]{1,0:T(8,128)S(1)} %collective-permute-done.1.below) | copy-start | bytes 12292
  28.6 0.6 copy-start.12
  31.9 6.9 %copy-start.10 = (f32[128,8]{0,1:T(8,128)S(1)}, f32[128,8]{0,1:T(8,128)}, u32[]{:S(2)}) copy-start(f32[128,8]{0,1:T(8,128)} %param.20) | copy-start | bytes 12292
  31.9 16.4 %all-to-all-start = ((f32[16,64,128]{2,1,0:T(8,128)}), f32[16,64,128]{2,1,0:T(8,128)S(1)}, u32[]{:S(2)}, u32[]{:S(2)}) async-start(f32[16,64,128]{2,1,0:T(8,128)} %get-tuple-element.22), calls=%async_computation | async-start | bytes 1048576 | tf_op jit(solution)/shard_map/all_to_all | solution.py:499
  48.3 0.8 copy-start
  54.6 4.7 %collective-permute-start.3 = (f32[96,128]{1,0:T(8,128)}, f32[96,128]{1,0:T(8,128)S(1)}, u32[]{:S(2)}, u32[]{:S(2)}) collective-permute-start(f32[96,128]{1,0:T(8,128)} %get-tuple-element.26), channel_id=1, source_target_pairs={{0,1},{1,2},{2,3},{3,4},{4,5},{5,6},{6,7},{7,8},{8,9},{9,10},{10,1... | collective-permute-start | bytes 147464 | tf_op jit(solution)/shard_map/ppermute | solution.py:459
  57.8 4.9 %collective-permute-start.4 = (f32[96,128]{1,0:T(8,128)}, f32[96,128]{1,0:T(8,128)S(1)}, u32[]{:S(2)}, u32[]{:S(2)}) collective-permute-start(f32[96,128]{1,0:T(8,128)} %get-tuple-element.27), channel_id=1, source_target_pairs={{0,79},{1,0},{2,1},{3,2},{4,3},{5,4},{6,5},{7,6},{8,7},{9,8},{10,9... | collective-permute-start | bytes 147464 | tf_op jit(solution)/shard_map/ppermute | solution.py:460
  59.3 3.4 %copy-start.2 = (f32[96,128]{1,0:T(8,128)}, f32[96,128]{1,0:T(8,128)S(1)}, u32[]{:S(2)}) copy-start(f32[96,128]{1,0:T(8,128)S(1)} %collective-permute-done.3.below) | copy-start | bytes 147460
  62.8 0.6 copy-start.4
  74.3 1.6 %collective-permute-start.5 = (f32[96,128]{1,0:T(8,128)}, f32[96,128]{1,0:T(8,128)S(1)}, u32[]{:S(2)}, u32[]{:S(2)}) collective-permute-start(f32[96,128]{1,0:T(8,128)} %get-tuple-element.30), channel_id=1, source_target_pairs={{0,1},{1,2},{2,3},{3,4},{4,5},{5,6},{6,7},{7,8},{8,9},{9,10},{10,1... | collective-permute-start | bytes 147464 | tf_op jit(solution)/shard_map/ppermute | solution.py:459
  74.4 4.9 %collective-permute-start.6 = (f32[96,128]{1,0:T(8,128)}, f32[96,128]{1,0:T(8,128)S(1)}, u32[]{:S(2)}, u32[]{:S(2)}) collective-permute-start(f32[96,128]{1,0:T(8,128)} %get-tuple-element.31), channel_id=1, source_target_pairs={{0,79},{1,0},{2,1},{3,2},{4,3},{5,4},{6,5},{7,6},{8,7},{9,8},{10,9... | collective-permute-start | bytes 147464 | tf_op jit(solution)/shard_map/ppermute | solution.py:460
  75.8 3.4 %copy-start.1 = (f32[96,128]{1,0:T(8,128)}, f32[96,128]{1,0:T(8,128)S(1)}, u32[]{:S(2)}) copy-start(f32[96,128]{1,0:T(8,128)S(1)} %collective-permute-done.5.below) | copy-start | bytes 147460
  79.3 0.6 copy-start.3
  90.8 1.4 %collective-permute-start.7 = (f32[16,128]{1,0:T(8,128)}, f32[16,128]{1,0:T(8,128)S(1)}, u32[]{:S(2)}, u32[]{:S(2)}) collective-permute-start(f32[16,128]{1,0:T(8,128)} %get-tuple-element.34), channel_id=1, source_target_pairs={{0,1},{1,2},{2,3},{3,4},{4,5},{5,6},{6,7},{7,8},{8,9},{9,10},{10,1... | collective-permute-start | bytes 24584 | tf_op jit(solution)/shard_map/ppermute | solution.py:459
  90.9 4.5 %collective-permute-start.8 = (f32[16,128]{1,0:T(8,128)}, f32[16,128]{1,0:T(8,128)S(1)}, u32[]{:S(2)}, u32[]{:S(2)}) collective-permute-start(f32[16,128]{1,0:T(8,128)} %get-tuple-element.35), channel_id=1, source_target_pairs={{0,79},{1,0},{2,1},{3,2},{4,3},{5,4},{6,5},{7,6},{8,7},{9,8},{10,9... | collective-permute-start | bytes 24584 | tf_op jit(solution)/shard_map/ppermute | solution.py:460
  92.2 3.2 %copy-start.6 = (f32[16,128]{1,0:T(8,128)}, f32[16,128]{1,0:T(8,128)S(1)}, u32[]{:S(2)}) copy-start(f32[16,128]{1,0:T(8,128)S(1)} %collective-permute-done.7.below) | copy-start | bytes 24580
  95.4 0.6 copy-start.7
  100.2 1.3 %copy-start.8 = (f32[12,128]{1,0:T(8,128)S(1)}, f32[12,128]{1,0:T(8,128)}, u32[]{:S(2)}) copy-start(f32[12,128]{1,0:T(8,128)} %get-tuple-element.37) | copy-start | bytes 18436

commit v2 on v1

--- a/solution.py
+++ b/solution.py
@@ -24,7 +24,7 @@
 inner_step = outer_step / NINNER
 f32 = jnp.float32
 bf16 = jnp.bfloat16
-VMEM_LIMIT = 56 * 1024 * 1024
+VMEM_LIMIT = 12 * 1024 * 1024
 
 
 def mode_matrix(count):
@@ -61,10 +61,22 @@
     return contract, expand
 
 
+def bf16_terms(matrix):
+    out, rest = [], matrix
+    for _ in range(3):
+        out.append(rest.astype(np.float32).astype(jnp.bfloat16))
+        rest = rest - out[-1].astype(np.float64)
+    return out
+
+
 def three_terms(matrix):
-    high = matrix.astype(np.float32).astype(jnp.bfloat16)
-    low = (matrix - high.astype(np.float64)).astype(np.float32).astype(jnp.bfloat16)
+    high, low, _ = bf16_terms(matrix)
     return np.concatenate([high, low, high], axis=1)
+
+
+def six_terms(matrix):
+    high, middle, low = bf16_terms(matrix)
+    return np.concatenate([high, high, middle, middle, high, low], axis=1)
 
 
 BEAD_OF_ROW = np.array([x * 8 + z * 4 + y for z in range(2) for x in range(4) for y in range(4)])
@@ -79,8 +91,8 @@
     step = np.block([[persist, coupling], [restoring, persist]])
     padded_expand = np.concatenate([expand, np.zeros((BEADS, 16 - CB))], axis=1)
     kick = np.concatenate([coupling @ padded_expand, persist @ padded_expand], axis=0)
-    first = three_terms(np.concatenate([step, 0.5 * outer_step * kick], axis=1))
-    later = three_terms(step)
+    first = six_terms(np.concatenate([step, 0.5 * outer_step * kick], axis=1))
+    later = six_terms(step)
     reduce_ = three_terms(np.concatenate([contract, np.zeros((16 - CB, BEADS))], axis=0))
     return first, later, reduce_, (0.5 * outer_step * expand).astype(np.float32)
 
@@ -101,6 +113,15 @@
 
 def dot3(matrix, value):
     return jnp.dot(matrix, split_rows(value), preferred_element_type=f32)
+
+
+def dot6(matrix, value):
+    high = value.astype(bf16)
+    rest = value - high.astype(f32)
+    middle = rest.astype(bf16)
+    low = (rest - middle.astype(f32)).astype(bf16)
+    terms = jnp.concatenate([high, middle, high, middle, low, high], axis=0)
+    return jnp.dot(matrix, terms, preferred_element_type=f32)
 
 
 def by_species(species, table):
@@ -207,14 +228,15 @@
     rounded = coords[...].astype(bf16).astype(f32)
     rounded = rounded + (coords[...] - rounded).astype(bf16).astype(f32)
     total[...] = jnp.zeros_like(total)
-    unroll = 4
+    unroll = 8
+    place = lax.broadcasted_iota(jnp.int16, (256, ATOMS), 0)
 
     def group(i, _):
         for j in range(unroll):
             slot = i * unroll + j
             index = neighbours[pl.ds(slot, 1), :]
-            place = lax.broadcasted_iota(jnp.int32, (256, ATOMS), 0)
-            chosen = jnp.where(place == (index & 255), 1.0, 0.0).astype(bf16)
+            column = jnp.broadcast_to(index & 255, (16, ATOMS)).astype(jnp.int16)
+            chosen = jnp.where(place == jnp.tile(column, (16, 1)), bf16(1), bf16(0))
             picked = jnp.dot(
                 stacked[...], jnp.concatenate([chosen, chosen], axis=0), preferred_element_type=f32
             )
@@ -243,50 +265,40 @@
         if extra is not None:
             pieces.append(extra[x])
         wide.append(jnp.concatenate(pieces, axis=0))
-    return dot3(table[...], jnp.concatenate(wide, axis=1))
-
-
-def first_kernel(pos, mom, species, mass_table, out):
-    mass = by_species(species[...], mass_table)
-    out[0:12] = pos[...]
+    return dot6(table[...], jnp.concatenate(wide, axis=1))
+
+
+def first_kernel(pos, mom, species, scale, mass_table, out):
+    inverse = by_species(species[...], [1.0 / mass_table[0], 1.0 / mass_table[1]])
     for x in range(3):
-        out[12 + 4 * x : 16 + 4 * x] = mom[4 * x : 4 * x + 4] / mass
-
-
-def send_kernel(place, own, peer, species, scale, ghost_rows, down, up, rows):
-    upper = place[0] == 0
-    low = jnp.where(upper, own[...], peer[...])
-    high = jnp.where(upper, peer[...], own[...])
-    charge = by_species(species[...], scale)
+        out[x : x + 1] = pos[x]
+        out[3 + x : 4 + x] = mom[x] * inverse
+    out[6:7] = by_species(species[...], scale)
+    out[7:8] = inverse
+
+
+def send_kernel(pair, ghost_rows, down, up, rows):
+    rows[0:3] = pair[0, 0:3]
+    rows[3:6] = pair[1, 0:3]
+    rows[6:8] = pair[0, 6:8]
+    chunk = lambda k: rows[:, 128 * k : 128 * k + 128]
+    down[...] = ghosts_of(chunk, ghost_rows[0:1])
+    up[...] = ghosts_of(chunk, ghost_rows[1:2])
+
+
+def pack_kernel(pair, below, above, neighbours, out, weights, block, charges):
+    charges[0:1] = below[6:7]
     for k in range(CHUNKS):
-        for x in range(3):
-            rows[k, x : x + 1] = low[4 * x + k : 4 * x + k + 1]
-            rows[k, 3 + x : 4 + x] = high[4 * x + k : 4 * x + k + 1]
-        rows[k, 6:7] = charge[k : k + 1]
-        rows[k, 7:8] = charge[k : k + 1]
-    down[...] = ghosts_of(lambda k: rows[k], ghost_rows[0:1])
-    up[...] = ghosts_of(lambda k: rows[k], ghost_rows[1:2])
-
-
-def pack_kernel(
-    place, own, peer, below, above, species, scale, mass_table, neighbours, out, weights, block, charges
-):
-    upper = place[0] == 0
-    low = jnp.where(upper, own[...], peer[...])
-    high = jnp.where(upper, peer[...], own[...])
-    charge = by_species(species[...], scale)
-    inverse = by_species(species[...], [1.0 / mass_table[0], 1.0 / mass_table[1]])
-    charges[0:1] = below[6:7]
-    charges[1:5] = charge
+        charges[1 + k : 2 + k] = pair[0, 6:7, 128 * k : 128 * k + 128]
     charges[5:6] = above[6:7]
-    for k, state in enumerate((low, high)):
+    for k in range(2):
         base = 32 * k
         for x in range(3):
             at = base + 6 * x
             block[at : at + 1] = below[3 * k + x : 3 * k + x + 1]
-            block[at + 1 : at + 5] = state[4 * x : 4 * x + 4]
+            for i in range(CHUNKS):
+                block[at + 1 + i : at + 2 + i] = pair[k, x : x + 1, 128 * i : 128 * i + 128]
             block[at + 5 : at + 6] = above[3 * k + x : 3 * k + x + 1]
-        block[base + 18 : base + 30] = state[12:24]
         block[base + 30 : base + 32] = jnp.zeros((2, 128), f32)
     for a in range(CHUNKS):
         itself = 128 + 128 * a + lax.broadcasted_iota(jnp.int32, (8, 128), 1)
@@ -295,16 +307,17 @@
             lane, masks, index = tile_index(neighbours, g, a)
             q = looked_up(rows, lane, masks)
             weights[8 * g : 8 * g + 8, 128 * a : 128 * a + 128] = jnp.where(index == itself, 0.0, q)
-    for k in range(2):
-        base = 32 * k
-        for a in range(CHUNKS):
+    for a in range(CHUNKS):
+        at = slice(128 * a, 128 * a + 128)
+        gain = pair[0, 6:7, at] * pair[0, 7:8, at] * (0.5 * inner_step)
+        for k in range(2):
+            base = 32 * k
             force = cheap_by_lanes(
                 lambda x, w: block[base + 6 * x + w : base + 6 * x + w + 1], neighbours, weights, a
             )
-            gain = charge[a : a + 1] * inverse[a : a + 1]
             for x in range(3):
-                at = base + 18 + 4 * x + a
-                block[at : at + 1] = block[at : at + 1] + gain * force[x]
+                row = base + 18 + 4 * x + a
+                block[row : row + 1] = pair[k, 3 + x : 4 + x, at] + gain * force[x]
     for i in range(16):
         out[i] = block[...]
 
@@ -420,11 +433,11 @@
         )
         at = slice(128 * a, 128 * a + 128)
         for x in range(3):
-            value = mass[a : a + 1] * own[3 + x : 4 + x, at] + (0.5 * inner_step) * charge[a : a + 1] * force[x]
+            value = mass[:, at] * own[3 + x : 4 + x, at] + (0.5 * inner_step) * charge[:, at] * force[x]
             for c in range(CB):
                 value = value + expand[place[1], c] * slow[c, x, a : a + 1]
-            new_mom[4 * x + a : 4 * x + a + 1] = value
-            new_pos[4 * x + a : 4 * x + a + 1] = own[x : x + 1, at]
+            new_mom[x, :, at] = value
+            new_pos[x, :, at] = own[x : x + 1, at]
 
 
 def call(kernel, outs, scratch, args, scalars):
@@ -476,24 +489,22 @@
     row_above = jnp.where(domain == N_SPACE - 1, other, row)
     place = jnp.stack([half, row, row_below, row_above]).astype(jnp.int32)
 
-    pos = positions.reshape(12, 128)
-    mom = momenta.reshape(12, 128)
-    sp4 = species.reshape(4, 128)
-    sp1 = species.reshape(1, ATOMS)
+    pos = positions.transpose(1, 0, 2)
+    mom = momenta.transpose(1, 0, 2)
+    kinds = species.reshape(1, ATOMS)
     ghosts = ghost_rows.reshape(2, 128)
 
-    (own,) = call(first_kernel, [(24, 128)], [], (pos, mom, sp4, mass_table), (3,))
-    peer = lax.ppermute(own, "bead", [(b, b ^ 4) for b in range(BEADS)])
-    down, up = call(
-        send_kernel, [(8, 128)] * 2, [((4, 8, 128), f32)], (place, own, peer, sp4, species_scale, ghosts), (0, 4)
-    )
+    (mine,) = call(first_kernel, [(8, ATOMS)], [], (pos, mom, kinds, species_scale, mass_table), (3, 4))
+    halves = [[x * 8 + z * 4 + y for z in range(2)] for x in range(4) for y in range(4)]
+    pair = lax.all_gather(mine, "bead", axis=0, axis_index_groups=halves)
+    down, up = call(send_kernel, [(8, 128)] * 2, [((8, ATOMS), f32)], (pair, ghosts), ())
     below, above = exchange(down, up)
     block, weights = call(
         pack_kernel,
         [(16, 64, 128), (SLOTS, ATOMS)],
         [((64, 128), f32), ((8, 128), f32)],
-        (place, own, peer, below, above, sp4, species_scale, mass_table, neighbours),
-        (0, 6, 7),
+        (pair, below, above, neighbours),
+        (),
     )
     groups = [[x * 8 + z * 4 + y for x in range(4) for y in range(4)] for z in range(2)]
     gathered = lax.all_to_all(block, "bead", 0, 0, axis_index_groups=groups, tiled=True)
@@ -505,7 +516,7 @@
             ((96, 768), f32), ((96, ATOMS), f32), ((3, 16, 768), f32), offsets, ((NRBF, CB * ATOMS), f32),
             ((NRBF, CB * ATOMS), f32), ((3, 16, ATOMS), f32),
         ],
-        (gathered, neighbours, weights, sp1, mass_table, ghosts, w_in, w_out, first, reduce_),
+        (gathered, neighbours, weights, kinds, mass_table, ghosts, w_in, w_out, first, reduce_),
         (4,),
     )
     big = [((3 * 96, 512), bf16), ((96, ATOMS), f32)]
@@ -514,29 +525,29 @@
         middle_kernel,
         [(96, ATOMS), (96, ATOMS), (96, 128), (96, 128)],
         big,
-        (coords, veloc, below, above, neighbours, weights, sp1, species_scale, mass_table, ghosts, later),
+        (coords, veloc, below, above, neighbours, weights, kinds, species_scale, mass_table, ghosts, later),
         (7, 8),
     )
     below, above = exchange(down, up)
-    mine, contracted, down, up = call(
+    own, contracted, down, up = call(
         last_kernel,
         [(8, ATOMS), (16, ATOMS), (16, 128), (16, 128)],
         big + [((2 * BEADS, 3 * ATOMS), f32), ((16, ATOMS), f32)],
-        (place, coords, veloc, below, above, neighbours, weights, sp1, species_scale, mass_table, ghosts, later, reduce_),
+        (place, coords, veloc, below, above, neighbours, weights, kinds, species_scale, mass_table, ghosts, later, reduce_),
         (0, 8, 9),
     )
     below, above = exchange(down, up)
     new_pos, new_mom = call(
         end_kernel,
-        [(12, 128), (12, 128)],
+        [(3, 1, ATOMS), (3, 1, ATOMS)],
         [
             ((16, 768), f32), offsets, ((NRBF, CB * ATOMS), f32), ((NRBF, CB * ATOMS), f32),
             ((CB, 3, CHUNKS, 128), f32),
         ],
-        (place, expand, mine, contracted, below, above, neighbours, weights, sp4, species_scale, mass_table, w_in, w_out),
+        (place, expand, own, contracted, below, above, neighbours, weights, kinds, species_scale, mass_table, w_in, w_out),
         (0, 1, 9, 10),
     )
-    return new_pos.reshape(1, 3, ATOMS), new_mom.reshape(1, 3, ATOMS)
+    return new_pos.transpose(1, 0, 2), new_mom.transpose(1, 0, 2)
 
 
 def solution(mesh):

time: 103 us -> 85.2 us (0.83)
  blocking collectives: 0 us -> 12.7 us
  starting transfers between devices: 27.7 us -> 15.1 us
  Pallas kernels: 37.1 us -> 25.1 us
  local copies, waits for them, and re-layouts: 7.77 us -> 4.87 us
  waiting for transfers between devices: 27.5 us -> 26.2 us
  other arithmetic: 1.33 us -> 0.08 us
    ppermute x1 -> x0, starting transfers between devices: 12.7 us -> none  [body(): peer = lax.ppermute(own, 'bead', [(b, b ^ 4) for b in range(BEADS)])]
    all_gather x0 -> x1, blocking collectives: none -> 12.7 us  [body(): pair = lax.all_gather(mine, 'bead', axis=0, axis_index_groups=halves)]
    pallas_call x7, Pallas kernels: 37.1 us -> 25.1 us  [call(): pl.pallas_call(kernel, out_shape=shapes, in_specs=specs, out_specs=[pl.Bl...]
    reshape x4 -> x0, local copies, waits for them, and re-layouts: 3.13 us -> none  [the longest x2 1.92 us: body(): return (new_pos.reshape(1, 3, ATOMS), new_mom.reshape(1, 3, ATOMS))]
    ppermute x4, waiting for transfers between devices: 4.39 us -> 3.23 us  [exchange(): below = lax.ppermute(up, RING, ring(1))]
    unnamed x27 -> x33, local copies, waits for them, and re-layouts: 4.65 us -> 4.87 us
  transfers between devices with their start and end apart: 10 -> 9, of which waited for: 10 -> 9; matrix products, arithmetic and copies ran while one was open for 1% -> 0% of each run, Pallas kernels for 0% -> 0%
where the time goes in v2:
time: 85.2 us; the launch traced here: 84.8 us
  waiting for transfers between devices  26.2 us (31%)
  Pallas kernels  25.1 us (29%)
  starting transfers between devices  15.1 us (18%)
  blocking collectives  12.7 us (15%)
  local copies, waits for them, and re-layouts  4.87 us (6%)
    pallas_call x7, Pallas kernels, call(): pl.pallas_call(kernel, out_shape=shapes, in_specs=specs, out_specs=[pl.Bl...  25.1 us
    ppermute x4, waiting for transfers between devices, exchange(): above = lax.ppermute(down, RING, ring(-1))  13.7 us
    all_gather x1, blocking collectives, body(): pair = lax.all_gather(mine, 'bead', axis=0, axis_index_groups=halves)  12.7 us
    all_to_all x1, waiting for transfers between devices, body(): lax.all_to_all(block, 'bead', 0, 0, axis_index_groups=groups, tiled=True)  9.28 us
    ppermute x4, starting transfers between devices, exchange(): below = lax.ppermute(up, RING, ring(1))  7.22 us
    all_to_all x1, starting transfers between devices, body(): lax.all_to_all(block, 'bead', 0, 0, axis_index_groups=groups, tiled=True)  6.89 us
    unnamed x33, local copies, waits for them, and re-layouts  4.87 us
    ppermute x4, waiting for transfers between devices, exchange(): below = lax.ppermute(up, RING, ring(1))  3.23 us
  transfers between devices with their start and end apart: 9, of which 9 were waited for; matrix products, arithmetic and copies ran while one was open for 0% of the time, Pallas kernels for 0%

profile of v2, /device:TPU:97, one launch (start us, length us, event | category | flops | bytes accessed | tf_op | source)
XLA Modules:
  0.0 84.8 jit_solution(17542772544260289978)
XLA Ops:
  0.6 0.0 copy-start
  0.6 0.0 copy-start.3
  0.7 0.7 copy-done.3
  1.4 0.0 copy-start.9
  1.4 0.7 copy-done.9
  2.0 0.0 copy-start.11
  2.0 0.7 copy-done.11
  2.7 0.0 copy-start.13
  2.7 0.7 copy-done.13
  3.4 0.0 copy-start.14
  3.4 0.7 copy-done.14
  4.1 0.6 shard_map.140
  4.6 12.7 %all-gather = f32[16,512]{1,0:T(8,128)S(1)} all-gather(f32[8,512]{1,0:T(8,128)S(1)} %shard_map.140), channel_id=2, replica_groups={{0,64},{16,80},{32,96},{48,112},{128,192},{144,208},{160,224},{176,240}..., dimensions={0}, use_global_device_ids=true | all-gather | bytes 49152 | tf_op jit(solution)/shard_map/all_gather | solution.py:499
  17.4 0.0 copy-start.7
  17.4 0.7 copy-done.7
  18.0 0.1 shard_map.141
  18.1 3.8 %collective-permute-start = (f32[8,128]{1,0:T(8,128)S(1)}, f32[8,128]{1,0:T(8,128)S(1)}, u32[]{:S(2)}, u32[]{:S(2)}) collective-permute-start(f32[8,128]{1,0:T(8,128)S(1)} %get-tuple-element.20), channel_id=1, source_target_pairs={{0,1},{1,2},{2,3},{3,4},{4,5},{5,6},{6,7},{7,8},{8,9},{9,10},{10,1... | collective-permute-start | bytes 12296 | tf_op jit(solution)/shard_map/ppermute | solution.py:472
  22.0 0.0 collective-permute-start.1
  22.0 0.8 collective-permute-done.below
  22.7 3.5 %collective-permute-done.1.above = f32[8,128]{1,0:T(8,128)S(1)} collective-permute-done((f32[8,128]{1,0:T(8,128)S(1)}, f32[8,128]{1,0:T(8,128)S(1)}, u32[]{:S(2)}, u32[]{:S(2)}) %collective-permute-start.1) | collective-permute-done | bytes 4128 | tf_op jit(solution)/shard_map/ppermute | solution.py:473
  26.2 0.0 copy-done
  26.2 1.8 %shard_map.142 = (f32[16,64,128]{2,1,0:T(8,128)}, f32[32,512]{1,0:T(8,128)S(1)}) custom-call(f32[2,8,512]{2,1,0:T(8,128)S(1)} %bitcast.12, f32[8,128]{1,0:T(8,128)S(1)} %collective-permute-done.below, f32[8,128]{1,0:T(8,128)S(1)} %collective-permute-done.1.above, s32[32,512]{1,0:T(8,128)S(1)} %copy-done), custom_call_target="tpu_custom_call" | custom-call | tf_op jit(solution)/shard_map/pallas_call | solution.py:448
  28.0 0.0 copy-start.15
  28.0 0.0 copy-start.5
  28.0 0.0 copy-start.6
  28.0 6.9 %all-to-all-start = ((f32[16,64,128]{2,1,0:T(8,128)}), f32[16,64,128]{2,1,0:T(8,128)S(1)}, u32[]{:S(2)}, u32[]{:S(2)}) async-start(f32[16,64,128]{2,1,0:T(8,128)} %get-tuple-element.22), calls=%async_computation | async-start | bytes 1048576 | tf_op jit(solution)/shard_map/all_to_all | solution.py:510
  34.9 0.0 copy-done.15
  34.9 0.0 copy-start.2
  35.0 0.0 copy-start.4
  35.0 0.1 copy.15.w_in
  35.1 0.0 copy-start.10
  35.1 9.3 %all-to-all-done.gathered = f32[16,64,128]{2,1,0:T(8,128)S(1)} async-done(((f32[16,64,128]{2,1,0:T(8,128)}), f32[16,64,128]{2,1,0:T(8,128)S(1)}, u32[]{:S(2)}, u32[]{:S(2)}) %all-to-all-start) | async-done | bytes 524320 | tf_op jit(solution)/shard_map/all_to_all | solution.py:510
  44.4 0.0 copy-done.5
  44.4 0.0 copy-done.6
  44.4 0.0 copy-done.2
  44.4 0.0 copy-done.4
  44.4 0.0 copy-done.10
  44.4 4.3 %shard_map.143 = (f32[96,512]{1,0:T(8,128)S(1)}, f32[96,512]{1,0:T(8,128)S(1)}, f32[96,128]{1,0:T(8,128)S(1)}, f32[96,128]{1,0:T(8,128)S(1)}) custom-call(f32[16,64,128]{2,1,0:T(8,128)S(1)} %all-to-all-done.gathered, s32[32,512]{1,0:T(8,128)S(1)} %copy-done, f32[32,512]{1,0:T(8,128)S(1)} %get-tuple-element.23.weights, s32[1,512]{1,0:T(1,128)S(1)} %bitcast.14, ...), custom_call_target="tpu_custom_call" | custom-call | tf_op jit(solution)/shard_map/pallas_call | solution.py:448
  48.7 3.3 %collective-permute-start.2 = (f32[96,128]{1,0:T(8,128)S(1)}, f32[96,128]{1,0:T(8,128)S(1)}, u32[]{:S(2)}, u32[]{:S(2)}) collective-permute-start(f32[96,128]{1,0:T(8,128)S(1)} %get-tuple-element.26), channel_id=1, source_target_pairs={{0,1},{1,2},{2,3},{3,4},{4,5},{5,6},{6,7},{7,8},{8,9},{9,10},{10,1... | collective-permute-start | bytes 147464 | tf_op jit(solution)/shard_map/ppermute | solution.py:472
  52.1 0.0 collective-permute-start.3
  52.1 0.0 copy-start.1
  52.1 1.2 %collective-permute-done.2.below = f32[96,128]{1,0:T(8,128)S(1)} collective-permute-done((f32[96,128]{1,0:T(8,128)S(1)}, f32[96,128]{1,0:T(8,128)S(1)}, u32[]{:S(2)}, u32[]{:S(2)}) %collective-permute-start.2) | collective-permute-done | bytes 49184 | tf_op jit(solution)/shard_map/ppermute | solution.py:472
  53.2 3.5 %collective-permute-done.3.above = f32[96,128]{1,0:T(8,128)S(1)} collective-permute-done((f32[96,128]{1,0:T(8,128)S(1)}, f32[96,128]{1,0:T(8,128)S(1)}, u32[]{:S(2)}, u32[]{:S(2)}) %collective-permute-start.3) | collective-permute-done | bytes 49184 | tf_op jit(solution)/shard_map/ppermute | solution.py:473
  56.8 0.0 copy-start.12
  56.8 0.0 copy-done.1
  56.8 0.7 copy-done.12
  57.4 7.1 %shard_map.144 = (f32[96,512]{1,0:T(8,128)S(1)}, f32[96,512]{1,0:T(8,128)S(1)}, f32[96,128]{1,0:T(8,128)S(1)}, f32[96,128]{1,0:T(8,128)S(1)}) custom-call(f32[96,512]{1,0:T(8,128)S(1)} %get-tuple-element.24.coords, f32[96,512]{1,0:T(8,128)S(1)} %get-tuple-element.25.veloc, f32[96,128]{1,0:T(8,128)S(1)} %collective-permute-done.2.below, ...), custom_call_target="tpu_custom_call" | custom-call | tf_op jit(solution)/shard_map/pallas_call | solution.py:448
  64.6 0.0 collective-permute-start.4
  64.6 0.5 collective-permute-start.5
  65.1 0.1 pad_add_fusion.place
  65.2 0.6 collective-permute-done.4.below
  65.8 3.5 %collective-permute-done.5.above = f32[96,128]{1,0:T(8,128)S(1)} collective-permute-done((f32[96,128]{1,0:T(8,128)S(1)}, f32[96,128]{1,0:T(8,128)S(1)}, u32[]{:S(2)}, u32[]{:S(2)}) %collective-permute-start.5) | collective-permute-done | bytes 49184 | tf_op jit(solution)/shard_map/ppermute | solution.py:473
  69.3 0.0 copy-start.8
  69.3 7.2 %shard_map.145 = (f32[8,512]{1,0:T(8,128)S(1)}, f32[16,512]{1,0:T(8,128)S(1)}, f32[16,128]{1,0:T(8,128)S(1)}, f32[16,128]{1,0:T(8,128)S(1)}) custom-call(s32[4]{0:T(128)S(1)} %pad_add_fusion.place, f32[96,512]{1,0:T(8,128)S(1)} %get-tuple-element.28.coords, f32[96,512]{1,0:T(8,128)S(1)} %get-tuple-element.29.veloc, ...), custom_call_target="tpu_custom_call" | custom-call | tf_op jit(solution)/shard_map/pallas_call | solution.py:448
  76.5 0.0 collective-permute-start.6
  76.5 0.5 collective-permute-start.7
  77.0 0.7 collective-permute-done.6.below
  77.7 3.1 %collective-permute-done.7.above = f32[16,128]{1,0:T(8,128)S(1)} collective-permute-done((f32[16,128]{1,0:T(8,128)S(1)}, f32[16,128]{1,0:T(8,128)S(1)}, u32[]{:S(2)}, u32[]{:S(2)}) %collective-permute-start.7) | collective-permute-done | bytes 8224 | tf_op jit(solution)/shard_map/ppermute | solution.py:473
  80.8 0.0 copy-done.8
  80.8 4.0 %shard_map.146 = (f32[3,1,512]{2,1,0:T(1,128)}, f32[3,1,512]{2,1,0:T(1,128)}) custom-call(s32[4]{0:T(128)S(1)} %pad_add_fusion.place, f32[32,4]{1,0:T(8,128)S(1)} %copy-done.8, f32[8,512]{1,0:T(8,128)S(1)} %get-tuple-element.32.own, f32[16,512]{1,0:T(8,128)S(1)} %get-tuple-element.33.contracted, f32[16,128]{1,0:T(8,128)S(1)} %collective-permute-done.6.below, ...), custom_call_target="tpu_custom_call" | custom-call | tf_op jit(solution)/shard_map/pallas_call | solution.py:448
Async XLA Ops:
  0.6 25.6 %copy-start = (s32[32,512]{1,0:T(8,128)S(1)}, s32[32,512]{1,0:T(8,128)}, u32[]{:S(2)}) copy-start(s32[32,512]{1,0:T(8,128)} %neighbours.9) | copy-start | bytes 196612
  0.6 0.7 copy-start.3
  1.4 0.7 copy-start.9
  2.0 0.7 copy-start.11
  2.7 0.7 copy-start.13
  3.4 0.7 copy-start.14
  17.4 0.7 copy-start.7
  18.1 4.6 %collective-permute-start = (f32[8,128]{1,0:T(8,128)S(1)}, f32[8,128]{1,0:T(8,128)S(1)}, u32[]{:S(2)}, u32[]{:S(2)}) collective-permute-start(f32[8,128]{1,0:T(8,128)S(1)} %get-tuple-element.20), channel_id=1, source_target_pairs={{0,1},{1,2},{2,3},{3,4},{4,5},{5,6},{6,7},{7,8},{8,9},{9,10},{10,1... | collective-permute-start | bytes 12296 | tf_op jit(solution)/shard_map/ppermute | solution.py:472
  22.0 4.2 %collective-permute-start.1 = (f32[8,128]{1,0:T(8,128)S(1)}, f32[8,128]{1,0:T(8,128)S(1)}, u32[]{:S(2)}, u32[]{:S(2)}) collective-permute-start(f32[8,128]{1,0:T(8,128)S(1)} %get-tuple-element.21), channel_id=1, source_target_pairs={{0,79},{1,0},{2,1},{3,2},{4,3},{5,4},{6,5},{7,6},{8,7},{9,8},{10,9... | collective-permute-start | bytes 12296 | tf_op jit(solution)/shard_map/ppermute | solution.py:473
  28.0 6.9 %copy-start.15 = (f32[128,8]{0,1:T(8,128)S(1)}, f32[128,8]{0,1:T(8,128)}, u32[]{:S(2)}) copy-start(f32[128,8]{0,1:T(8,128)} %param.20) | copy-start | bytes 12292
  28.0 16.3 %copy-start.5 = (f32[8,128]{1,0:T(8,128)S(1)}, f32[8,128]{1,0:T(8,128)}, u32[]{:S(2)}) copy-start(f32[8,128]{1,0:T(8,128)} %w_out.3) | copy-start | bytes 12292
  28.0 16.3 %copy-start.6 = (bf16[16,96]{1,0:T(8,128)(2,1)S(1)}, bf16[16,96]{1,0:T(8,128)(2,1)}, u32[]{:S(2)}) copy-start(bf16[16,96]{1,0:T(8,128)(2,1)} %constant.73.clone.reduce_) | copy-start | bytes 9220
  28.0 16.3 %all-to-all-start = ((f32[16,64,128]{2,1,0:T(8,128)}), f32[16,64,128]{2,1,0:T(8,128)S(1)}, u32[]{:S(2)}, u32[]{:S(2)}) async-start(f32[16,64,128]{2,1,0:T(8,128)} %get-tuple-element.22), calls=%async_computation | async-start | bytes 1048576 | tf_op jit(solution)/shard_map/all_to_all | solution.py:510
  34.9 9.4 %copy-start.2 = (bf16[64,480]{1,0:T(8,128)(2,1)S(1)}, bf16[64,480]{1,0:T(8,128)(2,1)}, u32[]{:S(2)}) copy-start(bf16[64,480]{1,0:T(8,128)(2,1)} %constant.71.clone.first) | copy-start | bytes 184324
  35.0 9.4 %copy-start.4 = (s32[512]{0:T(512)S(1)}, s32[512]{0:T(512)}, u32[]{:S(2)}) copy-start(s32[512]{0:T(512)} %param.17) | copy-start | bytes 6148
  35.1 9.3 %copy-start.10 = (f32[2]{0:T(128)S(1)}, f32[2]{0:T(128)}, u32[]{:S(2)}) copy-start(f32[2]{0:T(128)} %mass_table.9) | copy-start | bytes 28
  48.7 4.5 %collective-permute-start.2 = (f32[96,128]{1,0:T(8,128)S(1)}, f32[96,128]{1,0:T(8,128)S(1)}, u32[]{:S(2)}, u32[]{:S(2)}) collective-permute-start(f32[96,128]{1,0:T(8,128)S(1)} %get-tuple-element.26), channel_id=1, source_target_pairs={{0,1},{1,2},{2,3},{3,4},{4,5},{5,6},{6,7},{7,8},{8,9},{9,10},{10,1... | collective-permute-start | bytes 147464 | tf_op jit(solution)/shard_map/ppermute | solution.py:472
  52.1 4.7 %collective-permute-start.3 = (f32[96,128]{1,0:T(8,128)S(1)}, f32[96,128]{1,0:T(8,128)S(1)}, u32[]{:S(2)}, u32[]{:S(2)}) collective-permute-start(f32[96,128]{1,0:T(8,128)S(1)} %get-tuple-element.27), channel_id=1, source_target_pairs={{0,79},{1,0},{2,1},{3,2},{4,3},{5,4},{6,5},{7,6},{8,7},{9,8},{10,9... | collective-permute-start | bytes 147464 | tf_op jit(solution)/shard_map/ppermute | solution.py:473
  52.1 4.7 %copy-start.1 = (bf16[64,384]{1,0:T(8,128)(2,1)S(1)}, bf16[64,384]{1,0:T(8,128)(2,1)}, u32[]{:S(2)}) copy-start(bf16[64,384]{1,0:T(8,128)(2,1)} %constant.72.clone.later) | copy-start | bytes 147460
  56.8 0.7 copy-start.12
  64.6 1.2 %collective-permute-start.4 = (f32[96,128]{1,0:T(8,128)S(1)}, f32[96,128]{1,0:T(8,128)S(1)}, u32[]{:S(2)}, u32[]{:S(2)}) collective-permute-start(f32[96,128]{1,0:T(8,128)S(1)} %get-tuple-element.30), channel_id=1, source_target_pairs={{0,1},{1,2},{2,3},{3,4},{4,5},{5,6},{6,7},{7,8},{8,9},{9,10},{10,1... | collective-permute-start | bytes 147464 | tf_op jit(solution)/shard_map/ppermute | solution.py:472
  64.6 4.7 %collective-permute-start.5 = (f32[96,128]{1,0:T(8,128)S(1)}, f32[96,128]{1,0:T(8,128)S(1)}, u32[]{:S(2)}, u32[]{:S(2)}) collective-permute-start(f32[96,128]{1,0:T(8,128)S(1)} %get-tuple-element.31), channel_id=1, source_target_pairs={{0,79},{1,0},{2,1},{3,2},{4,3},{5,4},{6,5},{7,6},{8,7},{9,8},{10,9... | collective-permute-start | bytes 147464 | tf_op jit(solution)/shard_map/ppermute | solution.py:473
  69.3 11.5 %copy-start.8 = (f32[32,4]{1,0:T(8,128)S(1)}, f32[32,4]{1,0:T(8,128)}, u32[]{:S(2)}) copy-start(f32[32,4]{1,0:T(8,128)} %constant.74.clone.expand) | copy-start | bytes 1540
  76.5 1.2 %collective-permute-start.6 = (f32[16,128]{1,0:T(8,128)S(1)}, f32[16,128]{1,0:T(8,128)S(1)}, u32[]{:S(2)}, u32[]{:S(2)}) collective-permute-start(f32[16,128]{1,0:T(8,128)S(1)} %get-tuple-element.34), channel_id=1, source_target_pairs={{0,1},{1,2},{2,3},{3,4},{4,5},{5,6},{6,7},{7,8},{8,9},{9,10},{10,1... | collective-permute-start | bytes 24584 | tf_op jit(solution)/shard_map/ppermute | solution.py:472
  76.5 4.3 %collective-permute-start.7 = (f32[16,128]{1,0:T(8,128)S(1)}, f32[16,128]{1,0:T(8,128)S(1)}, u32[]{:S(2)}, u32[]{:S(2)}) collective-permute-start(f32[16,128]{1,0:T(8,128)S(1)} %get-tuple-element.35), channel_id=1, source_target_pairs={{0,79},{1,0},{2,1},{3,2},{4,3},{5,4},{6,5},{7,6},{8,7},{9,8},{10,9... | collective-permute-start | bytes 24584 | tf_op jit(solution)/shard_map/ppermute | solution.py:473

commit v3 on v2

--- a/solution.py
+++ b/solution.py
@@ -175,7 +175,13 @@
 
 
 def learned_by_lanes(table, neighbours, weights, w_in, w_out, offsets, messages, radials, store):
-    for c in range(CB):
+    high = w_in[...].astype(bf16).astype(f32)
+    first = jnp.concatenate([high, w_in[...] - high, high, jnp.zeros_like(high)], axis=0).astype(bf16)
+    high = w_out[...].astype(bf16).astype(f32)
+    second = jnp.concatenate([high, w_out[...] - high, high], axis=1)
+    second = jnp.concatenate([second, jnp.zeros_like(second)], axis=0).astype(bf16)
+
+    def message(c):
         for a in range(CHUNKS):
             rows = [[row8(table(c, x, k)) for k in range(WINDOW)] for x in range(3)]
             total = [jnp.zeros((8, 128), f32) for _ in range(NRBF)]
@@ -188,17 +194,22 @@
                 w = weights[8 * g : 8 * g + 8, 128 * a : 128 * a + 128]
                 for r, basis in enumerate(powers(squared)):
                     total[r] = total[r] + w * basis
-            at = c * ATOMS + a * 128
             for r in range(NRBF):
-                messages[r : r + 1, at : at + 128] = jnp.sum(total[r], axis=0, keepdims=True) * (1.0 / SLOTS)
-    highest = lax.Precision.HIGHEST
-    hidden = jnp.dot(w_in[...], messages[...], precision=highest, preferred_element_type=f32)
-    hidden = hidden * (1.0 / (1.0 + jnp.exp(-hidden)))
-    radials[...] = jnp.dot(w_out[...], hidden, precision=highest, preferred_element_type=f32)
-    for c in range(CB):
+                messages[c, r : r + 1, 128 * a : 128 * a + 128] = jnp.sum(total[r], axis=0, keepdims=True) * (
+                    1.0 / SLOTS
+                )
+
+    def network(c):
+        value = messages[c]
+        high = value.astype(bf16).astype(f32)
+        terms = jnp.concatenate([high, high, value - high, jnp.zeros_like(high)], axis=0).astype(bf16)
+        hidden = lax.dot_general(first, terms, (((0,), (0,)), ((), ())), preferred_element_type=f32)
+        hidden = hidden * (1.0 / (1.0 + jnp.exp(-hidden)))
+        radials[c] = jnp.dot(second, split_rows(hidden), preferred_element_type=f32)[0:NRBF]
+
+    def force(c):
         for a in range(CHUNKS):
-            at = c * ATOMS + a * 128
-            radial = [row8(radials[r : r + 1, at : at + 128]) for r in range(NRBF)]
+            radial = [row8(radials[c, r : r + 1, 128 * a : 128 * a + 128]) for r in range(NRBF)]
             total = [jnp.zeros((8, 128), f32) for _ in range(3)]
             for g in range(SLOTS // 8):
                 offset = [offsets[c, a, g, x] for x in range(3)]
@@ -213,48 +224,91 @@
             for x in range(3):
                 store(c, x, a, jnp.sum(total[x], axis=0, keepdims=True))
 
-
-def cheap_by_matmul(coords, below, above, neighbours, weights, stacked, total):
-    rows = 3 * BEADS
-    parts = (
-        jnp.concatenate([below[...], coords[:, 0:128]], axis=1),
-        coords[:, 128:384],
-        jnp.concatenate([coords[:, 384:512], above[...]], axis=1),
-    )
-    for k, part in enumerate(parts):
-        high = part.astype(bf16)
-        stacked[k * rows : (k + 1) * rows, 0:256] = high
-        stacked[k * rows : (k + 1) * rows, 256:512] = (part - high.astype(f32)).astype(bf16)
-    rounded = coords[...].astype(bf16).astype(f32)
-    rounded = rounded + (coords[...] - rounded).astype(bf16).astype(f32)
+    message(0)
+    for c in range(CB):
+        network(c)
+        if c + 1 < CB:
+            message(c + 1)
+        force(c)
+
+
+def cheap_of_all(coords, below, above, neighbours, weights, stacked, total, table, sums):
+    few = BEADS - 8
+    rows = 3 * few
+
+    def of_few(value):
+        return jnp.concatenate([value[BEADS * x : BEADS * x + few] for x in range(3)], axis=0)
+
+    own, low, high_ = of_few(coords), of_few(below), of_few(above)
+    stack = jnp.concatenate(
+        [
+            jnp.concatenate([low, own[:, 0:128]], axis=1),
+            own[:, 128:384],
+            jnp.concatenate([own[:, 384:512], high_], axis=1),
+            jnp.zeros((8, 256), f32),
+        ],
+        axis=0,
+    )
+    high = stack.astype(bf16)
+    stacked[:, 0:256] = high
+    stacked[:, 256:512] = (stack - high.astype(f32)).astype(bf16)
+    rounded = own.astype(bf16).astype(f32)
+    rounded = rounded + (own - rounded).astype(bf16).astype(f32)
+    for x in range(3):
+        at = slice(BEADS * x + few, BEADS * (x + 1))
+        table[8 * x : 8 * x + 8, 0:128] = below[at]
+        table[8 * x : 8 * x + 8, 128:640] = coords[at]
+        table[8 * x : 8 * x + 8, 640:768] = above[at]
     total[...] = jnp.zeros_like(total)
-    unroll = 8
+    sums[...] = jnp.zeros_like(sums)
     place = lax.broadcasted_iota(jnp.int16, (256, ATOMS), 0)
 
-    def group(i, _):
-        for j in range(unroll):
-            slot = i * unroll + j
-            index = neighbours[pl.ds(slot, 1), :]
-            column = jnp.broadcast_to(index & 255, (16, ATOMS)).astype(jnp.int16)
-            chosen = jnp.where(place == jnp.tile(column, (16, 1)), bf16(1), bf16(0))
-            picked = jnp.dot(
-                stacked[...], jnp.concatenate([chosen, chosen], axis=0), preferred_element_type=f32
-            )
-            part = index >> 8
-            other = jnp.where(
-                part == 0,
-                picked[0:rows],
-                jnp.where(part == 1, picked[rows : 2 * rows], picked[2 * rows : 3 * rows]),
-            )
-            offset = other - rounded
-            x, y, z = offset[0:BEADS], offset[BEADS : 2 * BEADS], offset[2 * BEADS :]
-            w = weights[pl.ds(slot, 1), :] * jnp.exp(-(x * x + y * y + z * z))
-            total[0:BEADS] += w * x
-            total[BEADS : 2 * BEADS] += w * y
-            total[2 * BEADS :] += w * z
+    def by_matmul(slot):
+        index = neighbours[pl.ds(slot, 1), :]
+        column = jnp.broadcast_to(index & 255, (16, ATOMS)).astype(jnp.int16)
+        chosen = jnp.where(place == jnp.tile(column, (16, 1)), bf16(1), bf16(0))
+        picked = jnp.dot(stacked[...], jnp.concatenate([chosen, chosen], axis=0), preferred_element_type=f32)
+        part = index >> 8
+        other = jnp.where(
+            part == 0,
+            picked[0:rows],
+            jnp.where(part == 1, picked[rows : 2 * rows], picked[2 * rows : 3 * rows]),
+        )
+        offset = other - rounded
+        x, y, z = offset[0:few], offset[few : 2 * few], offset[2 * few :]
+        w = weights[pl.ds(slot, 1), :] * jnp.exp(-(x * x + y * y + z * z))
+        total[0:few] += w * x
+        total[BEADS : BEADS + few] += w * y
+        total[2 * BEADS : 2 * BEADS + few] += w * z
+
+    def by_lanes(g, a):
+        at = slice(128 * a, 128 * a + 128)
+        slots = pl.ds(pl.multiple_of(8 * g, 8), 8)
+        index = neighbours[slots, at]
+        lane, masks = index & 127, [(index >> 7) == k for k in range(1, WINDOW)]
+        weight = weights[slots, at]
+        for bead in range(8):
+            rows_of = lambda x, k: row8(table[8 * x + bead : 8 * x + bead + 1, 128 * k : 128 * k + 128])
+            offset = [
+                looked_up([rows_of(x, k) for k in range(WINDOW)], lane, masks) - rows_of(x, 1 + a)
+                for x in range(3)
+            ]
+            w = weight * jnp.exp(-(offset[0] * offset[0] + offset[1] * offset[1] + offset[2] * offset[2]))
+            for x in range(3):
+                sums[8 * x + bead, :, at] += w * offset[x]
+
+    def group(g, _):
+        for j in range(8):
+            by_matmul(g * 8 + j)
+            if j % 2:
+                by_lanes(g, j // 2)
         return 0
 
-    lax.fori_loop(0, SLOTS // unroll, group, 0)
+    lax.fori_loop(0, SLOTS // 8, group, 0)
+    for x in range(3):
+        for bead in range(8):
+            row = BEADS * x + few + bead
+            total[row : row + 1] = jnp.sum(sums[8 * x + bead], axis=0, keepdims=True)
 
 
 def propagated(coords, veloc, table, extra=None):
@@ -268,13 +322,28 @@
     return dot6(table[...], jnp.concatenate(wide, axis=1))
 
 
-def first_kernel(pos, mom, species, scale, mass_table, out):
-    inverse = by_species(species[...], [1.0 / mass_table[0], 1.0 / mass_table[1]])
+def first_kernel(
+    pos, mom, species, ghost_rows, scale, mass_table, out, ghosts, pos_in, mom_in, species_in, scale_in, mass_in, sems
+):
+    copies = [
+        pltpu.make_async_copy(source, target, sems.at[i])
+        for i, (source, target) in enumerate(
+            (
+                (scale, scale_in), (mass_table, mass_in), (species, species_in), (mom, mom_in), (pos, pos_in),
+                (ghost_rows, ghosts),
+            )
+        )
+    ]
+    for copy in copies:
+        copy.start()
+    for copy in copies:
+        copy.wait()
+    mass = by_species(species_in[...], mass_in)
     for x in range(3):
-        out[x : x + 1] = pos[x]
-        out[3 + x : 4 + x] = mom[x] * inverse
-    out[6:7] = by_species(species[...], scale)
-    out[7:8] = inverse
+        out[x : x + 1] = pos_in[x]
+        out[3 + x : 4 + x] = mom_in[x] / mass
+    out[6:7] = by_species(species_in[...], scale_in)
+    out[7:8] = mass
 
 
 def send_kernel(pair, ghost_rows, down, up, rows):
@@ -309,7 +378,7 @@
             weights[8 * g : 8 * g + 8, 128 * a : 128 * a + 128] = jnp.where(index == itself, 0.0, q)
     for a in range(CHUNKS):
         at = slice(128 * a, 128 * a + 128)
-        gain = pair[0, 6:7, at] * pair[0, 7:8, at] * (0.5 * inner_step)
+        gain = pair[0, 6:7, at] / pair[0, 7:8, at] * (0.5 * inner_step)
         for k in range(2):
             base = 32 * k
             force = cheap_by_lanes(
@@ -323,11 +392,11 @@
 
 
 def begin_kernel(
-    gathered, neighbours, weights, species, mass_table, ghost_rows, w_in, w_out, first, reduce_,
+    gathered, neighbours, weights, mine, ghost_rows, w_in, w_out, first, reduce_,
     coords, veloc, down, up,
     window, start, contracted, offsets, messages, radials, slow,
 ):
-    inverse = by_species(species[...], [1.0 / mass_table[0], 1.0 / mass_table[1]])
+    inverse = 1.0 / mine[7:8]
     for z in range(2):
         for x in range(3):
             at = slice(x * BEADS + 16 * z, x * BEADS + 16 * z + 16)
@@ -363,30 +432,25 @@
         up[8 * i : 8 * i + 8] = ghosts_of(chunk, ghost_rows[1:2])
 
 
-def kicked(coords, veloc, below, above, neighbours, weights, species, scale, mass_table, stacked, total):
-    cheap_by_matmul(coords, below, above, neighbours, weights, stacked, total)
-    gain = by_species(species[...], [scale[0] / mass_table[0], scale[1] / mass_table[1]]) * inner_step
-    return veloc[...] + gain * total[...]
+def kicked(coords, veloc, below, above, neighbours, weights, mine, scratch):
+    total = scratch[1]
+    cheap_of_all(coords, below, above, neighbours, weights, *scratch)
+    return veloc[...] + inner_step * mine[6:7] / mine[7:8] * total[...]
 
 
 def middle_kernel(
-    coords, veloc, below, above, neighbours, weights, species, scale, mass_table, ghost_rows, later,
-    new_coords, new_veloc, down, up, stacked, total,
+    coords, veloc, below, above, neighbours, weights, mine, ghost_rows, later, new_coords, new_veloc, down, up, *scratch
 ):
-    velocities = kicked(
-        coords, veloc, below, above, neighbours, weights, species, scale, mass_table, stacked, total
-    )
+    velocities = kicked(coords, veloc, below, above, neighbours, weights, mine, scratch)
     moved = propagated(coords[...], velocities, later)
     finish_step(moved, new_coords, new_veloc, ghost_rows, down, up)
 
 
 def last_kernel(
-    place, coords, veloc, below, above, neighbours, weights, species, scale, mass_table, ghost_rows, later,
-    reduce_, own, contracted, down, up, stacked, total, moved, rows,
+    place, coords, veloc, below, above, neighbours, weights, mine, ghost_rows, later, reduce_,
+    own, contracted, down, up, moved, rows, *scratch,
 ):
-    velocities = kicked(
-        coords, veloc, below, above, neighbours, weights, species, scale, mass_table, stacked, total
-    )
+    velocities = kicked(coords, veloc, below, above, neighbours, weights, mine, scratch)
     moved[...] = propagated(coords[...], velocities, later)
     small = dot3(reduce_[...], moved[0:BEADS, :])
     for x in range(3):
@@ -394,7 +458,7 @@
         own[x : x + 1] = moved[pl.ds(place[1], 1), at]
         own[3 + x : 4 + x] = moved[pl.ds(BEADS + place[1], 1), at]
         contracted[4 * x : 4 * x + 4] = small[0:4, at]
-    own[6:8] = jnp.zeros((2, ATOMS), f32)
+    own[6:8] = mine[6:8]
     contracted[12:16] = jnp.zeros((4, ATOMS), f32)
     rows[0:12] = contracted[0:12]
     for which, out in ((2, down), (3, up)):
@@ -409,12 +473,11 @@
 
 
 def end_kernel(
-    place, expand, own, contracted, below, above, neighbours, weights, species, scale, mass_table, w_in, w_out,
+    place, expand, own, contracted, below, above, neighbours, weights, w_in, w_out,
     new_pos, new_mom,
     window, offsets, messages, radials, slow,
 ):
-    charge = by_species(species[...], scale)
-    mass = by_species(species[...], mass_table)
+    charge, mass = own[6:7], own[7:8]
     window[0:16, 0:128] = below[...]
     window[0:16, 640:768] = above[...]
     window[0:12, 128:640] = contracted[0:12]
@@ -440,17 +503,15 @@
             new_pos[x, :, at] = own[x : x + 1, at]
 
 
-def call(kernel, outs, scratch, args, scalars):
-    specs = [
-        pl.BlockSpec(memory_space=pltpu.SMEM if i in scalars else pltpu.VMEM) for i in range(len(args))
-    ]
-    shapes = [jax.ShapeDtypeStruct(s, f32) for s in outs]
+def call(kernel, outs, scratch, args, scalars=(), space=pltpu.VMEM):
+    specs = [pl.BlockSpec(memory_space=pltpu.SMEM if i in scalars else space) for i in range(len(args))]
+    shapes = [s if isinstance(s, jax.ShapeDtypeStruct) else jax.ShapeDtypeStruct(s, f32) for s in outs]
     return pl.pallas_call(
         kernel,
         out_shape=shapes,
         in_specs=specs,
         out_specs=[pl.BlockSpec(memory_space=pltpu.VMEM)] * len(outs),
-        scratch_shapes=[pltpu.VMEM(s, d) for s, d in scratch],
+        scratch_shapes=[pltpu.VMEM(*s) if isinstance(s, tuple) else s for s in scratch],
         compiler_params=pltpu.CompilerParams(vmem_limit_bytes=VMEM_LIMIT),
     )(*args)
 
@@ -494,7 +555,16 @@
     kinds = species.reshape(1, ATOMS)
     ghosts = ghost_rows.reshape(2, 128)
 
-    (mine,) = call(first_kernel, [(8, ATOMS)], [], (pos, mom, kinds, species_scale, mass_table), (3, 4))
+    mine, ghosts = call(
+        first_kernel,
+        [(8, ATOMS), jax.ShapeDtypeStruct((2, 128), jnp.int32)],
+        [
+            ((3, 1, ATOMS), f32), ((3, 1, ATOMS), f32), ((1, ATOMS), jnp.int32),
+            pltpu.SMEM((2,), f32), pltpu.SMEM((2,), f32), pltpu.SemaphoreType.DMA((6,)),
+        ],
+        (pos, mom, kinds, ghosts, species_scale, mass_table),
+        space=pltpu.HBM,
+    )
     halves = [[x * 8 + z * 4 + y for z in range(2)] for x in range(4) for y in range(4)]
     pair = lax.all_gather(mine, "bead", axis=0, axis_index_groups=halves)
     down, up = call(send_kernel, [(8, 128)] * 2, [((8, ATOMS), f32)], (pair, ghosts), ())
@@ -509,43 +579,40 @@
     groups = [[x * 8 + z * 4 + y for x in range(4) for y in range(4)] for z in range(2)]
     gathered = lax.all_to_all(block, "bead", 0, 0, axis_index_groups=groups, tiled=True)
     offsets = ((CB, CHUNKS, SLOTS // 8, 3, 8, 128), f32)
+    network = ((CB, NRBF, ATOMS), f32)
+    w_in = w_in.T
     coords, veloc, down, up = call(
         begin_kernel,
         [(96, ATOMS), (96, ATOMS), (96, 128), (96, 128)],
         [
-            ((96, 768), f32), ((96, ATOMS), f32), ((3, 16, 768), f32), offsets, ((NRBF, CB * ATOMS), f32),
-            ((NRBF, CB * ATOMS), f32), ((3, 16, ATOMS), f32),
+            ((96, 768), f32), ((96, ATOMS), f32), ((3, 16, 768), f32), offsets, network, network,
+            ((3, 16, ATOMS), f32),
         ],
-        (gathered, neighbours, weights, kinds, mass_table, ghosts, w_in, w_out, first, reduce_),
-        (4,),
-    )
-    big = [((3 * 96, 512), bf16), ((96, ATOMS), f32)]
+        (gathered, neighbours, weights, mine, ghosts, w_in, w_out, first, reduce_),
+    )
+    big = [((3 * 72 + 8, 512), bf16), ((96, ATOMS), f32), ((24, 768), f32), ((24, 8, ATOMS), f32)]
     below, above = exchange(down, up)
     coords, veloc, down, up = call(
         middle_kernel,
         [(96, ATOMS), (96, ATOMS), (96, 128), (96, 128)],
         big,
-        (coords, veloc, below, above, neighbours, weights, kinds, species_scale, mass_table, ghosts, later),
-        (7, 8),
+        (coords, veloc, below, above, neighbours, weights, mine, ghosts, later),
     )
     below, above = exchange(down, up)
     own, contracted, down, up = call(
         last_kernel,
         [(8, ATOMS), (16, ATOMS), (16, 128), (16, 128)],
-        big + [((2 * BEADS, 3 * ATOMS), f32), ((16, ATOMS), f32)],
-        (place, coords, veloc, below, above, neighbours, weights, kinds, species_scale, mass_table, ghosts, later, reduce_),
-        (0, 8, 9),
+        [((2 * BEADS, 3 * ATOMS), f32), ((16, ATOMS), f32)] + big,
+        (place, coords, veloc, below, above, neighbours, weights, mine, ghosts, later, reduce_),
+        (0,),
     )
     below, above = exchange(down, up)
     new_pos, new_mom = call(
         end_kernel,
         [(3, 1, ATOMS), (3, 1, ATOMS)],
-        [
-            ((16, 768), f32), offsets, ((NRBF, CB * ATOMS), f32), ((NRBF, CB * ATOMS), f32),
-            ((CB, 3, CHUNKS, 128), f32),
-        ],
-        (place, expand, own, contracted, below, above, neighbours, weights, kinds, species_scale, mass_table, w_in, w_out),
-        (0, 1, 9, 10),
+        [((16, 768), f32), offsets, network, network, ((CB, 3, CHUNKS, 128), f32)],
+        (place, expand, own, contracted, below, above, neighbours, weights, w_in, w_out),
+        (0, 1),
     )
     return new_pos.transpose(1, 0, 2), new_mom.transpose(1, 0, 2)
 

time: 85.2 us -> 79.4 us (0.932)
  blocking collectives: 12.7 us -> 28.8 us
  waiting for transfers between devices: 26.2 us -> 16.9 us
  starting transfers between devices: 15.1 us -> 8.22 us
  Pallas kernels: 25.1 us -> 20.3 us
    all_to_all x0 -> x1, blocking collectives: none -> 16.1 us  [body(): lax.all_to_all(block, 'bead', 0, 0, axis_index_groups=groups, tiled=True)]
    all_to_all x1 -> x0, waiting for transfers between devices: 9.28 us -> none  [body(): lax.all_to_all(block, 'bead', 0, 0, axis_index_groups=groups, tiled=True)]
    all_to_all x1 -> x0, starting transfers between devices: 6.89 us -> none  [body(): lax.all_to_all(block, 'bead', 0, 0, axis_index_groups=groups, tiled=True)]
    pallas_call x7, Pallas kernels: 25.1 us -> 20.3 us  [call(): pl.pallas_call(kernel, out_shape=shapes, in_specs=specs, out_specs=[pl.Bl...]
    unnamed x33 -> x26, local copies, waits for them, and re-layouts: 4.87 us -> 4.07 us
  transfers between devices with their start and end apart: 9 -> 8, of which waited for: 9 -> 8; matrix products, arithmetic and copies ran while one was open for 0% -> 0% of each run, Pallas kernels for 0% -> 0%
where the time goes in v3:
time: 79.4 us; the launch traced here: 79.1 us
  blocking collectives  28.8 us (36%)
  Pallas kernels  20.3 us (26%)
  waiting for transfers between devices  16.9 us (21%)
  starting transfers between devices  8.22 us (10%)
  local copies, waits for them, and re-layouts  4.07 us (5%)
    pallas_call x7, Pallas kernels, call(): pl.pallas_call(kernel, out_shape=shapes, in_specs=specs, out_specs=[pl.Bl...  20.3 us
    all_to_all x1, blocking collectives, body(): lax.all_to_all(block, 'bead', 0, 0, axis_index_groups=groups, tiled=True)  16.1 us
    ppermute x4, waiting for transfers between devices, exchange(): above = lax.ppermute(down, RING, ring(-1))  13.7 us
    all_gather x1, blocking collectives, body(): pair = lax.all_gather(mine, 'bead', axis=0, axis_index_groups=halves)  12.7 us
    ppermute x4, starting transfers between devices, exchange(): below = lax.ppermute(up, RING, ring(1))  7.21 us
    unnamed x26, local copies, waits for them, and re-layouts  4.07 us
    ppermute x4, waiting for transfers between devices, exchange(): below = lax.ppermute(up, RING, ring(1))  3.23 us
  transfers between devices with their start and end apart: 8, of which 8 were waited for; matrix products, arithmetic and copies ran while one was open for 0% of the time, Pallas kernels for 0%

profile of v3, /device:TPU:97, one launch (start us, length us, event | category | flops | bytes accessed | tf_op | source)
XLA Modules:
  0.0 79.1 jit_solution(4460133304106265674)
XLA Ops:
  0.6 0.0 copy-start.7
  0.6 0.0 copy-start
  0.7 0.7 copy-done.7
  1.3 0.0 copy-start.8
  1.3 0.7 copy-done.8
  2.0 0.0 copy-start.9
  2.0 0.7 copy-done.9
  2.7 0.0 copy-start.10
  2.7 0.7 copy-done.10
  3.4 0.0 copy-start.11
  3.4 0.7 copy-done.11
  4.0 0.0 copy-start.12
  4.0 0.7 copy-done.12
  4.7 0.6 shard_map.140
  5.3 12.7 %all-gather = f32[16,512]{1,0:T(8,128)S(1)} all-gather(f32[8,512]{1,0:T(8,128)S(1)} %get-tuple-element.22.mine), channel_id=2, replica_groups={{0,64},{16,80},{32,96},{48,112},{128,192},{144,208},{160,224},{176,240}..., dimensions={0}, use_global_device_ids=true | all-gather | bytes 49152 | tf_op jit(solution)/shard_map/all_gather | solution.py:569
  18.0 0.1 shard_map.141
  18.1 3.9 %collective-permute-start = (f32[8,128]{1,0:T(8,128)S(1)}, f32[8,128]{1,0:T(8,128)S(1)}, u32[]{:S(2)}, u32[]{:S(2)}) collective-permute-start(f32[8,128]{1,0:T(8,128)S(1)} %get-tuple-element.24), channel_id=1, source_target_pairs={{0,1},{1,2},{2,3},{3,4},{4,5},{5,6},{6,7},{7,8},{8,9},{9,10},{10,1... | collective-permute-start | bytes 12296 | tf_op jit(solution)/shard_map/ppermute | solution.py:533
  22.0 0.0 collective-permute-start.1
  22.0 0.8 collective-permute-done.below
  22.7 3.5 %collective-permute-done.1.above = f32[8,128]{1,0:T(8,128)S(1)} collective-permute-done((f32[8,128]{1,0:T(8,128)S(1)}, f32[8,128]{1,0:T(8,128)S(1)}, u32[]{:S(2)}, u32[]{:S(2)}) %collective-permute-start.1) | collective-permute-done | bytes 4128 | tf_op jit(solution)/shard_map/ppermute | solution.py:534
  26.2 0.0 copy-done
  26.2 1.0 %shard_map.142 = (f32[16,64,128]{2,1,0:T(8,128)S(1)}, f32[32,512]{1,0:T(8,128)S(1)}) custom-call(f32[2,8,512]{2,1,0:T(8,128)S(1)} %bitcast.13, f32[8,128]{1,0:T(8,128)S(1)} %collective-permute-done.below, f32[8,128]{1,0:T(8,128)S(1)} %collective-permute-done.1.above, s32[32,512]{1,0:T(8,128)S(1)} %copy-done), custom_call_target="tpu_custom_call" | custom-call | tf_op jit(solution)/shard_map/pallas_call | solution.py:509
  27.2 0.0 copy-start.2
  27.2 0.0 copy-start.3
  27.2 0.0 copy-start.4
  27.3 0.0 copy-start.5
  27.3 16.1 %all_to_all.5.gathered = f32[16,64,128]{2,1,0:T(8,128)S(1)} all-to-all(f32[16,64,128]{2,1,0:T(8,128)S(1)} %get-tuple-element.26), channel_id=1, replica_groups={{0,16,32,48,128,144,160,176,256,272,288,304,384,400,416,432},{64,80,96,..., dimensions={0} | all-to-all | bytes 1048576 | tf_op jit(solution)/shard_map/all_to_all | solution.py:580
  43.4 0.0 copy-done.2
  43.4 0.0 copy-done.3
  43.4 0.0 copy-done.4
  43.4 0.0 copy-done.5
  43.4 3.2 %shard_map.143 = (f32[96,512]{1,0:T(8,128)S(1)}, f32[96,512]{1,0:T(8,128)S(1)}, f32[96,128]{1,0:T(8,128)S(1)}, f32[96,128]{1,0:T(8,128)S(1)}) custom-call(f32[16,64,128]{2,1,0:T(8,128)S(1)} %all_to_all.5.gathered, s32[32,512]{1,0:T(8,128)S(1)} %copy-done, f32[32,512]{1,0:T(8,128)S(1)} %get-tuple-element.27.weights, f32[8,512]{1,0:T(8,128)S(1)} %get-tuple-element.22.mine, ...), custom_call_target="tpu_custom_call" | custom-call | tf_op jit(solution)/shard_map/pallas_call | solution.py:509
  46.6 3.3 %collective-permute-start.2 = (f32[96,128]{1,0:T(8,128)S(1)}, f32[96,128]{1,0:T(8,128)S(1)}, u32[]{:S(2)}, u32[]{:S(2)}) collective-permute-start(f32[96,128]{1,0:T(8,128)S(1)} %get-tuple-element.30), channel_id=1, source_target_pairs={{0,1},{1,2},{2,3},{3,4},{4,5},{5,6},{6,7},{7,8},{8,9},{9,10},{10,1... | collective-permute-start | bytes 147464 | tf_op jit(solution)/shard_map/ppermute | solution.py:533
  49.9 0.0 collective-permute-start.3
  49.9 0.0 copy-start.1
  49.9 1.2 %collective-permute-done.2.below = f32[96,128]{1,0:T(8,128)S(1)} collective-permute-done((f32[96,128]{1,0:T(8,128)S(1)}, f32[96,128]{1,0:T(8,128)S(1)}, u32[]{:S(2)}, u32[]{:S(2)}) %collective-permute-start.2) | collective-permute-done | bytes 49184 | tf_op jit(solution)/shard_map/ppermute | solution.py:533
  51.1 3.5 %collective-permute-done.3.above = f32[96,128]{1,0:T(8,128)S(1)} collective-permute-done((f32[96,128]{1,0:T(8,128)S(1)}, f32[96,128]{1,0:T(8,128)S(1)}, u32[]{:S(2)}, u32[]{:S(2)}) %collective-permute-start.3) | collective-permute-done | bytes 49184 | tf_op jit(solution)/shard_map/ppermute | solution.py:534
  54.6 0.0 copy-done.1
  54.6 5.5 %shard_map.144 = (f32[96,512]{1,0:T(8,128)S(1)}, f32[96,512]{1,0:T(8,128)S(1)}, f32[96,128]{1,0:T(8,128)S(1)}, f32[96,128]{1,0:T(8,128)S(1)}) custom-call(f32[96,512]{1,0:T(8,128)S(1)} %get-tuple-element.28.coords, f32[96,512]{1,0:T(8,128)S(1)} %get-tuple-element.29.veloc, f32[96,128]{1,0:T(8,128)S(1)} %collective-permute-done.2.below, ...), custom_call_target="tpu_custom_call" | custom-call | tf_op jit(solution)/shard_map/pallas_call | solution.py:509
  60.2 0.0 collective-permute-start.4
  60.2 0.5 collective-permute-start.5
  60.7 0.1 pad_add_fusion.place
  60.8 0.6 collective-permute-done.4.below
  61.4 3.5 %collective-permute-done.5.above = f32[96,128]{1,0:T(8,128)S(1)} collective-permute-done((f32[96,128]{1,0:T(8,128)S(1)}, f32[96,128]{1,0:T(8,128)S(1)}, u32[]{:S(2)}, u32[]{:S(2)}) %collective-permute-start.5) | collective-permute-done | bytes 49184 | tf_op jit(solution)/shard_map/ppermute | solution.py:534
  65.0 0.0 copy-start.6
  65.0 6.1 %shard_map.145 = (f32[8,512]{1,0:T(8,128)S(1)}, f32[16,512]{1,0:T(8,128)S(1)}, f32[16,128]{1,0:T(8,128)S(1)}, f32[16,128]{1,0:T(8,128)S(1)}) custom-call(s32[4]{0:T(128)S(1)} %pad_add_fusion.place, f32[96,512]{1,0:T(8,128)S(1)} %get-tuple-element.32.coords, f32[96,512]{1,0:T(8,128)S(1)} %get-tuple-element.33.veloc, ...), custom_call_target="tpu_custom_call" | custom-call | tf_op jit(solution)/shard_map/pallas_call | solution.py:509
  71.1 0.0 collective-permute-start.6
  71.1 0.5 collective-permute-start.7
  71.6 0.7 collective-permute-done.6.below
  72.3 3.1 %collective-permute-done.7.above = f32[16,128]{1,0:T(8,128)S(1)} collective-permute-done((f32[16,128]{1,0:T(8,128)S(1)}, f32[16,128]{1,0:T(8,128)S(1)}, u32[]{:S(2)}, u32[]{:S(2)}) %collective-permute-start.7) | collective-permute-done | bytes 8224 | tf_op jit(solution)/shard_map/ppermute | solution.py:534
  75.4 0.0 copy-done.6
  75.4 3.7 %shard_map.146 = (f32[3,1,512]{2,1,0:T(1,128)}, f32[3,1,512]{2,1,0:T(1,128)}) custom-call(s32[4]{0:T(128)S(1)} %pad_add_fusion.place, f32[32,4]{1,0:T(8,128)S(1)} %copy-done.6, f32[8,512]{1,0:T(8,128)S(1)} %get-tuple-element.36.own, f32[16,512]{1,0:T(8,128)S(1)} %get-tuple-element.37.contracted, f32[16,128]{1,0:T(8,128)S(1)} %collective-permute-done.6.below, ...), custom_call_target="tpu_custom_call" | custom-call | tf_op jit(solution)/shard_map/pallas_call | solution.py:509
Async XLA Ops:
  0.6 0.7 copy-start.7
  0.6 25.6 %copy-start = (s32[32,512]{1,0:T(8,128)S(1)}, s32[32,512]{1,0:T(8,128)}, u32[]{:S(2)}) copy-start(s32[32,512]{1,0:T(8,128)} %neighbours.9) | copy-start | bytes 196612
  1.3 0.7 copy-start.8
  2.0 0.7 copy-start.9
  2.7 0.7 copy-start.10
  3.4 0.7 copy-start.11
  4.0 0.7 copy-start.12
  18.1 4.6 %collective-permute-start = (f32[8,128]{1,0:T(8,128)S(1)}, f32[8,128]{1,0:T(8,128)S(1)}, u32[]{:S(2)}, u32[]{:S(2)}) collective-permute-start(f32[8,128]{1,0:T(8,128)S(1)} %get-tuple-element.24), channel_id=1, source_target_pairs={{0,1},{1,2},{2,3},{3,4},{4,5},{5,6},{6,7},{7,8},{8,9},{9,10},{10,1... | collective-permute-start | bytes 12296 | tf_op jit(solution)/shard_map/ppermute | solution.py:533
  22.0 4.2 %collective-permute-start.1 = (f32[8,128]{1,0:T(8,128)S(1)}, f32[8,128]{1,0:T(8,128)S(1)}, u32[]{:S(2)}, u32[]{:S(2)}) collective-permute-start(f32[8,128]{1,0:T(8,128)S(1)} %get-tuple-element.25), channel_id=1, source_target_pairs={{0,79},{1,0},{2,1},{3,2},{4,3},{5,4},{6,5},{7,6},{8,7},{9,8},{10,9... | collective-permute-start | bytes 12296 | tf_op jit(solution)/shard_map/ppermute | solution.py:534
  27.2 16.2 %copy-start.2 = (bf16[64,480]{1,0:T(8,128)(2,1)S(1)}, bf16[64,480]{1,0:T(8,128)(2,1)}, u32[]{:S(2)}) copy-start(bf16[64,480]{1,0:T(8,128)(2,1)} %constant.71.clone.first) | copy-start | bytes 184324
  27.2 16.1 %copy-start.3 = (f32[128,8]{0,1:T(8,128)S(1)}, f32[128,8]{0,1:T(8,128)}, u32[]{:S(2)}) copy-start(f32[128,8]{0,1:T(8,128)} %param.20) | copy-start | bytes 12292
  27.2 16.1 %copy-start.4 = (f32[8,128]{1,0:T(8,128)S(1)}, f32[8,128]{1,0:T(8,128)}, u32[]{:S(2)}) copy-start(f32[8,128]{1,0:T(8,128)} %w_out.3) | copy-start | bytes 12292
  27.3 16.1 %copy-start.5 = (bf16[16,96]{1,0:T(8,128)(2,1)S(1)}, bf16[16,96]{1,0:T(8,128)(2,1)}, u32[]{:S(2)}) copy-start(bf16[16,96]{1,0:T(8,128)(2,1)} %constant.73.clone.reduce_) | copy-start | bytes 9220
  46.6 4.5 %collective-permute-start.2 = (f32[96,128]{1,0:T(8,128)S(1)}, f32[96,128]{1,0:T(8,128)S(1)}, u32[]{:S(2)}, u32[]{:S(2)}) collective-permute-start(f32[96,128]{1,0:T(8,128)S(1)} %get-tuple-element.30), channel_id=1, source_target_pairs={{0,1},{1,2},{2,3},{3,4},{4,5},{5,6},{6,7},{7,8},{8,9},{9,10},{10,1... | collective-permute-start | bytes 147464 | tf_op jit(solution)/shard_map/ppermute | solution.py:533
  49.9 4.7 %collective-permute-start.3 = (f32[96,128]{1,0:T(8,128)S(1)}, f32[96,128]{1,0:T(8,128)S(1)}, u32[]{:S(2)}, u32[]{:S(2)}) collective-permute-start(f32[96,128]{1,0:T(8,128)S(1)} %get-tuple-element.31), channel_id=1, source_target_pairs={{0,79},{1,0},{2,1},{3,2},{4,3},{5,4},{6,5},{7,6},{8,7},{9,8},{10,9... | collective-permute-start | bytes 147464 | tf_op jit(solution)/shard_map/ppermute | solution.py:534
  49.9 4.7 %copy-start.1 = (bf16[64,384]{1,0:T(8,128)(2,1)S(1)}, bf16[64,384]{1,0:T(8,128)(2,1)}, u32[]{:S(2)}) copy-start(bf16[64,384]{1,0:T(8,128)(2,1)} %constant.72.clone.later) | copy-start | bytes 147460
  60.2 1.2 %collective-permute-start.4 = (f32[96,128]{1,0:T(8,128)S(1)}, f32[96,128]{1,0:T(8,128)S(1)}, u32[]{:S(2)}, u32[]{:S(2)}) collective-permute-start(f32[96,128]{1,0:T(8,128)S(1)} %get-tuple-element.34), channel_id=1, source_target_pairs={{0,1},{1,2},{2,3},{3,4},{4,5},{5,6},{6,7},{7,8},{8,9},{9,10},{10,1... | collective-permute-start | bytes 147464 | tf_op jit(solution)/shard_map/ppermute | solution.py:533
  60.2 4.7 %collective-permute-start.5 = (f32[96,128]{1,0:T(8,128)S(1)}, f32[96,128]{1,0:T(8,128)S(1)}, u32[]{:S(2)}, u32[]{:S(2)}) collective-permute-start(f32[96,128]{1,0:T(8,128)S(1)} %get-tuple-element.35), channel_id=1, source_target_pairs={{0,79},{1,0},{2,1},{3,2},{4,3},{5,4},{6,5},{7,6},{8,7},{9,8},{10,9... | collective-permute-start | bytes 147464 | tf_op jit(solution)/shard_map/ppermute | solution.py:534
  65.0 10.5 %copy-start.6 = (f32[32,4]{1,0:T(8,128)S(1)}, f32[32,4]{1,0:T(8,128)}, u32[]{:S(2)}) copy-start(f32[32,4]{1,0:T(8,128)} %constant.74.clone.expand) | copy-start | bytes 1540
  71.1 1.2 %collective-permute-start.6 = (f32[16,128]{1,0:T(8,128)S(1)}, f32[16,128]{1,0:T(8,128)S(1)}, u32[]{:S(2)}, u32[]{:S(2)}) collective-permute-start(f32[16,128]{1,0:T(8,128)S(1)} %get-tuple-element.38), channel_id=1, source_target_pairs={{0,1},{1,2},{2,3},{3,4},{4,5},{5,6},{6,7},{7,8},{8,9},{9,10},{10,1... | collective-permute-start | bytes 24584 | tf_op jit(solution)/shard_map/ppermute | solution.py:533
  71.1 4.3 %collective-permute-start.7 = (f32[16,128]{1,0:T(8,128)S(1)}, f32[16,128]{1,0:T(8,128)S(1)}, u32[]{:S(2)}, u32[]{:S(2)}) collective-permute-start(f32[16,128]{1,0:T(8,128)S(1)} %get-tuple-element.39), channel_id=1, source_target_pairs={{0,79},{1,0},{2,1},{3,2},{4,3},{5,4},{6,5},{7,6},{8,7},{9,8},{10,9... | collective-permute-start | bytes 24584 | tf_op jit(solution)/shard_map/ppermute | solution.py:534

commit v4 on v3

--- a/solution.py
+++ b/solution.py
@@ -93,8 +93,10 @@
     kick = np.concatenate([coupling @ padded_expand, persist @ padded_expand], axis=0)
     first = six_terms(np.concatenate([step, 0.5 * outer_step * kick], axis=1))
     later = six_terms(step)
-    reduce_ = three_terms(np.concatenate([contract, np.zeros((16 - CB, BEADS))], axis=0))
-    return first, later, reduce_, (0.5 * outer_step * expand).astype(np.float32)
+    padded_contract = np.concatenate([contract, np.zeros((16 - CB, BEADS))], axis=0)
+    last = six_terms(np.concatenate([step, padded_contract @ step[:BEADS]], axis=0))
+    reduce_ = three_terms(padded_contract)
+    return first, later, last, reduce_, (0.5 * outer_step * expand).astype(np.float32)
 
 
 def lanes(source, index):
@@ -447,17 +449,16 @@
 
 
 def last_kernel(
-    place, coords, veloc, below, above, neighbours, weights, mine, ghost_rows, later, reduce_,
+    place, coords, veloc, below, above, neighbours, weights, mine, ghost_rows, last,
     own, contracted, down, up, moved, rows, *scratch,
 ):
     velocities = kicked(coords, veloc, below, above, neighbours, weights, mine, scratch)
-    moved[...] = propagated(coords[...], velocities, later)
-    small = dot3(reduce_[...], moved[0:BEADS, :])
+    moved[...] = propagated(coords[...], velocities, last)
     for x in range(3):
         at = slice(ATOMS * x, ATOMS * (x + 1))
         own[x : x + 1] = moved[pl.ds(place[1], 1), at]
         own[3 + x : 4 + x] = moved[pl.ds(BEADS + place[1], 1), at]
-        contracted[4 * x : 4 * x + 4] = small[0:4, at]
+        contracted[4 * x : 4 * x + 4] = moved[2 * BEADS : 2 * BEADS + CB, at]
     own[6:8] = mine[6:8]
     contracted[12:16] = jnp.zeros((4, ATOMS), f32)
     rows[0:12] = contracted[0:12]
@@ -538,8 +539,8 @@
 def body(
     positions, momenta, neighbours, ghost_rows, species, species_scale, mass_table, w_in, w_out
 ):
-    first, later, reduce_, expand = tables()
-    first, later, reduce_ = (jnp.asarray(t) for t in (first, later, reduce_))
+    first, later, last, reduce_, expand = tables()
+    first, later, last, reduce_ = (jnp.asarray(t) for t in (first, later, last, reduce_))
     expand = jnp.asarray(expand)
     bead = lax.axis_index("bead")
     domain = lax.axis_index("space")
@@ -562,7 +563,10 @@
             ((3, 1, ATOMS), f32), ((3, 1, ATOMS), f32), ((1, ATOMS), jnp.int32),
             pltpu.SMEM((2,), f32), pltpu.SMEM((2,), f32), pltpu.SemaphoreType.DMA((6,)),
         ],
-        (pos, mom, kinds, ghosts, species_scale, mass_table),
+        tuple(
+            pltpu.with_memory_space_constraint(v, pltpu.HBM)
+            for v in (pos, mom, kinds, ghosts, species_scale, mass_table)
+        ),
         space=pltpu.HBM,
     )
     halves = [[x * 8 + z * 4 + y for z in range(2)] for x in range(4) for y in range(4)]
@@ -602,8 +606,8 @@
     own, contracted, down, up = call(
         last_kernel,
         [(8, ATOMS), (16, ATOMS), (16, 128), (16, 128)],
-        [((2 * BEADS, 3 * ATOMS), f32), ((16, ATOMS), f32)] + big,
-        (place, coords, veloc, below, above, neighbours, weights, mine, ghosts, later, reduce_),
+        [((2 * BEADS + 16, 3 * ATOMS), f32), ((16, ATOMS), f32)] + big,
+        (place, coords, veloc, below, above, neighbours, weights, mine, ghosts, last),
         (0,),
     )
     below, above = exchange(down, up)

time: 79.4 us -> 75.5 us (0.951)
  local copies, waits for them, and re-layouts: 4.07 us -> 0.04 us
    unnamed x26 -> x16, local copies, waits for them, and re-layouts: 4.07 us -> 0.04 us
where the time goes in v4:
time: 75.5 us; the launch traced here: 75.2 us
  blocking collectives  28.8 us (38%)
  Pallas kernels  20.4 us (27%)
  waiting for transfers between devices  16.9 us (22%)
  starting transfers between devices  8.22 us (11%)
    pallas_call x7, Pallas kernels, call(): pl.pallas_call(kernel, out_shape=shapes, in_specs=specs, out_specs=[pl.Bl...  20.4 us
    all_to_all x1, blocking collectives, body(): lax.all_to_all(block, 'bead', 0, 0, axis_index_groups=groups, tiled=True)  16.1 us
    ppermute x4, waiting for transfers between devices, exchange(): above = lax.ppermute(down, RING, ring(-1))  13.7 us
    all_gather x1, blocking collectives, body(): pair = lax.all_gather(mine, 'bead', axis=0, axis_index_groups=halves)  12.7 us
    ppermute x4, starting transfers between devices, exchange(): below = lax.ppermute(up, RING, ring(1))  7.22 us
    ppermute x4, waiting for transfers between devices, exchange(): below = lax.ppermute(up, RING, ring(1))  3.23 us
  transfers between devices with their start and end apart: 8, of which 8 were waited for; matrix products, arithmetic and copies ran while one was open for 0% of the time, Pallas kernels for 0%

profile of v4, /device:TPU:97, one launch (start us, length us, event | category | flops | bytes accessed | tf_op | source)
XLA Modules:
  0.0 75.2 jit_solution(18114492439866466086)
XLA Ops:
  0.6 0.0 copy-start
  0.6 0.9 %shard_map.149 = (f32[8,512]{1,0:T(8,128)S(1)}, s32[2,128]{1,0:T(2,128)S(1)}) custom-call(f32[3,1,512]{2,1,0:T(1,128)} %bitcast.16, f32[3,1,512]{2,1,0:T(1,128)} %bitcast.17, s32[1,512]{1,0:T(1,128)} %bitcast.18, s32[2,128]{1,0:T(2,128)} %bitcast.19, f32[2]{0:T(128)} %scale.1, f32[2]{0:T(128)} %mass_table.1), custom_call_target="tpu_custom_call" | custom-call | tf_op jit(solution)/shard_map/pallas_call | solution.py:510
  1.5 12.7 %all-gather = f32[16,512]{1,0:T(8,128)S(1)} all-gather(f32[8,512]{1,0:T(8,128)S(1)} %get-tuple-element.22.mine), channel_id=2, replica_groups={{0,64},{16,80},{32,96},{48,112},{128,192},{144,208},{160,224},{176,240}..., dimensions={0}, use_global_device_ids=true | all-gather | bytes 49152 | tf_op jit(solution)/shard_map/all_gather | solution.py:573
  14.2 0.1 shard_map.150
  14.3 3.9 %collective-permute-start = (f32[8,128]{1,0:T(8,128)S(1)}, f32[8,128]{1,0:T(8,128)S(1)}, u32[]{:S(2)}, u32[]{:S(2)}) collective-permute-start(f32[8,128]{1,0:T(8,128)S(1)} %get-tuple-element.24), channel_id=1, source_target_pairs={{0,1},{1,2},{2,3},{3,4},{4,5},{5,6},{6,7},{7,8},{8,9},{9,10},{10,1... | collective-permute-start | bytes 12296 | tf_op jit(solution)/shard_map/ppermute | solution.py:534
  18.2 0.0 collective-permute-start.1
  18.2 0.8 collective-permute-done.below
  18.9 3.5 %collective-permute-done.1.above = f32[8,128]{1,0:T(8,128)S(1)} collective-permute-done((f32[8,128]{1,0:T(8,128)S(1)}, f32[8,128]{1,0:T(8,128)S(1)}, u32[]{:S(2)}, u32[]{:S(2)}) %collective-permute-start.1) | collective-permute-done | bytes 4128 | tf_op jit(solution)/shard_map/ppermute | solution.py:535
  22.4 0.0 copy-done
  22.4 1.0 %shard_map.151 = (f32[16,64,128]{2,1,0:T(8,128)S(1)}, f32[32,512]{1,0:T(8,128)S(1)}) custom-call(f32[2,8,512]{2,1,0:T(8,128)S(1)} %bitcast.13, f32[8,128]{1,0:T(8,128)S(1)} %collective-permute-done.below, f32[8,128]{1,0:T(8,128)S(1)} %collective-permute-done.1.above, s32[32,512]{1,0:T(8,128)S(1)} %copy-done), custom_call_target="tpu_custom_call" | custom-call | tf_op jit(solution)/shard_map/pallas_call | solution.py:510
  23.4 0.0 copy-start.1
  23.4 0.0 copy-start.4
  23.4 0.0 copy-start.5
  23.5 0.0 copy-start.7
  23.5 16.1 %all_to_all.5.gathered = f32[16,64,128]{2,1,0:T(8,128)S(1)} all-to-all(f32[16,64,128]{2,1,0:T(8,128)S(1)} %get-tuple-element.26), channel_id=1, replica_groups={{0,16,32,48,128,144,160,176,256,272,288,304,384,400,416,432},{64,80,96,..., dimensions={0} | all-to-all | bytes 1048576 | tf_op jit(solution)/shard_map/all_to_all | solution.py:584
  39.6 0.0 copy-done.1
  39.6 0.0 copy-done.4
  39.6 0.0 copy-done.5
  39.6 0.0 copy-done.7
  39.6 3.2 %shard_map.152 = (f32[96,512]{1,0:T(8,128)S(1)}, f32[96,512]{1,0:T(8,128)S(1)}, f32[96,128]{1,0:T(8,128)S(1)}, f32[96,128]{1,0:T(8,128)S(1)}) custom-call(f32[16,64,128]{2,1,0:T(8,128)S(1)} %all_to_all.5.gathered, s32[32,512]{1,0:T(8,128)S(1)} %copy-done, f32[32,512]{1,0:T(8,128)S(1)} %get-tuple-element.27.weights, f32[8,512]{1,0:T(8,128)S(1)} %get-tuple-element.22.mine, ...), custom_call_target="tpu_custom_call" | custom-call | tf_op jit(solution)/shard_map/pallas_call | solution.py:510
  42.8 3.3 %collective-permute-start.2 = (f32[96,128]{1,0:T(8,128)S(1)}, f32[96,128]{1,0:T(8,128)S(1)}, u32[]{:S(2)}, u32[]{:S(2)}) collective-permute-start(f32[96,128]{1,0:T(8,128)S(1)} %get-tuple-element.30), channel_id=1, source_target_pairs={{0,1},{1,2},{2,3},{3,4},{4,5},{5,6},{6,7},{7,8},{8,9},{9,10},{10,1... | collective-permute-start | bytes 147464 | tf_op jit(solution)/shard_map/ppermute | solution.py:534
  46.1 0.0 collective-permute-start.3
  46.1 0.0 copy-start.3
  46.1 1.2 %collective-permute-done.2.below = f32[96,128]{1,0:T(8,128)S(1)} collective-permute-done((f32[96,128]{1,0:T(8,128)S(1)}, f32[96,128]{1,0:T(8,128)S(1)}, u32[]{:S(2)}, u32[]{:S(2)}) %collective-permute-start.2) | collective-permute-done | bytes 49184 | tf_op jit(solution)/shard_map/ppermute | solution.py:534
  47.3 3.5 %collective-permute-done.3.above = f32[96,128]{1,0:T(8,128)S(1)} collective-permute-done((f32[96,128]{1,0:T(8,128)S(1)}, f32[96,128]{1,0:T(8,128)S(1)}, u32[]{:S(2)}, u32[]{:S(2)}) %collective-permute-start.3) | collective-permute-done | bytes 49184 | tf_op jit(solution)/shard_map/ppermute | solution.py:535
  50.8 0.0 copy-done.3
  50.8 0.0 copy-start.2
  50.8 5.5 %shard_map.153 = (f32[96,512]{1,0:T(8,128)S(1)}, f32[96,512]{1,0:T(8,128)S(1)}, f32[96,128]{1,0:T(8,128)S(1)}, f32[96,128]{1,0:T(8,128)S(1)}) custom-call(f32[96,512]{1,0:T(8,128)S(1)} %get-tuple-element.28.coords, f32[96,512]{1,0:T(8,128)S(1)} %get-tuple-element.29.veloc, f32[96,128]{1,0:T(8,128)S(1)} %collective-permute-done.2.below, ...), custom_call_target="tpu_custom_call" | custom-call | tf_op jit(solution)/shard_map/pallas_call | solution.py:510
  56.4 0.0 collective-permute-start.4
  56.4 0.5 collective-permute-start.5
  56.9 0.1 pad_add_fusion.place
  57.0 0.6 collective-permute-done.4.below
  57.6 3.5 %collective-permute-done.5.above = f32[96,128]{1,0:T(8,128)S(1)} collective-permute-done((f32[96,128]{1,0:T(8,128)S(1)}, f32[96,128]{1,0:T(8,128)S(1)}, u32[]{:S(2)}, u32[]{:S(2)}) %collective-permute-start.5) | collective-permute-done | bytes 49184 | tf_op jit(solution)/shard_map/ppermute | solution.py:535
  61.1 0.0 copy-done.2
  61.2 0.0 copy-start.6
  61.2 6.1 %shard_map.154 = (f32[8,512]{1,0:T(8,128)S(1)}, f32[16,512]{1,0:T(8,128)S(1)}, f32[16,128]{1,0:T(8,128)S(1)}, f32[16,128]{1,0:T(8,128)S(1)}) custom-call(s32[4]{0:T(128)S(1)} %pad_add_fusion.place, f32[96,512]{1,0:T(8,128)S(1)} %get-tuple-element.32.coords, f32[96,512]{1,0:T(8,128)S(1)} %get-tuple-element.33.veloc, ...), custom_call_target="tpu_custom_call" | custom-call | tf_op jit(solution)/shard_map/pallas_call | solution.py:510
  67.2 0.0 collective-permute-start.6
  67.2 0.5 collective-permute-start.7
  67.7 0.7 collective-permute-done.6.below
  68.4 3.1 %collective-permute-done.7.above = f32[16,128]{1,0:T(8,128)S(1)} collective-permute-done((f32[16,128]{1,0:T(8,128)S(1)}, f32[16,128]{1,0:T(8,128)S(1)}, u32[]{:S(2)}, u32[]{:S(2)}) %collective-permute-start.7) | collective-permute-done | bytes 8224 | tf_op jit(solution)/shard_map/ppermute | solution.py:535
  71.5 0.0 copy-done.6
  71.5 3.7 %shard_map.155 = (f32[3,1,512]{2,1,0:T(1,128)}, f32[3,1,512]{2,1,0:T(1,128)}) custom-call(s32[4]{0:T(128)S(1)} %pad_add_fusion.place, f32[32,4]{1,0:T(8,128)S(1)} %copy-done.6, f32[8,512]{1,0:T(8,128)S(1)} %get-tuple-element.36.own, f32[16,512]{1,0:T(8,128)S(1)} %get-tuple-element.37.contracted, f32[16,128]{1,0:T(8,128)S(1)} %collective-permute-done.6.below, ...), custom_call_target="tpu_custom_call" | custom-call | tf_op jit(solution)/shard_map/pallas_call | solution.py:510
Async XLA Ops:
  0.6 21.8 %copy-start = (s32[32,512]{1,0:T(8,128)S(1)}, s32[32,512]{1,0:T(8,128)}, u32[]{:S(2)}) copy-start(s32[32,512]{1,0:T(8,128)} %neighbours.9) | copy-start | bytes 196612
  14.3 4.6 %collective-permute-start = (f32[8,128]{1,0:T(8,128)S(1)}, f32[8,128]{1,0:T(8,128)S(1)}, u32[]{:S(2)}, u32[]{:S(2)}) collective-permute-start(f32[8,128]{1,0:T(8,128)S(1)} %get-tuple-element.24), channel_id=1, source_target_pairs={{0,1},{1,2},{2,3},{3,4},{4,5},{5,6},{6,7},{7,8},{8,9},{9,10},{10,1... | collective-permute-start | bytes 12296 | tf_op jit(solution)/shard_map/ppermute | solution.py:534
  18.2 4.2 %collective-permute-start.1 = (f32[8,128]{1,0:T(8,128)S(1)}, f32[8,128]{1,0:T(8,128)S(1)}, u32[]{:S(2)}, u32[]{:S(2)}) collective-permute-start(f32[8,128]{1,0:T(8,128)S(1)} %get-tuple-element.25), channel_id=1, source_target_pairs={{0,79},{1,0},{2,1},{3,2},{4,3},{5,4},{6,5},{7,6},{8,7},{9,8},{10,9... | collective-permute-start | bytes 12296 | tf_op jit(solution)/shard_map/ppermute | solution.py:535
  23.4 16.2 %copy-start.1 = (bf16[64,480]{1,0:T(8,128)(2,1)S(1)}, bf16[64,480]{1,0:T(8,128)(2,1)}, u32[]{:S(2)}) copy-start(bf16[64,480]{1,0:T(8,128)(2,1)} %constant.73.clone.first) | copy-start | bytes 184324
  23.4 16.1 %copy-start.4 = (f32[128,8]{0,1:T(8,128)S(1)}, f32[128,8]{0,1:T(8,128)}, u32[]{:S(2)}) copy-start(f32[128,8]{0,1:T(8,128)} %param.21) | copy-start | bytes 12292
  23.4 16.1 %copy-start.5 = (f32[8,128]{1,0:T(8,128)S(1)}, f32[8,128]{1,0:T(8,128)}, u32[]{:S(2)}) copy-start(f32[8,128]{1,0:T(8,128)} %w_out.3) | copy-start | bytes 12292
  23.5 16.1 %copy-start.7 = (bf16[16,96]{1,0:T(8,128)(2,1)S(1)}, bf16[16,96]{1,0:T(8,128)(2,1)}, u32[]{:S(2)}) copy-start(bf16[16,96]{1,0:T(8,128)(2,1)} %constant.76.clone.reduce_) | copy-start | bytes 9220
  42.8 4.5 %collective-permute-start.2 = (f32[96,128]{1,0:T(8,128)S(1)}, f32[96,128]{1,0:T(8,128)S(1)}, u32[]{:S(2)}, u32[]{:S(2)}) collective-permute-start(f32[96,128]{1,0:T(8,128)S(1)} %get-tuple-element.30), channel_id=1, source_target_pairs={{0,1},{1,2},{2,3},{3,4},{4,5},{5,6},{6,7},{7,8},{8,9},{9,10},{10,1... | collective-permute-start | bytes 147464 | tf_op jit(solution)/shard_map/ppermute | solution.py:534
  46.1 4.7 %collective-permute-start.3 = (f32[96,128]{1,0:T(8,128)S(1)}, f32[96,128]{1,0:T(8,128)S(1)}, u32[]{:S(2)}, u32[]{:S(2)}) collective-permute-start(f32[96,128]{1,0:T(8,128)S(1)} %get-tuple-element.31), channel_id=1, source_target_pairs={{0,79},{1,0},{2,1},{3,2},{4,3},{5,4},{6,5},{7,6},{8,7},{9,8},{10,9... | collective-permute-start | bytes 147464 | tf_op jit(solution)/shard_map/ppermute | solution.py:535
  46.1 4.7 %copy-start.3 = (bf16[64,384]{1,0:T(8,128)(2,1)S(1)}, bf16[64,384]{1,0:T(8,128)(2,1)}, u32[]{:S(2)}) copy-start(bf16[64,384]{1,0:T(8,128)(2,1)} %constant.74.clone.later) | copy-start | bytes 147460
  50.8 10.3 %copy-start.2 = (bf16[80,384]{1,0:T(8,128)(2,1)S(1)}, bf16[80,384]{1,0:T(8,128)(2,1)}, u32[]{:S(2)}) copy-start(bf16[80,384]{1,0:T(8,128)(2,1)} %constant.75.clone.last) | copy-start | bytes 184324
  56.4 1.2 %collective-permute-start.4 = (f32[96,128]{1,0:T(8,128)S(1)}, f32[96,128]{1,0:T(8,128)S(1)}, u32[]{:S(2)}, u32[]{:S(2)}) collective-permute-start(f32[96,128]{1,0:T(8,128)S(1)} %get-tuple-element.34), channel_id=1, source_target_pairs={{0,1},{1,2},{2,3},{3,4},{4,5},{5,6},{6,7},{7,8},{8,9},{9,10},{10,1... | collective-permute-start | bytes 147464 | tf_op jit(solution)/shard_map/ppermute | solution.py:534
  56.4 4.7 %collective-permute-start.5 = (f32[96,128]{1,0:T(8,128)S(1)}, f32[96,128]{1,0:T(8,128)S(1)}, u32[]{:S(2)}, u32[]{:S(2)}) collective-permute-start(f32[96,128]{1,0:T(8,128)S(1)} %get-tuple-element.35), channel_id=1, source_target_pairs={{0,79},{1,0},{2,1},{3,2},{4,3},{5,4},{6,5},{7,6},{8,7},{9,8},{10,9... | collective-permute-start | bytes 147464 | tf_op jit(solution)/shard_map/ppermute | solution.py:535
  61.2 10.4 %copy-start.6 = (f32[32,4]{1,0:T(8,128)S(1)}, f32[32,4]{1,0:T(8,128)}, u32[]{:S(2)}) copy-start(f32[32,4]{1,0:T(8,128)} %constant.77.clone.expand) | copy-start | bytes 1540
  67.2 1.2 %collective-permute-start.6 = (f32[16,128]{1,0:T(8,128)S(1)}, f32[16,128]{1,0:T(8,128)S(1)}, u32[]{:S(2)}, u32[]{:S(2)}) collective-permute-start(f32[16,128]{1,0:T(8,128)S(1)} %get-tuple-element.38), channel_id=1, source_target_pairs={{0,1},{1,2},{2,3},{3,4},{4,5},{5,6},{6,7},{7,8},{8,9},{9,10},{10,1... | collective-permute-start | bytes 24584 | tf_op jit(solution)/shard_map/ppermute | solution.py:534
  67.2 4.3 %collective-permute-start.7 = (f32[16,128]{1,0:T(8,128)S(1)}, f32[16,128]{1,0:T(8,128)S(1)}, u32[]{:S(2)}, u32[]{:S(2)}) collective-permute-start(f32[16,128]{1,0:T(8,128)S(1)} %get-tuple-element.39), channel_id=1, source_target_pairs={{0,79},{1,0},{2,1},{3,2},{4,3},{5,4},{6,5},{7,6},{8,7},{9,8},{10,9... | collective-permute-start | bytes 24584 | tf_op jit(solution)/shard_map/ppermute | solution.py:535

commit v5 on v4

--- a/solution.py
+++ b/solution.py
@@ -153,12 +153,27 @@
     return out
 
 
-def cheap_by_lanes(table, neighbours, weights, a):
-    rows = [[row8(table(x, k)) for k in range(WINDOW)] for x in range(3)]
+def own_lookup(row, neighbours, g, a):
+    index = neighbours[8 * g : 8 * g + 8, 128 * a : 128 * a + 128]
+    lane, part = index & 127, index >> 7
+    out = lanes(row8(row(0)), lane)
+    for k in range(1, CHUNKS):
+        out = jnp.where(part == k + 1, lanes(row8(row(k)), lane), out)
+    return out
+
+
+def with_ghosts(early, low, high, index):
+    lane, part = index & 127, index >> 7
+    out = jnp.where(part == 0, lanes(row8(low), lane), early)
+    return jnp.where(part == WINDOW - 1, lanes(row8(high), lane), out)
+
+
+def cheap_by_lanes(looked, centre, neighbours, weights, a):
+    centre = [row8(row) for row in centre]
     total = [jnp.zeros((8, 128), f32) for _ in range(3)]
     for g in range(SLOTS // 8):
-        lane, masks, _ = tile_index(neighbours, g, a)
-        offset = [looked_up(rows[x], lane, masks) - rows[x][1 + a] for x in range(3)]
+        index = neighbours[8 * g : 8 * g + 8, 128 * a : 128 * a + 128]
+        offset = [looked(x, g, index) - centre[x] for x in range(3)]
         squared = offset[0] * offset[0] + offset[1] * offset[1] + offset[2] * offset[2]
         w = weights[8 * g : 8 * g + 8, 128 * a : 128 * a + 128] * jnp.exp(-squared)
         for x in range(3):
@@ -176,7 +191,7 @@
     return out
 
 
-def learned_by_lanes(table, neighbours, weights, w_in, w_out, offsets, messages, radials, store):
+def learned_by_lanes(looked, centre, neighbours, weights, w_in, w_out, offsets, messages, radials, store):
     high = w_in[...].astype(bf16).astype(f32)
     first = jnp.concatenate([high, w_in[...] - high, high, jnp.zeros_like(high)], axis=0).astype(bf16)
     high = w_out[...].astype(bf16).astype(f32)
@@ -185,11 +200,10 @@
 
     def message(c):
         for a in range(CHUNKS):
-            rows = [[row8(table(c, x, k)) for k in range(WINDOW)] for x in range(3)]
+            middle = [row8(centre(c, x, a)) for x in range(3)]
             total = [jnp.zeros((8, 128), f32) for _ in range(NRBF)]
             for g in range(SLOTS // 8):
-                lane, masks, _ = tile_index(neighbours, g, a)
-                offset = [looked_up(rows[x], lane, masks) - rows[x][1 + a] for x in range(3)]
+                offset = [looked(c, x, a, g) - middle[x] for x in range(3)]
                 squared = offset[0] * offset[0] + offset[1] * offset[1] + offset[2] * offset[2]
                 for x in range(3):
                     offsets[c, a, g, x] = offset[x]
@@ -357,11 +371,18 @@
     up[...] = ghosts_of(chunk, ghost_rows[1:2])
 
 
-def pack_kernel(pair, below, above, neighbours, out, weights, block, charges):
-    charges[0:1] = below[6:7]
-    for k in range(CHUNKS):
-        charges[1 + k : 2 + k] = pair[0, 6:7, 128 * k : 128 * k + 128]
-    charges[5:6] = above[6:7]
+def early_pack_kernel(pair, neighbours, early):
+    for a in range(CHUNKS):
+        for g in range(SLOTS // 8):
+            for k in range(2):
+                for x in range(3):
+                    early[3 * k + x, a, g] = own_lookup(
+                        lambda i: pair[k, x : x + 1, 128 * i : 128 * i + 128], neighbours, g, a
+                    )
+            early[6, a, g] = own_lookup(lambda i: pair[0, 6:7, 128 * i : 128 * i + 128], neighbours, g, a)
+
+
+def pack_kernel(pair, early, below, above, neighbours, out, weights, block):
     for k in range(2):
         base = 32 * k
         for x in range(3):
@@ -373,19 +394,21 @@
         block[base + 30 : base + 32] = jnp.zeros((2, 128), f32)
     for a in range(CHUNKS):
         itself = 128 + 128 * a + lax.broadcasted_iota(jnp.int32, (8, 128), 1)
-        rows = [row8(charges[k : k + 1]) for k in range(WINDOW)]
         for g in range(SLOTS // 8):
-            lane, masks, index = tile_index(neighbours, g, a)
-            q = looked_up(rows, lane, masks)
+            index = neighbours[8 * g : 8 * g + 8, 128 * a : 128 * a + 128]
+            q = with_ghosts(early[6, a, g], below[6:7], above[6:7], index)
             weights[8 * g : 8 * g + 8, 128 * a : 128 * a + 128] = jnp.where(index == itself, 0.0, q)
     for a in range(CHUNKS):
         at = slice(128 * a, 128 * a + 128)
         gain = pair[0, 6:7, at] / pair[0, 7:8, at] * (0.5 * inner_step)
         for k in range(2):
             base = 32 * k
-            force = cheap_by_lanes(
-                lambda x, w: block[base + 6 * x + w : base + 6 * x + w + 1], neighbours, weights, a
-            )
+
+            def looked(x, g, index):
+                i = 3 * k + x
+                return with_ghosts(early[i, a, g], below[i : i + 1], above[i : i + 1], index)
+
+            force = cheap_by_lanes(looked, [pair[k, x : x + 1, at] for x in range(3)], neighbours, weights, a)
             for x in range(3):
                 row = base + 18 + 4 * x + a
                 block[row : row + 1] = pair[k, 3 + x : 4 + x, at] + gain * force[x]
@@ -413,9 +436,13 @@
     def store(c, x, a, value):
         slow[x, c : c + 1, 128 * a : 128 * a + 128] = value
 
+    def looked(c, x, a, g):
+        rows = [row8(contracted[x, c : c + 1, 128 * k : 128 * k + 128]) for k in range(WINDOW)]
+        lane, masks, _ = tile_index(neighbours, g, a)
+        return looked_up(rows, lane, masks)
+
     learned_by_lanes(
-        lambda c, x, k: contracted[x, c : c + 1, 128 * k : 128 * k + 128],
-        neighbours, weights, w_in, w_out, offsets, messages, radials, store,
+        looked, lambda c, x, a: contracted[x, c : c + 1, 128 + 128 * a : 256 + 128 * a], neighbours, weights, w_in, w_out, offsets, messages, radials, store,
     )
     moved = propagated(
         window[:, 128:640], start[...], first, [slow[x] * inverse for x in range(3)]
@@ -461,41 +488,50 @@
         contracted[4 * x : 4 * x + 4] = moved[2 * BEADS : 2 * BEADS + CB, at]
     own[6:8] = mine[6:8]
     contracted[12:16] = jnp.zeros((4, ATOMS), f32)
-    rows[0:12] = contracted[0:12]
-    for which, out in ((2, down), (3, up)):
+    for which, out in ((0, down), (1, up)):
+        rows[which, 0:4] = contracted[8:12]
         for x in range(3):
-            rows[12 + x : 13 + x] = moved[pl.ds(place[which], 1), ATOMS * x : ATOMS * (x + 1)]
-        rows[15:16] = contracted[12:13]
-        index = ghost_rows[which - 2 : which - 1]
-        for i in range(2):
-            out[8 * i : 8 * i + 8] = ghosts_of(
-                lambda k: rows[8 * i : 8 * i + 8, 128 * k : 128 * k + 128], index
-            )
+            rows[which, 4 + x : 5 + x] = moved[pl.ds(place[2 + which], 1), ATOMS * x : ATOMS * (x + 1)]
+        rows[which, 7:8] = contracted[12:13]
+        index = ghost_rows[which : which + 1]
+        out[0:8] = ghosts_of(lambda k: contracted[0:8, 128 * k : 128 * k + 128], index)
+        out[8:16] = ghosts_of(lambda k: rows[which, :, 128 * k : 128 * k + 128], index)
+
+
+def early_end_kernel(own, contracted, neighbours, early):
+    for a in range(CHUNKS):
+        for g in range(SLOTS // 8):
+            for i in range(15):
+                source, row = (contracted, i) if i < 12 else (own, i - 12)
+                early[i, a, g] = own_lookup(
+                    lambda k: source[row : row + 1, 128 * k : 128 * k + 128], neighbours, g, a
+                )
 
 
 def end_kernel(
-    place, expand, own, contracted, below, above, neighbours, weights, w_in, w_out,
+    place, expand, own, contracted, early, below, above, neighbours, weights, w_in, w_out,
     new_pos, new_mom,
-    window, offsets, messages, radials, slow,
+    offsets, messages, radials, slow,
 ):
     charge, mass = own[6:7], own[7:8]
-    window[0:16, 0:128] = below[...]
-    window[0:16, 640:768] = above[...]
-    window[0:12, 128:640] = contracted[0:12]
-    window[12:15, 128:640] = own[0:3]
 
     def store(c, x, a, value):
         slow[c, x, a : a + 1] = value
 
+    def looked_at(i, a, g):
+        index = neighbours[8 * g : 8 * g + 8, 128 * a : 128 * a + 128]
+        return with_ghosts(early[i, a, g], below[i : i + 1], above[i : i + 1], index)
+
     learned_by_lanes(
-        lambda c, x, k: window[4 * x + c : 4 * x + c + 1, 128 * k : 128 * k + 128],
+        lambda c, x, a, g: looked_at(4 * x + c, a, g),
+        lambda c, x, a: contracted[4 * x + c : 4 * x + c + 1, 128 * a : 128 * a + 128],
         neighbours, weights, w_in, w_out, offsets, messages, radials, store,
     )
     for a in range(CHUNKS):
+        at = slice(128 * a, 128 * a + 128)
         force = cheap_by_lanes(
-            lambda x, k: window[12 + x : 13 + x, 128 * k : 128 * k + 128], neighbours, weights, a
+            lambda x, g, index: looked_at(12 + x, a, g), [own[x : x + 1, at] for x in range(3)], neighbours, weights, a
         )
-        at = slice(128 * a, 128 * a + 128)
         for x in range(3):
             value = mass[:, at] * own[3 + x : 4 + x, at] + (0.5 * inner_step) * charge[:, at] * force[x]
             for c in range(CB):
@@ -504,7 +540,7 @@
             new_pos[x, :, at] = own[x : x + 1, at]
 
 
-def call(kernel, outs, scratch, args, scalars=(), space=pltpu.VMEM):
+def call(kernel, outs, scratch, args, scalars=(), space=pltpu.VMEM, cost=None):
     specs = [pl.BlockSpec(memory_space=pltpu.SMEM if i in scalars else space) for i in range(len(args))]
     shapes = [s if isinstance(s, jax.ShapeDtypeStruct) else jax.ShapeDtypeStruct(s, f32) for s in outs]
     return pl.pallas_call(
@@ -514,6 +550,7 @@
         out_specs=[pl.BlockSpec(memory_space=pltpu.VMEM)] * len(outs),
         scratch_shapes=[pltpu.VMEM(*s) if isinstance(s, tuple) else s for s in scratch],
         compiler_params=pltpu.CompilerParams(vmem_limit_bytes=VMEM_LIMIT),
+        cost_estimate=cost,
     )(*args)
 
 
@@ -569,16 +606,19 @@
         ),
         space=pltpu.HBM,
     )
+    cost = pl.CostEstimate(flops=10**9, bytes_accessed=10**6, transcendentals=0)
     halves = [[x * 8 + z * 4 + y for z in range(2)] for x in range(4) for y in range(4)]
     pair = lax.all_gather(mine, "bead", axis=0, axis_index_groups=halves)
     down, up = call(send_kernel, [(8, 128)] * 2, [((8, ATOMS), f32)], (pair, ghosts), ())
     below, above = exchange(down, up)
+    (early,) = call(
+        early_pack_kernel, [(7, CHUNKS, SLOTS // 8, 8, 128)], [], (pair, neighbours), cost=cost
+    )
     block, weights = call(
         pack_kernel,
         [(16, 64, 128), (SLOTS, ATOMS)],
-        [((64, 128), f32), ((8, 128), f32)],
-        (pair, below, above, neighbours),
-        (),
+        [((64, 128), f32)],
+        (pair, early, below, above, neighbours),
     )
     groups = [[x * 8 + z * 4 + y for x in range(4) for y in range(4)] for z in range(2)]
     gathered = lax.all_to_all(block, "bead", 0, 0, axis_index_groups=groups, tiled=True)
@@ -606,16 +646,19 @@
     own, contracted, down, up = call(
         last_kernel,
         [(8, ATOMS), (16, ATOMS), (16, 128), (16, 128)],
-        [((2 * BEADS + 16, 3 * ATOMS), f32), ((16, ATOMS), f32)] + big,
+        [((2 * BEADS + 16, 3 * ATOMS), f32), ((2, 8, ATOMS), f32)] + big,
         (place, coords, veloc, below, above, neighbours, weights, mine, ghosts, last),
         (0,),
     )
     below, above = exchange(down, up)
+    (early,) = call(
+        early_end_kernel, [(15, CHUNKS, SLOTS // 8, 8, 128)], [], (own, contracted, neighbours), cost=cost
+    )
     new_pos, new_mom = call(
         end_kernel,
         [(3, 1, ATOMS), (3, 1, ATOMS)],
-        [((16, 768), f32), offsets, network, network, ((CB, 3, CHUNKS, 128), f32)],
-        (place, expand, own, contracted, below, above, neighbours, weights, w_in, w_out),
+        [offsets, network, network, ((CB, 3, CHUNKS, 128), f32)],
+        (place, expand, own, contracted, early, below, above, neighbours, weights, w_in, w_out),
         (0, 1),
     )
     return new_pos.transpose(1, 0, 2), new_mom.transpose(1, 0, 2)

time: 75.5 us -> 74.6 us (0.988)
  waiting for transfers between devices: 16.9 us -> 14.2 us
  Pallas kernels: 20.4 us -> 22.3 us
    pallas_call x7 -> x9, Pallas kernels: 20.4 us -> 22.3 us  [call(): pl.pallas_call(kernel, out_shape=shapes, in_specs=specs, out_specs=[pl.Bl...]
    ppermute x4, waiting for transfers between devices: 3.23 us -> 1.82 us  [exchange(): below = lax.ppermute(up, RING, ring(1))]
    ppermute x4, waiting for transfers between devices: 13.7 us -> 12.3 us  [exchange(): above = lax.ppermute(down, RING, ring(-1))]
  transfers between devices with their start and end apart: 8 -> 8, of which waited for: 8 -> 6; matrix products, arithmetic and copies ran while one was open for 0% -> 0% of each run, Pallas kernels for 0% -> 4%
where the time goes in v5:
time: 74.6 us; the launch traced here: 74.3 us
  blocking collectives  28.8 us (39%)
  Pallas kernels  22.3 us (30%)
  waiting for transfers between devices  14.2 us (19%)
  starting transfers between devices  8.22 us (11%)
  between operations  0.76 us (1%)
    pallas_call x9, Pallas kernels, call(): pl.pallas_call(kernel, out_shape=shapes, in_specs=specs, out_specs=[pl.Bl...  22.3 us
    all_to_all x1, blocking collectives, body(): lax.all_to_all(block, 'bead', 0, 0, axis_index_groups=groups, tiled=True)  16.1 us
    all_gather x1, blocking collectives, body(): pair = lax.all_gather(mine, 'bead', axis=0, axis_index_groups=halves)  12.7 us
    ppermute x4, waiting for transfers between devices, exchange(): above = lax.ppermute(down, RING, ring(-1))  12.3 us
    ppermute x4, starting transfers between devices, exchange(): below = lax.ppermute(up, RING, ring(1))  7.22 us
    ppermute x4, waiting for transfers between devices, exchange(): below = lax.ppermute(up, RING, ring(1))  1.82 us
  transfers between devices with their start and end apart: 8, of which 6 were waited for; matrix products, arithmetic and copies ran while one was open for 0% of the time, Pallas kernels for 4%

profile of v5, /device:TPU:97, one launch (start us, length us, event | category | flops | bytes accessed | tf_op | source)
XLA Modules:
  0.0 74.3 jit_solution(2941105809085069966)
XLA Ops:
  0.6 0.0 copy-start
  0.6 0.9 %shard_map.149 = (f32[8,512]{1,0:T(8,128)S(1)}, s32[2,128]{1,0:T(2,128)S(1)}) custom-call(f32[3,1,512]{2,1,0:T(1,128)} %bitcast.17, f32[3,1,512]{2,1,0:T(1,128)} %bitcast.18, s32[1,512]{1,0:T(1,128)} %bitcast.19, s32[2,128]{1,0:T(2,128)} %bitcast.20, f32[2]{0:T(128)} %scale.1, f32[2]{0:T(128)} %mass_table.1), custom_call_target="tpu_custom_call" | custom-call | tf_op jit(solution)/shard_map/pallas_call | solution.py:546
  1.5 12.7 %all-gather = f32[16,512]{1,0:T(8,128)S(1)} all-gather(f32[8,512]{1,0:T(8,128)S(1)} %get-tuple-element.22.mine), channel_id=2, replica_groups={{0,64},{16,80},{32,96},{48,112},{128,192},{144,208},{160,224},{176,240}..., dimensions={0}, use_global_device_ids=true | all-gather | bytes 49152 | tf_op jit(solution)/shard_map/all_gather | solution.py:611
  14.2 0.1 shard_map.151
  14.3 3.9 %collective-permute-start = (f32[8,128]{1,0:T(8,128)S(1)}, f32[8,128]{1,0:T(8,128)S(1)}, u32[]{:S(2)}, u32[]{:S(2)}) collective-permute-start(f32[8,128]{1,0:T(8,128)S(1)} %get-tuple-element.24), channel_id=1, source_target_pairs={{0,1},{1,2},{2,3},{3,4},{4,5},{5,6},{6,7},{7,8},{8,9},{9,10},{10,1... | collective-permute-start | bytes 12296 | tf_op jit(solution)/shard_map/ppermute | solution.py:571
  18.2 0.0 collective-permute-start.1
  18.2 0.0 copy-done
  18.2 0.9 %shard_map.150.early = f32[7,4,4,8,128]{4,3,2,1,0:T(8,128)S(1)} custom-call(f32[2,8,512]{2,1,0:T(8,128)S(1)} %bitcast.13, s32[32,512]{1,0:T(8,128)S(1)} %copy-done), custom_call_target="tpu_custom_call" | custom-call | flops 1000000000 | bytes 1000000 | tf_op jit(solution)/shard_map/pallas_call | solution.py:546
  19.1 0.0 collective-permute-done.below
  19.1 3.3 %collective-permute-done.1.above = f32[8,128]{1,0:T(8,128)S(1)} collective-permute-done((f32[8,128]{1,0:T(8,128)S(1)}, f32[8,128]{1,0:T(8,128)S(1)}, u32[]{:S(2)}, u32[]{:S(2)}) %collective-permute-start.1) | collective-permute-done | bytes 4128 | tf_op jit(solution)/shard_map/ppermute | solution.py:572
  22.4 0.5 shard_map.152
  22.9 0.0 copy-start.1
  22.9 0.0 copy-start.5
  23.0 0.0 copy-start.6
  23.0 0.0 copy-start.7
  23.0 16.1 %all_to_all.5.gathered = f32[16,64,128]{2,1,0:T(8,128)S(1)} all-to-all(f32[16,64,128]{2,1,0:T(8,128)S(1)} %get-tuple-element.26), channel_id=1, replica_groups={{0,16,32,48,128,144,160,176,256,272,288,304,384,400,416,432},{64,80,96,..., dimensions={0} | all-to-all | bytes 1048576 | tf_op jit(solution)/shard_map/all_to_all | solution.py:624
  39.1 0.0 copy-done.1
  39.1 0.0 copy-done.5
  39.1 0.0 copy-done.6
  39.1 0.0 copy-done.7
  39.1 3.2 %shard_map.153 = (f32[96,512]{1,0:T(8,128)S(1)}, f32[96,512]{1,0:T(8,128)S(1)}, f32[96,128]{1,0:T(8,128)S(1)}, f32[96,128]{1,0:T(8,128)S(1)}) custom-call(f32[16,64,128]{2,1,0:T(8,128)S(1)} %all_to_all.5.gathered, s32[32,512]{1,0:T(8,128)S(1)} %copy-done, f32[32,512]{1,0:T(8,128)S(1)} %get-tuple-element.27.weights, f32[8,512]{1,0:T(8,128)S(1)} %get-tuple-element.22.mine, ...), custom_call_target="tpu_custom_call" | custom-call | tf_op jit(solution)/shard_map/pallas_call | solution.py:546
  42.3 3.3 %collective-permute-start.2 = (f32[96,128]{1,0:T(8,128)S(1)}, f32[96,128]{1,0:T(8,128)S(1)}, u32[]{:S(2)}, u32[]{:S(2)}) collective-permute-start(f32[96,128]{1,0:T(8,128)S(1)} %get-tuple-element.30), channel_id=1, source_target_pairs={{0,1},{1,2},{2,3},{3,4},{4,5},{5,6},{6,7},{7,8},{8,9},{9,10},{10,1... | collective-permute-start | bytes 147464 | tf_op jit(solution)/shard_map/ppermute | solution.py:571
  45.6 0.0 collective-permute-start.3
  45.6 0.0 copy-start.3
  45.6 1.2 %collective-permute-done.2.below = f32[96,128]{1,0:T(8,128)S(1)} collective-permute-done((f32[96,128]{1,0:T(8,128)S(1)}, f32[96,128]{1,0:T(8,128)S(1)}, u32[]{:S(2)}, u32[]{:S(2)}) %collective-permute-start.2) | collective-permute-done | bytes 49184 | tf_op jit(solution)/shard_map/ppermute | solution.py:571
  46.8 3.5 %collective-permute-done.3.above = f32[96,128]{1,0:T(8,128)S(1)} collective-permute-done((f32[96,128]{1,0:T(8,128)S(1)}, f32[96,128]{1,0:T(8,128)S(1)}, u32[]{:S(2)}, u32[]{:S(2)}) %collective-permute-start.3) | collective-permute-done | bytes 49184 | tf_op jit(solution)/shard_map/ppermute | solution.py:572
  50.4 0.0 copy-done.3
  50.4 0.0 copy-start.2
  50.4 5.5 %shard_map.154 = (f32[96,512]{1,0:T(8,128)S(1)}, f32[96,512]{1,0:T(8,128)S(1)}, f32[96,128]{1,0:T(8,128)S(1)}, f32[96,128]{1,0:T(8,128)S(1)}) custom-call(f32[96,512]{1,0:T(8,128)S(1)} %get-tuple-element.28.coords, f32[96,512]{1,0:T(8,128)S(1)} %get-tuple-element.29.veloc, f32[96,128]{1,0:T(8,128)S(1)} %collective-permute-done.2.below, ...), custom_call_target="tpu_custom_call" | custom-call | tf_op jit(solution)/shard_map/pallas_call | solution.py:546
  55.9 0.0 collective-permute-start.4
  55.9 0.5 collective-permute-start.5
  56.4 0.1 pad_add_fusion.place
  56.5 0.6 collective-permute-done.4.below
  57.1 3.5 %collective-permute-done.5.above = f32[96,128]{1,0:T(8,128)S(1)} collective-permute-done((f32[96,128]{1,0:T(8,128)S(1)}, f32[96,128]{1,0:T(8,128)S(1)}, u32[]{:S(2)}, u32[]{:S(2)}) %collective-permute-start.5) | collective-permute-done | bytes 49184 | tf_op jit(solution)/shard_map/ppermute | solution.py:572
  60.7 0.0 copy-done.2
  60.7 6.0 %shard_map.155 = (f32[8,512]{1,0:T(8,128)S(1)}, f32[16,512]{1,0:T(8,128)S(1)}, f32[16,128]{1,0:T(8,128)S(1)}, f32[16,128]{1,0:T(8,128)S(1)}) custom-call(s32[4]{0:T(128)S(1)} %pad_add_fusion.place, f32[96,512]{1,0:T(8,128)S(1)} %get-tuple-element.32.coords, f32[96,512]{1,0:T(8,128)S(1)} %get-tuple-element.33.veloc, ...), custom_call_target="tpu_custom_call" | custom-call | tf_op jit(solution)/shard_map/pallas_call | solution.py:546
  66.7 0.0 collective-permute-start.6
  66.7 0.5 collective-permute-start.7
  67.2 0.0 copy-start.4
  67.2 1.8 %shard_map.156.early = f32[15,4,4,8,128]{4,3,2,1,0:T(8,128)S(1)} custom-call(f32[8,512]{1,0:T(8,128)S(1)} %get-tuple-element.36.own, f32[16,512]{1,0:T(8,128)S(1)} %get-tuple-element.37.contracted, s32[32,512]{1,0:T(8,128)S(1)} %copy-done), custom_call_target="tpu_custom_call" | custom-call | flops 1000000000 | bytes 1000000 | tf_op jit(solution)/shard_map/pallas_call | solution.py:546
  69.1 0.0 collective-permute-done.6.below
  69.1 1.9 %collective-permute-done.7.above = f32[16,128]{1,0:T(8,128)S(1)} collective-permute-done((f32[16,128]{1,0:T(8,128)S(1)}, f32[16,128]{1,0:T(8,128)S(1)}, u32[]{:S(2)}, u32[]{:S(2)}) %collective-permute-start.7) | collective-permute-done | bytes 8224 | tf_op jit(solution)/shard_map/ppermute | solution.py:572
  71.0 0.0 copy-done.4
  71.0 3.3 %shard_map.157 = (f32[3,1,512]{2,1,0:T(1,128)}, f32[3,1,512]{2,1,0:T(1,128)}) custom-call(s32[4]{0:T(128)S(1)} %pad_add_fusion.place, f32[32,4]{1,0:T(8,128)S(1)} %copy-done.4, f32[8,512]{1,0:T(8,128)S(1)} %get-tuple-element.36.own, f32[16,512]{1,0:T(8,128)S(1)} %get-tuple-element.37.contracted, f32[15,4,4,8,128]{4,3,2,1,0:T(8,128)S(1)} %shard_map.156.early, ...), custom_call_target="tpu_custom_call" | custom-call | tf_op jit(solution)/shard_map/pallas_call | solution.py:546
Async XLA Ops:
  0.6 17.5 %copy-start = (s32[32,512]{1,0:T(8,128)S(1)}, s32[32,512]{1,0:T(8,128)}, u32[]{:S(2)}) copy-start(s32[32,512]{1,0:T(8,128)} %neighbours.13) | copy-start | bytes 196612
  14.3 4.8 %collective-permute-start = (f32[8,128]{1,0:T(8,128)S(1)}, f32[8,128]{1,0:T(8,128)S(1)}, u32[]{:S(2)}, u32[]{:S(2)}) collective-permute-start(f32[8,128]{1,0:T(8,128)S(1)} %get-tuple-element.24), channel_id=1, source_target_pairs={{0,1},{1,2},{2,3},{3,4},{4,5},{5,6},{6,7},{7,8},{8,9},{9,10},{10,1... | collective-permute-start | bytes 12296 | tf_op jit(solution)/shard_map/ppermute | solution.py:571
  18.2 4.2 %collective-permute-start.1 = (f32[8,128]{1,0:T(8,128)S(1)}, f32[8,128]{1,0:T(8,128)S(1)}, u32[]{:S(2)}, u32[]{:S(2)}) collective-permute-start(f32[8,128]{1,0:T(8,128)S(1)} %get-tuple-element.25), channel_id=1, source_target_pairs={{0,79},{1,0},{2,1},{3,2},{4,3},{5,4},{6,5},{7,6},{8,7},{9,8},{10,9... | collective-permute-start | bytes 12296 | tf_op jit(solution)/shard_map/ppermute | solution.py:572
  22.9 16.2 %copy-start.1 = (bf16[64,480]{1,0:T(8,128)(2,1)S(1)}, bf16[64,480]{1,0:T(8,128)(2,1)}, u32[]{:S(2)}) copy-start(bf16[64,480]{1,0:T(8,128)(2,1)} %constant.73.clone.first) | copy-start | bytes 184324
  22.9 16.1 %copy-start.5 = (f32[128,8]{0,1:T(8,128)S(1)}, f32[128,8]{0,1:T(8,128)}, u32[]{:S(2)}) copy-start(f32[128,8]{0,1:T(8,128)} %param.21) | copy-start | bytes 12292
  23.0 16.1 %copy-start.6 = (f32[8,128]{1,0:T(8,128)S(1)}, f32[8,128]{1,0:T(8,128)}, u32[]{:S(2)}) copy-start(f32[8,128]{1,0:T(8,128)} %w_out.3) | copy-start | bytes 12292
  23.0 16.1 %copy-start.7 = (bf16[16,96]{1,0:T(8,128)(2,1)S(1)}, bf16[16,96]{1,0:T(8,128)(2,1)}, u32[]{:S(2)}) copy-start(bf16[16,96]{1,0:T(8,128)(2,1)} %constant.76.clone.reduce_) | copy-start | bytes 9220
  42.3 4.5 %collective-permute-start.2 = (f32[96,128]{1,0:T(8,128)S(1)}, f32[96,128]{1,0:T(8,128)S(1)}, u32[]{:S(2)}, u32[]{:S(2)}) collective-permute-start(f32[96,128]{1,0:T(8,128)S(1)} %get-tuple-element.30), channel_id=1, source_target_pairs={{0,1},{1,2},{2,3},{3,4},{4,5},{5,6},{6,7},{7,8},{8,9},{9,10},{10,1... | collective-permute-start | bytes 147464 | tf_op jit(solution)/shard_map/ppermute | solution.py:571
  45.6 4.7 %collective-permute-start.3 = (f32[96,128]{1,0:T(8,128)S(1)}, f32[96,128]{1,0:T(8,128)S(1)}, u32[]{:S(2)}, u32[]{:S(2)}) collective-permute-start(f32[96,128]{1,0:T(8,128)S(1)} %get-tuple-element.31), channel_id=1, source_target_pairs={{0,79},{1,0},{2,1},{3,2},{4,3},{5,4},{6,5},{7,6},{8,7},{9,8},{10,9... | collective-permute-start | bytes 147464 | tf_op jit(solution)/shard_map/ppermute | solution.py:572
  45.6 4.7 %copy-start.3 = (bf16[64,384]{1,0:T(8,128)(2,1)S(1)}, bf16[64,384]{1,0:T(8,128)(2,1)}, u32[]{:S(2)}) copy-start(bf16[64,384]{1,0:T(8,128)(2,1)} %constant.74.clone.later) | copy-start | bytes 147460
  50.4 10.3 %copy-start.2 = (bf16[80,384]{1,0:T(8,128)(2,1)S(1)}, bf16[80,384]{1,0:T(8,128)(2,1)}, u32[]{:S(2)}) copy-start(bf16[80,384]{1,0:T(8,128)(2,1)} %constant.75.clone.last) | copy-start | bytes 184324
  55.9 1.2 %collective-permute-start.4 = (f32[96,128]{1,0:T(8,128)S(1)}, f32[96,128]{1,0:T(8,128)S(1)}, u32[]{:S(2)}, u32[]{:S(2)}) collective-permute-start(f32[96,128]{1,0:T(8,128)S(1)} %get-tuple-element.34), channel_id=1, source_target_pairs={{0,1},{1,2},{2,3},{3,4},{4,5},{5,6},{6,7},{7,8},{8,9},{9,10},{10,1... | collective-permute-start | bytes 147464 | tf_op jit(solution)/shard_map/ppermute | solution.py:571
  55.9 4.7 %collective-permute-start.5 = (f32[96,128]{1,0:T(8,128)S(1)}, f32[96,128]{1,0:T(8,128)S(1)}, u32[]{:S(2)}, u32[]{:S(2)}) collective-permute-start(f32[96,128]{1,0:T(8,128)S(1)} %get-tuple-element.35), channel_id=1, source_target_pairs={{0,79},{1,0},{2,1},{3,2},{4,3},{5,4},{6,5},{7,6},{8,7},{9,8},{10,9... | collective-permute-start | bytes 147464 | tf_op jit(solution)/shard_map/ppermute | solution.py:572
  66.7 2.4 %collective-permute-start.6 = (f32[16,128]{1,0:T(8,128)S(1)}, f32[16,128]{1,0:T(8,128)S(1)}, u32[]{:S(2)}, u32[]{:S(2)}) collective-permute-start(f32[16,128]{1,0:T(8,128)S(1)} %get-tuple-element.38), channel_id=1, source_target_pairs={{0,1},{1,2},{2,3},{3,4},{4,5},{5,6},{6,7},{7,8},{8,9},{9,10},{10,1... | collective-permute-start | bytes 24584 | tf_op jit(solution)/shard_map/ppermute | solution.py:571
  66.7 4.3 %collective-permute-start.7 = (f32[16,128]{1,0:T(8,128)S(1)}, f32[16,128]{1,0:T(8,128)S(1)}, u32[]{:S(2)}, u32[]{:S(2)}) collective-permute-start(f32[16,128]{1,0:T(8,128)S(1)} %get-tuple-element.39), channel_id=1, source_target_pairs={{0,79},{1,0},{2,1},{3,2},{4,3},{5,4},{6,5},{7,6},{8,7},{9,8},{10,9... | collective-permute-start | bytes 24584 | tf_op jit(solution)/shard_map/ppermute | solution.py:572
  67.2 3.8 %copy-start.4 = (f32[32,4]{1,0:T(8,128)S(1)}, f32[32,4]{1,0:T(8,128)}, u32[]{:S(2)}) copy-start(f32[32,4]{1,0:T(8,128)} %constant.77.clone.expand) | copy-start | bytes 1540

commit v6 on v5

--- a/solution.py
+++ b/solution.py
@@ -96,7 +96,7 @@
     padded_contract = np.concatenate([contract, np.zeros((16 - CB, BEADS))], axis=0)
     last = six_terms(np.concatenate([step, padded_contract @ step[:BEADS]], axis=0))
     reduce_ = three_terms(padded_contract)
-    return first, later, last, reduce_, (0.5 * outer_step * expand).astype(np.float32)
+    return first, later, last.astype(np.float32), reduce_, (0.5 * outer_step * expand).astype(np.float32)
 
 
 def lanes(source, index):
@@ -175,15 +175,20 @@
         index = neighbours[8 * g : 8 * g + 8, 128 * a : 128 * a + 128]
         offset = [looked(x, g, index) - centre[x] for x in range(3)]
         squared = offset[0] * offset[0] + offset[1] * offset[1] + offset[2] * offset[2]
-        w = weights[8 * g : 8 * g + 8, 128 * a : 128 * a + 128] * jnp.exp(-squared)
+        w = weights[8 * g : 8 * g + 8, 128 * a : 128 * a + 128] * jnp.exp2(-LOG2E * squared)
         for x in range(3):
             total[x] = total[x] + w * offset[x]
     return [jnp.sum(t, axis=0, keepdims=True) for t in total]
 
 
-def powers(squared):
-    even = jnp.exp(-0.2 * squared)
-    odd = jnp.exp(-(0.2 * 2.0**0.5) * squared)
+LOG2E = 1.4426950408889634
+
+
+def roots(squared):
+    return jnp.exp2((-0.2 * LOG2E) * squared), jnp.exp2((-0.2 * 2.0**0.5 * LOG2E) * squared)
+
+
+def powers(even, odd):
     out = [even, odd]
     for _ in range(3):
         even, odd = even * even, odd * odd
@@ -205,10 +210,13 @@
             for g in range(SLOTS // 8):
                 offset = [looked(c, x, a, g) - middle[x] for x in range(3)]
                 squared = offset[0] * offset[0] + offset[1] * offset[1] + offset[2] * offset[2]
+                even, odd = roots(squared)
                 for x in range(3):
                     offsets[c, a, g, x] = offset[x]
+                offsets[c, a, g, 3] = even
+                offsets[c, a, g, 4] = odd
                 w = weights[8 * g : 8 * g + 8, 128 * a : 128 * a + 128]
-                for r, basis in enumerate(powers(squared)):
+                for r, basis in enumerate(powers(even, odd)):
                     total[r] = total[r] + w * basis
             for r in range(NRBF):
                 messages[c, r : r + 1, 128 * a : 128 * a + 128] = jnp.sum(total[r], axis=0, keepdims=True) * (
@@ -220,7 +228,8 @@
         high = value.astype(bf16).astype(f32)
         terms = jnp.concatenate([high, high, value - high, jnp.zeros_like(high)], axis=0).astype(bf16)
         hidden = lax.dot_general(first, terms, (((0,), (0,)), ((), ())), preferred_element_type=f32)
-        hidden = hidden * (1.0 / (1.0 + jnp.exp(-hidden)))
+        half = 0.5 * hidden
+        hidden = half + half * jnp.tanh(half)
         radials[c] = jnp.dot(second, split_rows(hidden), preferred_element_type=f32)[0:NRBF]
 
     def force(c):
@@ -229,8 +238,7 @@
             total = [jnp.zeros((8, 128), f32) for _ in range(3)]
             for g in range(SLOTS // 8):
                 offset = [offsets[c, a, g, x] for x in range(3)]
-                squared = offset[0] * offset[0] + offset[1] * offset[1] + offset[2] * offset[2]
-                basis = powers(squared)
+                basis = powers(offsets[c, a, g, 3], offsets[c, a, g, 4])
                 profile = radial[0] * basis[0]
                 for r in range(1, NRBF):
                     profile = profile + radial[r] * basis[r]
@@ -280,7 +288,7 @@
     place = lax.broadcasted_iota(jnp.int16, (256, ATOMS), 0)
 
     def by_matmul(slot):
-        index = neighbours[pl.ds(slot, 1), :]
+        index = neighbours[slot : slot + 1, :]
         column = jnp.broadcast_to(index & 255, (16, ATOMS)).astype(jnp.int16)
         chosen = jnp.where(place == jnp.tile(column, (16, 1)), bf16(1), bf16(0))
         picked = jnp.dot(stacked[...], jnp.concatenate([chosen, chosen], axis=0), preferred_element_type=f32)
@@ -292,14 +300,14 @@
         )
         offset = other - rounded
         x, y, z = offset[0:few], offset[few : 2 * few], offset[2 * few :]
-        w = weights[pl.ds(slot, 1), :] * jnp.exp(-(x * x + y * y + z * z))
+        w = weights[slot : slot + 1, :] * jnp.exp2(-LOG2E * (x * x + y * y + z * z))
         total[0:few] += w * x
         total[BEADS : BEADS + few] += w * y
         total[2 * BEADS : 2 * BEADS + few] += w * z
 
     def by_lanes(g, a):
         at = slice(128 * a, 128 * a + 128)
-        slots = pl.ds(pl.multiple_of(8 * g, 8), 8)
+        slots = slice(8 * g, 8 * g + 8)
         index = neighbours[slots, at]
         lane, masks = index & 127, [(index >> 7) == k for k in range(1, WINDOW)]
         weight = weights[slots, at]
@@ -309,18 +317,16 @@
                 looked_up([rows_of(x, k) for k in range(WINDOW)], lane, masks) - rows_of(x, 1 + a)
                 for x in range(3)
             ]
-            w = weight * jnp.exp(-(offset[0] * offset[0] + offset[1] * offset[1] + offset[2] * offset[2]))
+            squared = offset[0] * offset[0] + offset[1] * offset[1] + offset[2] * offset[2]
+            w = weight * jnp.exp2(-LOG2E * squared)
             for x in range(3):
                 sums[8 * x + bead, :, at] += w * offset[x]
 
-    def group(g, _):
+    for g in range(SLOTS // 8):
         for j in range(8):
             by_matmul(g * 8 + j)
             if j % 2:
                 by_lanes(g, j // 2)
-        return 0
-
-    lax.fori_loop(0, SLOTS // 8, group, 0)
     for x in range(3):
         for bead in range(8):
             row = BEADS * x + few + bead
@@ -477,22 +483,27 @@
 
 def last_kernel(
     place, coords, veloc, below, above, neighbours, weights, mine, ghost_rows, last,
-    own, contracted, down, up, moved, rows, *scratch,
+    own, contracted, down, up, chosen, rows, *scratch,
 ):
+    chosen[...] = jnp.zeros_like(chosen)
+    for i, row in enumerate((place[1], BEADS + place[1], place[2], place[3])):
+        chosen[i : i + 1] = last[pl.ds(row, 1)]
+    chosen[4:8] = last[2 * BEADS : 2 * BEADS + CB]
+    table = chosen[...].astype(bf16)
     velocities = kicked(coords, veloc, below, above, neighbours, weights, mine, scratch)
-    moved[...] = propagated(coords[...], velocities, last)
+    moved = propagated(coords[...], velocities, table)
     for x in range(3):
-        at = slice(ATOMS * x, ATOMS * (x + 1))
-        own[x : x + 1] = moved[pl.ds(place[1], 1), at]
-        own[3 + x : 4 + x] = moved[pl.ds(BEADS + place[1], 1), at]
-        contracted[4 * x : 4 * x + 4] = moved[2 * BEADS : 2 * BEADS + CB, at]
+        part = moved[:, ATOMS * x : ATOMS * (x + 1)]
+        own[x : x + 1] = part[0:1]
+        own[3 + x : 4 + x] = part[1:2]
+        contracted[4 * x : 4 * x + 4] = part[4:8]
+        rows[0, 4 + x : 5 + x] = part[2:3]
+        rows[1, 4 + x : 5 + x] = part[3:4]
     own[6:8] = mine[6:8]
     contracted[12:16] = jnp.zeros((4, ATOMS), f32)
     for which, out in ((0, down), (1, up)):
         rows[which, 0:4] = contracted[8:12]
-        for x in range(3):
-            rows[which, 4 + x : 5 + x] = moved[pl.ds(place[2 + which], 1), ATOMS * x : ATOMS * (x + 1)]
-        rows[which, 7:8] = contracted[12:13]
+        rows[which, 7:8] = mine[6:7]
         index = ghost_rows[which : which + 1]
         out[0:8] = ghosts_of(lambda k: contracted[0:8, 128 * k : 128 * k + 128], index)
         out[8:16] = ghosts_of(lambda k: rows[which, :, 128 * k : 128 * k + 128], index)
@@ -622,7 +633,7 @@
     )
     groups = [[x * 8 + z * 4 + y for x in range(4) for y in range(4)] for z in range(2)]
     gathered = lax.all_to_all(block, "bead", 0, 0, axis_index_groups=groups, tiled=True)
-    offsets = ((CB, CHUNKS, SLOTS // 8, 3, 8, 128), f32)
+    offsets = ((CB, CHUNKS, SLOTS // 8, 5, 8, 128), f32)
     network = ((CB, NRBF, ATOMS), f32)
     w_in = w_in.T
     coords, veloc, down, up = call(
@@ -646,7 +657,7 @@
     own, contracted, down, up = call(
         last_kernel,
         [(8, ATOMS), (16, ATOMS), (16, 128), (16, 128)],
-        [((2 * BEADS + 16, 3 * ATOMS), f32), ((2, 8, ATOMS), f32)] + big,
+        [((16, 384), f32), ((2, 8, ATOMS), f32)] + big,
         (place, coords, veloc, below, above, neighbours, weights, mine, ghosts, last),
         (0,),
     )

time: 74.6 us -> 73.4 us (0.984)
  Pallas kernels: 22.3 us -> 21.2 us
    pallas_call x9, Pallas kernels: 22.3 us -> 21.2 us  [call(): pl.pallas_call(kernel, out_shape=shapes, in_specs=specs, out_specs=[pl.Bl...]
where the time goes in v6:
time: 73.4 us; the launch traced here: 73.2 us
  blocking collectives  28.8 us (39%)
  Pallas kernels  21.2 us (29%)
  waiting for transfers between devices  14.2 us (19%)
  starting transfers between devices  8.22 us (11%)
  between operations  0.75 us (1%)
    pallas_call x9, Pallas kernels, call(): pl.pallas_call(kernel, out_shape=shapes, in_specs=specs, out_specs=[pl.Bl...  21.2 us
    all_to_all x1, blocking collectives, body(): lax.all_to_all(block, 'bead', 0, 0, axis_index_groups=groups, tiled=True)  16.1 us
    all_gather x1, blocking collectives, body(): pair = lax.all_gather(mine, 'bead', axis=0, axis_index_groups=halves)  12.7 us
    ppermute x4, waiting for transfers between devices, exchange(): above = lax.ppermute(down, RING, ring(-1))  12.3 us
    ppermute x4, starting transfers between devices, exchange(): below = lax.ppermute(up, RING, ring(1))  7.21 us
    ppermute x4, waiting for transfers between devices, exchange(): below = lax.ppermute(up, RING, ring(1))  1.82 us
  transfers between devices with their start and end apart: 8, of which 6 were waited for; matrix products, arithmetic and copies ran while one was open for 0% of the time, Pallas kernels for 4%

profile of v6, /device:TPU:97, one launch (start us, length us, event | category | flops | bytes accessed | tf_op | source)
XLA Modules:
  0.0 73.2 jit_solution(17235719028264715444)
XLA Ops:
  0.6 0.0 copy-start
  0.6 0.9 %shard_map.149 = (f32[8,512]{1,0:T(8,128)S(1)}, s32[2,128]{1,0:T(2,128)S(1)}) custom-call(f32[3,1,512]{2,1,0:T(1,128)} %bitcast.17, f32[3,1,512]{2,1,0:T(1,128)} %bitcast.18, s32[1,512]{1,0:T(1,128)} %bitcast.19, s32[2,128]{1,0:T(2,128)} %bitcast.20, f32[2]{0:T(128)} %scale.1, f32[2]{0:T(128)} %mass_table.1), custom_call_target="tpu_custom_call" | custom-call | tf_op jit(solution)/shard_map/pallas_call | solution.py:557
  1.5 12.7 %all-gather = f32[16,512]{1,0:T(8,128)S(1)} all-gather(f32[8,512]{1,0:T(8,128)S(1)} %get-tuple-element.22.mine), channel_id=2, replica_groups={{0,64},{16,80},{32,96},{48,112},{128,192},{144,208},{160,224},{176,240}..., dimensions={0}, use_global_device_ids=true | all-gather | bytes 49152 | tf_op jit(solution)/shard_map/all_gather | solution.py:622
  14.2 0.1 shard_map.151
  14.3 3.9 %collective-permute-start = (f32[8,128]{1,0:T(8,128)S(1)}, f32[8,128]{1,0:T(8,128)S(1)}, u32[]{:S(2)}, u32[]{:S(2)}) collective-permute-start(f32[8,128]{1,0:T(8,128)S(1)} %get-tuple-element.24), channel_id=1, source_target_pairs={{0,1},{1,2},{2,3},{3,4},{4,5},{5,6},{6,7},{7,8},{8,9},{9,10},{10,1... | collective-permute-start | bytes 12296 | tf_op jit(solution)/shard_map/ppermute | solution.py:582
  18.2 0.0 collective-permute-start.1
  18.2 0.0 copy-done
  18.2 0.9 %shard_map.150.early = f32[7,4,4,8,128]{4,3,2,1,0:T(8,128)S(1)} custom-call(f32[2,8,512]{2,1,0:T(8,128)S(1)} %bitcast.13, s32[32,512]{1,0:T(8,128)S(1)} %copy-done), custom_call_target="tpu_custom_call" | custom-call | flops 1000000000 | bytes 1000000 | tf_op jit(solution)/shard_map/pallas_call | solution.py:557
  19.1 0.0 collective-permute-done.below
  19.1 3.3 %collective-permute-done.1.above = f32[8,128]{1,0:T(8,128)S(1)} collective-permute-done((f32[8,128]{1,0:T(8,128)S(1)}, f32[8,128]{1,0:T(8,128)S(1)}, u32[]{:S(2)}, u32[]{:S(2)}) %collective-permute-start.1) | collective-permute-done | bytes 4128 | tf_op jit(solution)/shard_map/ppermute | solution.py:583
  22.4 0.5 shard_map.152
  22.9 0.0 copy-start.2
  23.0 0.0 copy-start.5
  23.0 0.0 copy-start.6
  23.0 0.0 copy-start.7
  23.0 16.1 %all_to_all.5.gathered = f32[16,64,128]{2,1,0:T(8,128)S(1)} all-to-all(f32[16,64,128]{2,1,0:T(8,128)S(1)} %get-tuple-element.26), channel_id=1, replica_groups={{0,16,32,48,128,144,160,176,256,272,288,304,384,400,416,432},{64,80,96,..., dimensions={0} | all-to-all | bytes 1048576 | tf_op jit(solution)/shard_map/all_to_all | solution.py:635
  39.1 0.0 copy-done.2
  39.1 0.0 copy-done.5
  39.1 0.0 copy-done.6
  39.1 0.0 copy-done.7
  39.1 3.1 %shard_map.153 = (f32[96,512]{1,0:T(8,128)S(1)}, f32[96,512]{1,0:T(8,128)S(1)}, f32[96,128]{1,0:T(8,128)S(1)}, f32[96,128]{1,0:T(8,128)S(1)}) custom-call(f32[16,64,128]{2,1,0:T(8,128)S(1)} %all_to_all.5.gathered, s32[32,512]{1,0:T(8,128)S(1)} %copy-done, f32[32,512]{1,0:T(8,128)S(1)} %get-tuple-element.27.weights, f32[8,512]{1,0:T(8,128)S(1)} %get-tuple-element.22.mine, ...), custom_call_target="tpu_custom_call" | custom-call | tf_op jit(solution)/shard_map/pallas_call | solution.py:557
  42.3 3.3 %collective-permute-start.2 = (f32[96,128]{1,0:T(8,128)S(1)}, f32[96,128]{1,0:T(8,128)S(1)}, u32[]{:S(2)}, u32[]{:S(2)}) collective-permute-start(f32[96,128]{1,0:T(8,128)S(1)} %get-tuple-element.30), channel_id=1, source_target_pairs={{0,1},{1,2},{2,3},{3,4},{4,5},{5,6},{6,7},{7,8},{8,9},{9,10},{10,1... | collective-permute-start | bytes 147464 | tf_op jit(solution)/shard_map/ppermute | solution.py:582
  45.6 0.0 collective-permute-start.3
  45.6 0.0 copy-start.3
  45.6 1.2 %collective-permute-done.2.below = f32[96,128]{1,0:T(8,128)S(1)} collective-permute-done((f32[96,128]{1,0:T(8,128)S(1)}, f32[96,128]{1,0:T(8,128)S(1)}, u32[]{:S(2)}, u32[]{:S(2)}) %collective-permute-start.2) | collective-permute-done | bytes 49184 | tf_op jit(solution)/shard_map/ppermute | solution.py:582
  46.8 3.5 %collective-permute-done.3.above = f32[96,128]{1,0:T(8,128)S(1)} collective-permute-done((f32[96,128]{1,0:T(8,128)S(1)}, f32[96,128]{1,0:T(8,128)S(1)}, u32[]{:S(2)}, u32[]{:S(2)}) %collective-permute-start.3) | collective-permute-done | bytes 49184 | tf_op jit(solution)/shard_map/ppermute | solution.py:583
  50.3 0.0 copy-done.3
  50.3 0.0 copy-start.1
  50.3 5.0 %shard_map.154 = (f32[96,512]{1,0:T(8,128)S(1)}, f32[96,512]{1,0:T(8,128)S(1)}, f32[96,128]{1,0:T(8,128)S(1)}, f32[96,128]{1,0:T(8,128)S(1)}) custom-call(f32[96,512]{1,0:T(8,128)S(1)} %get-tuple-element.28.coords, f32[96,512]{1,0:T(8,128)S(1)} %get-tuple-element.29.veloc, f32[96,128]{1,0:T(8,128)S(1)} %collective-permute-done.2.below, ...), custom_call_target="tpu_custom_call" | custom-call | tf_op jit(solution)/shard_map/pallas_call | solution.py:557
  55.3 0.0 collective-permute-start.4
  55.3 0.5 collective-permute-start.5
  55.8 0.1 pad_add_fusion.place
  55.9 0.6 collective-permute-done.4.below
  56.5 3.5 %collective-permute-done.5.above = f32[96,128]{1,0:T(8,128)S(1)} collective-permute-done((f32[96,128]{1,0:T(8,128)S(1)}, f32[96,128]{1,0:T(8,128)S(1)}, u32[]{:S(2)}, u32[]{:S(2)}) %collective-permute-start.5) | collective-permute-done | bytes 49184 | tf_op jit(solution)/shard_map/ppermute | solution.py:583
  60.1 0.0 copy-done.1
  60.1 5.6 %shard_map.155 = (f32[8,512]{1,0:T(8,128)S(1)}, f32[16,512]{1,0:T(8,128)S(1)}, f32[16,128]{1,0:T(8,128)S(1)}, f32[16,128]{1,0:T(8,128)S(1)}) custom-call(s32[4]{0:T(128)S(1)} %pad_add_fusion.place, f32[96,512]{1,0:T(8,128)S(1)} %get-tuple-element.32.coords, f32[96,512]{1,0:T(8,128)S(1)} %get-tuple-element.33.veloc, ...), custom_call_target="tpu_custom_call" | custom-call | tf_op jit(solution)/shard_map/pallas_call | solution.py:557
  65.7 0.0 collective-permute-start.6
  65.7 0.5 collective-permute-start.7
  66.2 0.0 copy-start.4
  66.2 1.8 %shard_map.156.early = f32[15,4,4,8,128]{4,3,2,1,0:T(8,128)S(1)} custom-call(f32[8,512]{1,0:T(8,128)S(1)} %get-tuple-element.36.own, f32[16,512]{1,0:T(8,128)S(1)} %get-tuple-element.37.contracted, s32[32,512]{1,0:T(8,128)S(1)} %copy-done), custom_call_target="tpu_custom_call" | custom-call | flops 1000000000 | bytes 1000000 | tf_op jit(solution)/shard_map/pallas_call | solution.py:557
  68.1 0.0 collective-permute-done.6.below
  68.1 1.9 %collective-permute-done.7.above = f32[16,128]{1,0:T(8,128)S(1)} collective-permute-done((f32[16,128]{1,0:T(8,128)S(1)}, f32[16,128]{1,0:T(8,128)S(1)}, u32[]{:S(2)}, u32[]{:S(2)}) %collective-permute-start.7) | collective-permute-done | bytes 8224 | tf_op jit(solution)/shard_map/ppermute | solution.py:583
  70.0 0.0 copy-done.4
  70.0 3.2 %shard_map.157 = (f32[3,1,512]{2,1,0:T(1,128)}, f32[3,1,512]{2,1,0:T(1,128)}) custom-call(s32[4]{0:T(128)S(1)} %pad_add_fusion.place, f32[32,4]{1,0:T(8,128)S(1)} %copy-done.4, f32[8,512]{1,0:T(8,128)S(1)} %get-tuple-element.36.own, f32[16,512]{1,0:T(8,128)S(1)} %get-tuple-element.37.contracted, f32[15,4,4,8,128]{4,3,2,1,0:T(8,128)S(1)} %shard_map.156.early, ...), custom_call_target="tpu_custom_call" | custom-call | tf_op jit(solution)/shard_map/pallas_call | solution.py:557
Async XLA Ops:
  0.6 17.5 %copy-start = (s32[32,512]{1,0:T(8,128)S(1)}, s32[32,512]{1,0:T(8,128)}, u32[]{:S(2)}) copy-start(s32[32,512]{1,0:T(8,128)} %neighbours.13) | copy-start | bytes 196612
  14.3 4.8 %collective-permute-start = (f32[8,128]{1,0:T(8,128)S(1)}, f32[8,128]{1,0:T(8,128)S(1)}, u32[]{:S(2)}, u32[]{:S(2)}) collective-permute-start(f32[8,128]{1,0:T(8,128)S(1)} %get-tuple-element.24), channel_id=1, source_target_pairs={{0,1},{1,2},{2,3},{3,4},{4,5},{5,6},{6,7},{7,8},{8,9},{9,10},{10,1... | collective-permute-start | bytes 12296 | tf_op jit(solution)/shard_map/ppermute | solution.py:582
  18.2 4.2 %collective-permute-start.1 = (f32[8,128]{1,0:T(8,128)S(1)}, f32[8,128]{1,0:T(8,128)S(1)}, u32[]{:S(2)}, u32[]{:S(2)}) collective-permute-start(f32[8,128]{1,0:T(8,128)S(1)} %get-tuple-element.25), channel_id=1, source_target_pairs={{0,79},{1,0},{2,1},{3,2},{4,3},{5,4},{6,5},{7,6},{8,7},{9,8},{10,9... | collective-permute-start | bytes 12296 | tf_op jit(solution)/shard_map/ppermute | solution.py:583
  22.9 16.2 %copy-start.2 = (bf16[64,480]{1,0:T(8,128)(2,1)S(1)}, bf16[64,480]{1,0:T(8,128)(2,1)}, u32[]{:S(2)}) copy-start(bf16[64,480]{1,0:T(8,128)(2,1)} %constant.73.clone.first) | copy-start | bytes 184324
  23.0 16.1 %copy-start.5 = (f32[128,8]{0,1:T(8,128)S(1)}, f32[128,8]{0,1:T(8,128)}, u32[]{:S(2)}) copy-start(f32[128,8]{0,1:T(8,128)} %param.21) | copy-start | bytes 12292
  23.0 16.1 %copy-start.6 = (f32[8,128]{1,0:T(8,128)S(1)}, f32[8,128]{1,0:T(8,128)}, u32[]{:S(2)}) copy-start(f32[8,128]{1,0:T(8,128)} %w_out.3) | copy-start | bytes 12292
  23.0 16.1 %copy-start.7 = (bf16[16,96]{1,0:T(8,128)(2,1)S(1)}, bf16[16,96]{1,0:T(8,128)(2,1)}, u32[]{:S(2)}) copy-start(bf16[16,96]{1,0:T(8,128)(2,1)} %constant.76.clone.reduce_) | copy-start | bytes 9220
  42.3 4.5 %collective-permute-start.2 = (f32[96,128]{1,0:T(8,128)S(1)}, f32[96,128]{1,0:T(8,128)S(1)}, u32[]{:S(2)}, u32[]{:S(2)}) collective-permute-start(f32[96,128]{1,0:T(8,128)S(1)} %get-tuple-element.30), channel_id=1, source_target_pairs={{0,1},{1,2},{2,3},{3,4},{4,5},{5,6},{6,7},{7,8},{8,9},{9,10},{10,1... | collective-permute-start | bytes 147464 | tf_op jit(solution)/shard_map/ppermute | solution.py:582
  45.6 4.7 %collective-permute-start.3 = (f32[96,128]{1,0:T(8,128)S(1)}, f32[96,128]{1,0:T(8,128)S(1)}, u32[]{:S(2)}, u32[]{:S(2)}) collective-permute-start(f32[96,128]{1,0:T(8,128)S(1)} %get-tuple-element.31), channel_id=1, source_target_pairs={{0,79},{1,0},{2,1},{3,2},{4,3},{5,4},{6,5},{7,6},{8,7},{9,8},{10,9... | collective-permute-start | bytes 147464 | tf_op jit(solution)/shard_map/ppermute | solution.py:583
  45.6 4.7 %copy-start.3 = (bf16[64,384]{1,0:T(8,128)(2,1)S(1)}, bf16[64,384]{1,0:T(8,128)(2,1)}, u32[]{:S(2)}) copy-start(bf16[64,384]{1,0:T(8,128)(2,1)} %constant.74.clone.later) | copy-start | bytes 147460
  50.3 9.7 %copy-start.1 = (f32[80,384]{1,0:T(8,128)S(1)}, f32[80,384]{1,0:T(8,128)}, u32[]{:S(2)}) copy-start(f32[80,384]{1,0:T(8,128)} %constant.75.clone.last) | copy-start | bytes 368644
  55.3 1.2 %collective-permute-start.4 = (f32[96,128]{1,0:T(8,128)S(1)}, f32[96,128]{1,0:T(8,128)S(1)}, u32[]{:S(2)}, u32[]{:S(2)}) collective-permute-start(f32[96,128]{1,0:T(8,128)S(1)} %get-tuple-element.34), channel_id=1, source_target_pairs={{0,1},{1,2},{2,3},{3,4},{4,5},{5,6},{6,7},{7,8},{8,9},{9,10},{10,1... | collective-permute-start | bytes 147464 | tf_op jit(solution)/shard_map/ppermute | solution.py:582
  55.3 4.7 %collective-permute-start.5 = (f32[96,128]{1,0:T(8,128)S(1)}, f32[96,128]{1,0:T(8,128)S(1)}, u32[]{:S(2)}, u32[]{:S(2)}) collective-permute-start(f32[96,128]{1,0:T(8,128)S(1)} %get-tuple-element.35), channel_id=1, source_target_pairs={{0,79},{1,0},{2,1},{3,2},{4,3},{5,4},{6,5},{7,6},{8,7},{9,8},{10,9... | collective-permute-start | bytes 147464 | tf_op jit(solution)/shard_map/ppermute | solution.py:583
  65.7 2.4 %collective-permute-start.6 = (f32[16,128]{1,0:T(8,128)S(1)}, f32[16,128]{1,0:T(8,128)S(1)}, u32[]{:S(2)}, u32[]{:S(2)}) collective-permute-start(f32[16,128]{1,0:T(8,128)S(1)} %get-tuple-element.38), channel_id=1, source_target_pairs={{0,1},{1,2},{2,3},{3,4},{4,5},{5,6},{6,7},{7,8},{8,9},{9,10},{10,1... | collective-permute-start | bytes 24584 | tf_op jit(solution)/shard_map/ppermute | solution.py:582
  65.7 4.3 %collective-permute-start.7 = (f32[16,128]{1,0:T(8,128)S(1)}, f32[16,128]{1,0:T(8,128)S(1)}, u32[]{:S(2)}, u32[]{:S(2)}) collective-permute-start(f32[16,128]{1,0:T(8,128)S(1)} %get-tuple-element.39), channel_id=1, source_target_pairs={{0,79},{1,0},{2,1},{3,2},{4,3},{5,4},{6,5},{7,6},{8,7},{9,8},{10,9... | collective-permute-start | bytes 24584 | tf_op jit(solution)/shard_map/ppermute | solution.py:583
  66.2 3.8 %copy-start.4 = (f32[32,4]{1,0:T(8,128)S(1)}, f32[32,4]{1,0:T(8,128)}, u32[]{:S(2)}) copy-start(f32[32,4]{1,0:T(8,128)} %constant.77.clone.expand) | copy-start | bytes 1540

commit v7 on v6

--- a/solution.py
+++ b/solution.py
@@ -94,9 +94,17 @@
     first = six_terms(np.concatenate([step, 0.5 * outer_step * kick], axis=1))
     later = six_terms(step)
     padded_contract = np.concatenate([contract, np.zeros((16 - CB, BEADS))], axis=0)
-    last = six_terms(np.concatenate([step, padded_contract @ step[:BEADS]], axis=0))
     reduce_ = three_terms(padded_contract)
-    return first, later, last.astype(np.float32), reduce_, (0.5 * outer_step * expand).astype(np.float32)
+    contracted = contract @ step[:BEADS]
+    last = np.zeros((BEADS, 3, 16, 6 * 2 * BEADS), jnp.bfloat16)
+    gains = np.zeros((BEADS, 8, 128), np.float32)
+    for row, bead in enumerate(order):
+        gains[bead, :CB] = 0.5 * outer_step * expand[row][:, None]
+        for place in range(3):
+            below = row ^ 16 if place == 0 else row
+            above = row ^ 16 if place == 2 else row
+            last[bead, place, :8] = six_terms(np.concatenate([step[[row, BEADS + row, below, above]], contracted]))
+    return first, later, last.reshape(3 * BEADS, 16, -1), reduce_, gains
 
 
 def lanes(source, index):
@@ -345,20 +353,24 @@
 
 
 def first_kernel(
-    pos, mom, species, ghost_rows, scale, mass_table, out, ghosts, pos_in, mom_in, species_in, scale_in, mass_in, sems
+    pos, mom, species, ghost_rows, scale, mass_table, all_last, all_gains,
+    out, ghosts, last, gains,
+    pos_in, mom_in, species_in, scale_in, mass_in, sems,
 ):
+    bead, domain = lax.axis_index("bead"), lax.axis_index("space")
+    place = jnp.where(domain == 0, 0, jnp.where(domain == N_SPACE - 1, 2, 1))
     copies = [
         pltpu.make_async_copy(source, target, sems.at[i])
         for i, (source, target) in enumerate(
             (
                 (scale, scale_in), (mass_table, mass_in), (species, species_in), (mom, mom_in), (pos, pos_in),
-                (ghost_rows, ghosts),
+                (ghost_rows, ghosts), (all_last.at[3 * bead + place], last), (all_gains.at[bead], gains),
             )
         )
     ]
     for copy in copies:
         copy.start()
-    for copy in copies:
+    for copy in copies[:5]:
         copy.wait()
     mass = by_species(species_in[...], mass_in)
     for x in range(3):
@@ -366,6 +378,8 @@
         out[3 + x : 4 + x] = mom_in[x] / mass
     out[6:7] = by_species(species_in[...], scale_in)
     out[7:8] = mass
+    for copy in copies[5:]:
+        copy.wait()
 
 
 def send_kernel(pair, ghost_rows, down, up, rows):
@@ -482,16 +496,11 @@
 
 
 def last_kernel(
-    place, coords, veloc, below, above, neighbours, weights, mine, ghost_rows, last,
-    own, contracted, down, up, chosen, rows, *scratch,
+    coords, veloc, below, above, neighbours, weights, mine, ghost_rows, last,
+    own, contracted, down, up, rows, *scratch,
 ):
-    chosen[...] = jnp.zeros_like(chosen)
-    for i, row in enumerate((place[1], BEADS + place[1], place[2], place[3])):
-        chosen[i : i + 1] = last[pl.ds(row, 1)]
-    chosen[4:8] = last[2 * BEADS : 2 * BEADS + CB]
-    table = chosen[...].astype(bf16)
     velocities = kicked(coords, veloc, below, above, neighbours, weights, mine, scratch)
-    moved = propagated(coords[...], velocities, table)
+    moved = propagated(coords[...], velocities, last)
     for x in range(3):
         part = moved[:, ATOMS * x : ATOMS * (x + 1)]
         own[x : x + 1] = part[0:1]
@@ -520,7 +529,7 @@
 
 
 def end_kernel(
-    place, expand, own, contracted, early, below, above, neighbours, weights, w_in, w_out,
+    gains, own, contracted, early, below, above, neighbours, weights, w_in, w_out,
     new_pos, new_mom,
     offsets, messages, radials, slow,
 ):
@@ -546,7 +555,7 @@
         for x in range(3):
             value = mass[:, at] * own[3 + x : 4 + x, at] + (0.5 * inner_step) * charge[:, at] * force[x]
             for c in range(CB):
-                value = value + expand[place[1], c] * slow[c, x, a : a + 1]
+                value = value + gains[c : c + 1] * slow[c, x, a : a + 1]
             new_mom[x, :, at] = value
             new_pos[x, :, at] = own[x : x + 1, at]
 
@@ -587,33 +596,26 @@
 def body(
     positions, momenta, neighbours, ghost_rows, species, species_scale, mass_table, w_in, w_out
 ):
-    first, later, last, reduce_, expand = tables()
-    first, later, last, reduce_ = (jnp.asarray(t) for t in (first, later, last, reduce_))
-    expand = jnp.asarray(expand)
-    bead = lax.axis_index("bead")
-    domain = lax.axis_index("space")
-    half = (bead // 4) % 2
-    row = half * 16 + (bead // 8) * 4 + bead % 4
-    other = (1 - half) * 16 + (bead // 8) * 4 + bead % 4
-    row_below = jnp.where(domain == 0, other, row)
-    row_above = jnp.where(domain == N_SPACE - 1, other, row)
-    place = jnp.stack([half, row, row_below, row_above]).astype(jnp.int32)
+    first, later, last, reduce_, gains = (jnp.asarray(t) for t in tables())
 
     pos = positions.transpose(1, 0, 2)
     mom = momenta.transpose(1, 0, 2)
     kinds = species.reshape(1, ATOMS)
     ghosts = ghost_rows.reshape(2, 128)
 
-    mine, ghosts = call(
+    mine, ghosts, last, gains = call(
         first_kernel,
-        [(8, ATOMS), jax.ShapeDtypeStruct((2, 128), jnp.int32)],
+        [
+            (8, ATOMS), jax.ShapeDtypeStruct((2, 128), jnp.int32), jax.ShapeDtypeStruct(last.shape[1:], bf16),
+            gains.shape[1:],
+        ],
         [
             ((3, 1, ATOMS), f32), ((3, 1, ATOMS), f32), ((1, ATOMS), jnp.int32),
-            pltpu.SMEM((2,), f32), pltpu.SMEM((2,), f32), pltpu.SemaphoreType.DMA((6,)),
+            pltpu.SMEM((2,), f32), pltpu.SMEM((2,), f32), pltpu.SemaphoreType.DMA((8,)),
         ],
         tuple(
             pltpu.with_memory_space_constraint(v, pltpu.HBM)
-            for v in (pos, mom, kinds, ghosts, species_scale, mass_table)
+            for v in (pos, mom, kinds, ghosts, species_scale, mass_table, last, gains)
         ),
         space=pltpu.HBM,
     )
@@ -657,9 +659,8 @@
     own, contracted, down, up = call(
         last_kernel,
         [(8, ATOMS), (16, ATOMS), (16, 128), (16, 128)],
-        [((16, 384), f32), ((2, 8, ATOMS), f32)] + big,
-        (place, coords, veloc, below, above, neighbours, weights, mine, ghosts, last),
-        (0,),
+        [((2, 8, ATOMS), f32)] + big,
+        (coords, veloc, below, above, neighbours, weights, mine, ghosts, last),
     )
     below, above = exchange(down, up)
     (early,) = call(
@@ -669,8 +670,7 @@
         end_kernel,
         [(3, 1, ATOMS), (3, 1, ATOMS)],
         [offsets, network, network, ((CB, 3, CHUNKS, 128), f32)],
-        (place, expand, own, contracted, early, below, above, neighbours, weights, w_in, w_out),
-        (0, 1),
+        (gains, own, contracted, early, below, above, neighbours, weights, w_in, w_out),
     )
     return new_pos.transpose(1, 0, 2), new_mom.transpose(1, 0, 2)
 

time: 73.4 us -> 71.9 us (0.980)
  Pallas kernels: 21.2 us -> 19.8 us
    pallas_call x9, Pallas kernels: 21.2 us -> 19.8 us  [call(): pl.pallas_call(kernel, out_shape=shapes, in_specs=specs, out_specs=[pl.Bl...]
where the time goes in v7:
time: 71.9 us; the launch traced here: 71.7 us
  blocking collectives  28.7 us (40%)
  Pallas kernels  19.8 us (28%)
  waiting for transfers between devices  14.2 us (20%)
  starting transfers between devices  8.21 us (11%)
  between operations  0.76 us (1%)
    pallas_call x9, Pallas kernels, call(): pl.pallas_call(kernel, out_shape=shapes, in_specs=specs, out_specs=[pl.Bl...  19.8 us
    all_to_all x1, blocking collectives, body(): lax.all_to_all(block, 'bead', 0, 0, axis_index_groups=groups, tiled=True)  16 us
    all_gather x1, blocking collectives, body(): pair = lax.all_gather(mine, 'bead', axis=0, axis_index_groups=halves)  12.7 us
    ppermute x4, waiting for transfers between devices, exchange(): above = lax.ppermute(down, RING, ring(-1))  12.3 us
    ppermute x4, starting transfers between devices, exchange(): below = lax.ppermute(up, RING, ring(1))  7.2 us
    ppermute x4, waiting for transfers between devices, exchange(): below = lax.ppermute(up, RING, ring(1))  1.9 us
  transfers between devices with their start and end apart: 8, of which 6 were waited for; matrix products, arithmetic and copies ran while one was open for 0% of the time, Pallas kernels for 4%

profile of v7, /device:TPU:97, one launch (start us, length us, event | category | flops | bytes accessed | tf_op | source)
XLA Modules:
  0.0 71.7 jit_solution(428640391530218213)
XLA Ops:
  0.6 0.0 copy-start
  0.6 0.9 %shard_map.149 = (f32[8,512]{1,0:T(8,128)S(1)}, s32[2,128]{1,0:T(2,128)S(1)}, bf16[16,384]{1,0:T(8,128)(2,1)S(1)}, f32[8,128]{1,0:T(8,128)S(1)}) custom-call(f32[3,1,512]{2,1,0:T(1,128)} %bitcast.13, f32[3,1,512]{2,1,0:T(1,128)} %bitcast.14, s32[1,512]{1,0:T(1,128)} %bitcast.15, s32[2,128]{1,0:T(2,128)} %bitcast.16, f32[2]{0:T(128)} %scale.1, f32[2]{0:T(128)} %mass_table.1, ...), custom_call_target="tpu_custom_call" | custom-call | tf_op jit(solution)/shard_map/pallas_call | solution.py:566
  1.5 12.7 %all-gather = f32[16,512]{1,0:T(8,128)S(1)} all-gather(f32[8,512]{1,0:T(8,128)S(1)} %get-tuple-element.25.mine), channel_id=2, replica_groups={{0,64},{16,80},{32,96},{48,112},{128,192},{144,208},{160,224},{176,240}..., dimensions={0}, use_global_device_ids=true | all-gather | bytes 49152 | tf_op jit(solution)/shard_map/all_gather | solution.py:624
  14.3 0.1 shard_map.151
  14.3 3.9 %collective-permute-start = (f32[8,128]{1,0:T(8,128)S(1)}, f32[8,128]{1,0:T(8,128)S(1)}, u32[]{:S(2)}, u32[]{:S(2)}) collective-permute-start(f32[8,128]{1,0:T(8,128)S(1)} %get-tuple-element.27), channel_id=1, source_target_pairs={{0,1},{1,2},{2,3},{3,4},{4,5},{5,6},{6,7},{7,8},{8,9},{9,10},{10,1... | collective-permute-start | bytes 12296 | tf_op jit(solution)/shard_map/ppermute | solution.py:591
  18.2 0.0 collective-permute-start.1
  18.2 0.0 copy-done
  18.2 0.9 %shard_map.150.early = f32[7,4,4,8,128]{4,3,2,1,0:T(8,128)S(1)} custom-call(f32[2,8,512]{2,1,0:T(8,128)S(1)} %bitcast.9, s32[32,512]{1,0:T(8,128)S(1)} %copy-done), custom_call_target="tpu_custom_call" | custom-call | flops 1000000000 | bytes 1000000 | tf_op jit(solution)/shard_map/pallas_call | solution.py:566
  19.1 0.0 copy-start.1
  19.1 0.0 copy-start.3
  19.1 0.0 copy-start.4
  19.1 0.0 copy-start.5
  19.1 0.0 copy-start.2
  19.2 0.0 collective-permute-done.below
  19.2 3.3 %collective-permute-done.1.above = f32[8,128]{1,0:T(8,128)S(1)} collective-permute-done((f32[8,128]{1,0:T(8,128)S(1)}, f32[8,128]{1,0:T(8,128)S(1)}, u32[]{:S(2)}, u32[]{:S(2)}) %collective-permute-start.1) | collective-permute-done | bytes 4128 | tf_op jit(solution)/shard_map/ppermute | solution.py:592
  22.4 0.5 shard_map.152
  23.0 16.0 %all_to_all.5.gathered = f32[16,64,128]{2,1,0:T(8,128)S(1)} all-to-all(f32[16,64,128]{2,1,0:T(8,128)S(1)} %get-tuple-element.29), channel_id=1, replica_groups={{0,16,32,48,128,144,160,176,256,272,288,304,384,400,416,432},{64,80,96,..., dimensions={0} | all-to-all | bytes 1048576 | tf_op jit(solution)/shard_map/all_to_all | solution.py:637
  38.9 0.0 copy-done.1
  39.0 0.0 copy-done.3
  39.0 0.0 copy-done.4
  39.0 0.0 copy-done.5
  39.0 3.1 %shard_map.153 = (f32[96,512]{1,0:T(8,128)S(1)}, f32[96,512]{1,0:T(8,128)S(1)}, f32[96,128]{1,0:T(8,128)S(1)}, f32[96,128]{1,0:T(8,128)S(1)}) custom-call(f32[16,64,128]{2,1,0:T(8,128)S(1)} %all_to_all.5.gathered, s32[32,512]{1,0:T(8,128)S(1)} %copy-done, f32[32,512]{1,0:T(8,128)S(1)} %get-tuple-element.30.weights, f32[8,512]{1,0:T(8,128)S(1)} %get-tuple-element.25.mine, ...), custom_call_target="tpu_custom_call" | custom-call | tf_op jit(solution)/shard_map/pallas_call | solution.py:566
  42.1 3.3 %collective-permute-start.2 = (f32[96,128]{1,0:T(8,128)S(1)}, f32[96,128]{1,0:T(8,128)S(1)}, u32[]{:S(2)}, u32[]{:S(2)}) collective-permute-start(f32[96,128]{1,0:T(8,128)S(1)} %get-tuple-element.33), channel_id=1, source_target_pairs={{0,1},{1,2},{2,3},{3,4},{4,5},{5,6},{6,7},{7,8},{8,9},{9,10},{10,1... | collective-permute-start | bytes 147464 | tf_op jit(solution)/shard_map/ppermute | solution.py:591
  45.4 0.0 collective-permute-start.3
  45.4 1.2 %collective-permute-done.2.below = f32[96,128]{1,0:T(8,128)S(1)} collective-permute-done((f32[96,128]{1,0:T(8,128)S(1)}, f32[96,128]{1,0:T(8,128)S(1)}, u32[]{:S(2)}, u32[]{:S(2)}) %collective-permute-start.2) | collective-permute-done | bytes 49184 | tf_op jit(solution)/shard_map/ppermute | solution.py:591
  46.6 3.5 %collective-permute-done.3.above = f32[96,128]{1,0:T(8,128)S(1)} collective-permute-done((f32[96,128]{1,0:T(8,128)S(1)}, f32[96,128]{1,0:T(8,128)S(1)}, u32[]{:S(2)}, u32[]{:S(2)}) %collective-permute-start.3) | collective-permute-done | bytes 49184 | tf_op jit(solution)/shard_map/ppermute | solution.py:592
  50.2 0.0 copy-done.2
  50.2 5.0 %shard_map.154 = (f32[96,512]{1,0:T(8,128)S(1)}, f32[96,512]{1,0:T(8,128)S(1)}, f32[96,128]{1,0:T(8,128)S(1)}, f32[96,128]{1,0:T(8,128)S(1)}) custom-call(f32[96,512]{1,0:T(8,128)S(1)} %get-tuple-element.31.coords, f32[96,512]{1,0:T(8,128)S(1)} %get-tuple-element.32.veloc, f32[96,128]{1,0:T(8,128)S(1)} %collective-permute-done.2.below, ...), custom_call_target="tpu_custom_call" | custom-call | tf_op jit(solution)/shard_map/pallas_call | solution.py:566
  55.1 0.0 collective-permute-start.4
  55.2 0.5 collective-permute-start.5
  55.7 0.7 %collective-permute-done.4.below = f32[96,128]{1,0:T(8,128)S(1)} collective-permute-done((f32[96,128]{1,0:T(8,128)S(1)}, f32[96,128]{1,0:T(8,128)S(1)}, u32[]{:S(2)}, u32[]{:S(2)}) %collective-permute-start.4) | collective-permute-done | bytes 49184 | tf_op jit(solution)/shard_map/ppermute | solution.py:591
  56.4 3.5 %collective-permute-done.5.above = f32[96,128]{1,0:T(8,128)S(1)} collective-permute-done((f32[96,128]{1,0:T(8,128)S(1)}, f32[96,128]{1,0:T(8,128)S(1)}, u32[]{:S(2)}, u32[]{:S(2)}) %collective-permute-start.5) | collective-permute-done | bytes 49184 | tf_op jit(solution)/shard_map/ppermute | solution.py:592
  59.9 5.1 %shard_map.155 = (f32[8,512]{1,0:T(8,128)S(1)}, f32[16,512]{1,0:T(8,128)S(1)}, f32[16,128]{1,0:T(8,128)S(1)}, f32[16,128]{1,0:T(8,128)S(1)}) custom-call(f32[96,512]{1,0:T(8,128)S(1)} %get-tuple-element.35.coords, f32[96,512]{1,0:T(8,128)S(1)} %get-tuple-element.36.veloc, f32[96,128]{1,0:T(8,128)S(1)} %collective-permute-done.4.below, ...), custom_call_target="tpu_custom_call" | custom-call | tf_op jit(solution)/shard_map/pallas_call | solution.py:566
  65.0 0.0 collective-permute-start.6
  65.0 0.5 collective-permute-start.7
  65.5 1.8 %shard_map.156.early = f32[15,4,4,8,128]{4,3,2,1,0:T(8,128)S(1)} custom-call(f32[8,512]{1,0:T(8,128)S(1)} %get-tuple-element.40.own, f32[16,512]{1,0:T(8,128)S(1)} %get-tuple-element.41.contracted, s32[32,512]{1,0:T(8,128)S(1)} %copy-done), custom_call_target="tpu_custom_call" | custom-call | flops 1000000000 | bytes 1000000 | tf_op jit(solution)/shard_map/pallas_call | solution.py:566
  67.3 0.0 collective-permute-done.6.below
  67.4 1.9 %collective-permute-done.7.above = f32[16,128]{1,0:T(8,128)S(1)} collective-permute-done((f32[16,128]{1,0:T(8,128)S(1)}, f32[16,128]{1,0:T(8,128)S(1)}, u32[]{:S(2)}, u32[]{:S(2)}) %collective-permute-start.7) | collective-permute-done | bytes 8224 | tf_op jit(solution)/shard_map/ppermute | solution.py:592
  69.3 2.4 %shard_map.157 = (f32[3,1,512]{2,1,0:T(1,128)}, f32[3,1,512]{2,1,0:T(1,128)}) custom-call(f32[8,128]{1,0:T(8,128)S(1)} %get-tuple-element.24.gains, f32[8,512]{1,0:T(8,128)S(1)} %get-tuple-element.40.own, f32[16,512]{1,0:T(8,128)S(1)} %get-tuple-element.41.contracted, f32[15,4,4,8,128]{4,3,2,1,0:T(8,128)S(1)} %shard_map.156.early, ...), custom_call_target="tpu_custom_call" | custom-call | tf_op jit(solution)/shard_map/pallas_call | solution.py:566
Async XLA Ops:
  0.6 17.6 %copy-start = (s32[32,512]{1,0:T(8,128)S(1)}, s32[32,512]{1,0:T(8,128)}, u32[]{:S(2)}) copy-start(s32[32,512]{1,0:T(8,128)} %neighbours.13) | copy-start | bytes 196612
  14.3 4.8 %collective-permute-start = (f32[8,128]{1,0:T(8,128)S(1)}, f32[8,128]{1,0:T(8,128)S(1)}, u32[]{:S(2)}, u32[]{:S(2)}) collective-permute-start(f32[8,128]{1,0:T(8,128)S(1)} %get-tuple-element.27), channel_id=1, source_target_pairs={{0,1},{1,2},{2,3},{3,4},{4,5},{5,6},{6,7},{7,8},{8,9},{9,10},{10,1... | collective-permute-start | bytes 12296 | tf_op jit(solution)/shard_map/ppermute | solution.py:591
  18.2 4.2 %collective-permute-start.1 = (f32[8,128]{1,0:T(8,128)S(1)}, f32[8,128]{1,0:T(8,128)S(1)}, u32[]{:S(2)}, u32[]{:S(2)}) collective-permute-start(f32[8,128]{1,0:T(8,128)S(1)} %get-tuple-element.28), channel_id=1, source_target_pairs={{0,79},{1,0},{2,1},{3,2},{4,3},{5,4},{6,5},{7,6},{8,7},{9,8},{10,9... | collective-permute-start | bytes 12296 | tf_op jit(solution)/shard_map/ppermute | solution.py:592
  19.1 19.9 %copy-start.1 = (bf16[64,480]{1,0:T(8,128)(2,1)S(1)}, bf16[64,480]{1,0:T(8,128)(2,1)}, u32[]{:S(2)}) copy-start(bf16[64,480]{1,0:T(8,128)(2,1)} %constant.10.clone.first) | copy-start | bytes 184324
  19.1 19.8 %copy-start.3 = (f32[128,8]{0,1:T(8,128)S(1)}, f32[128,8]{0,1:T(8,128)}, u32[]{:S(2)}) copy-start(f32[128,8]{0,1:T(8,128)} %param.21) | copy-start | bytes 12292
  19.1 19.8 %copy-start.4 = (f32[8,128]{1,0:T(8,128)S(1)}, f32[8,128]{1,0:T(8,128)}, u32[]{:S(2)}) copy-start(f32[8,128]{1,0:T(8,128)} %w_out.3) | copy-start | bytes 12292
  19.1 19.8 %copy-start.5 = (bf16[16,96]{1,0:T(8,128)(2,1)S(1)}, bf16[16,96]{1,0:T(8,128)(2,1)}, u32[]{:S(2)}) copy-start(bf16[16,96]{1,0:T(8,128)(2,1)} %constant.13.clone.reduce_) | copy-start | bytes 9220
  19.1 31.0 %copy-start.2 = (bf16[64,384]{1,0:T(8,128)(2,1)S(1)}, bf16[64,384]{1,0:T(8,128)(2,1)}, u32[]{:S(2)}) copy-start(bf16[64,384]{1,0:T(8,128)(2,1)} %constant.11.clone.later) | copy-start | bytes 147460
  42.1 4.5 %collective-permute-start.2 = (f32[96,128]{1,0:T(8,128)S(1)}, f32[96,128]{1,0:T(8,128)S(1)}, u32[]{:S(2)}, u32[]{:S(2)}) collective-permute-start(f32[96,128]{1,0:T(8,128)S(1)} %get-tuple-element.33), channel_id=1, source_target_pairs={{0,1},{1,2},{2,3},{3,4},{4,5},{5,6},{6,7},{7,8},{8,9},{9,10},{10,1... | collective-permute-start | bytes 147464 | tf_op jit(solution)/shard_map/ppermute | solution.py:591
  45.4 4.7 %collective-permute-start.3 = (f32[96,128]{1,0:T(8,128)S(1)}, f32[96,128]{1,0:T(8,128)S(1)}, u32[]{:S(2)}, u32[]{:S(2)}) collective-permute-start(f32[96,128]{1,0:T(8,128)S(1)} %get-tuple-element.34), channel_id=1, source_target_pairs={{0,79},{1,0},{2,1},{3,2},{4,3},{5,4},{6,5},{7,6},{8,7},{9,8},{10,9... | collective-permute-start | bytes 147464 | tf_op jit(solution)/shard_map/ppermute | solution.py:592
  55.1 1.2 %collective-permute-start.4 = (f32[96,128]{1,0:T(8,128)S(1)}, f32[96,128]{1,0:T(8,128)S(1)}, u32[]{:S(2)}, u32[]{:S(2)}) collective-permute-start(f32[96,128]{1,0:T(8,128)S(1)} %get-tuple-element.37), channel_id=1, source_target_pairs={{0,1},{1,2},{2,3},{3,4},{4,5},{5,6},{6,7},{7,8},{8,9},{9,10},{10,1... | collective-permute-start | bytes 147464 | tf_op jit(solution)/shard_map/ppermute | solution.py:591
  55.2 4.7 %collective-permute-start.5 = (f32[96,128]{1,0:T(8,128)S(1)}, f32[96,128]{1,0:T(8,128)S(1)}, u32[]{:S(2)}, u32[]{:S(2)}) collective-permute-start(f32[96,128]{1,0:T(8,128)S(1)} %get-tuple-element.38), channel_id=1, source_target_pairs={{0,79},{1,0},{2,1},{3,2},{4,3},{5,4},{6,5},{7,6},{8,7},{9,8},{10,9... | collective-permute-start | bytes 147464 | tf_op jit(solution)/shard_map/ppermute | solution.py:592
  65.0 2.4 %collective-permute-start.6 = (f32[16,128]{1,0:T(8,128)S(1)}, f32[16,128]{1,0:T(8,128)S(1)}, u32[]{:S(2)}, u32[]{:S(2)}) collective-permute-start(f32[16,128]{1,0:T(8,128)S(1)} %get-tuple-element.42), channel_id=1, source_target_pairs={{0,1},{1,2},{2,3},{3,4},{4,5},{5,6},{6,7},{7,8},{8,9},{9,10},{10,1... | collective-permute-start | bytes 24584 | tf_op jit(solution)/shard_map/ppermute | solution.py:591
  65.0 4.3 %collective-permute-start.7 = (f32[16,128]{1,0:T(8,128)S(1)}, f32[16,128]{1,0:T(8,128)S(1)}, u32[]{:S(2)}, u32[]{:S(2)}) collective-permute-start(f32[16,128]{1,0:T(8,128)S(1)} %get-tuple-element.43), channel_id=1, source_target_pairs={{0,79},{1,0},{2,1},{3,2},{4,3},{5,4},{6,5},{7,6},{8,7},{9,8},{10,9... | collective-permute-start | bytes 24584 | tf_op jit(solution)/shard_map/ppermute | solution.py:592

commit v8 on v7

--- a/solution.py
+++ b/solution.py
@@ -264,7 +264,10 @@
         force(c)
 
 
-def cheap_of_all(coords, below, above, neighbours, weights, stacked, total, table, sums):
+EARLY = 4
+
+
+def cheap_of_all(coords, below, above, neighbours, weights, early, stacked, total, table, sums):
     few = BEADS - 8
     rows = 3 * few
 
@@ -321,10 +324,14 @@
         weight = weights[slots, at]
         for bead in range(8):
             rows_of = lambda x, k: row8(table[8 * x + bead : 8 * x + bead + 1, 128 * k : 128 * k + 128])
-            offset = [
-                looked_up([rows_of(x, k) for k in range(WINDOW)], lane, masks) - rows_of(x, 1 + a)
-                for x in range(3)
-            ]
+            offset = []
+            for x in range(3):
+                if bead < EARLY:
+                    out = jnp.where(index >> 7 == 0, lanes(rows_of(x, 0), lane), early[EARLY * x + bead, a, g])
+                    out = jnp.where(masks[-1], lanes(rows_of(x, WINDOW - 1), lane), out)
+                else:
+                    out = looked_up([rows_of(x, k) for k in range(WINDOW)], lane, masks)
+                offset.append(out - rows_of(x, 1 + a))
             squared = offset[0] * offset[0] + offset[1] * offset[1] + offset[2] * offset[2]
             w = weight * jnp.exp2(-LOG2E * squared)
             for x in range(3):
@@ -481,25 +488,37 @@
         up[8 * i : 8 * i + 8] = ghosts_of(chunk, ghost_rows[1:2])
 
 
-def kicked(coords, veloc, below, above, neighbours, weights, mine, scratch):
+def early_middle_kernel(coords, neighbours, early):
+    for a in range(CHUNKS):
+        for g in range(SLOTS // 8):
+            for x in range(3):
+                for i in range(EARLY):
+                    row = BEADS * x + BEADS - 8 + i
+                    early[EARLY * x + i, a, g] = own_lookup(
+                        lambda k: coords[row : row + 1, 128 * k : 128 * k + 128], neighbours, g, a
+                    )
+
+
+def kicked(coords, veloc, below, above, neighbours, weights, early, mine, scratch):
     total = scratch[1]
-    cheap_of_all(coords, below, above, neighbours, weights, *scratch)
+    cheap_of_all(coords, below, above, neighbours, weights, early, *scratch)
     return veloc[...] + inner_step * mine[6:7] / mine[7:8] * total[...]
 
 
 def middle_kernel(
-    coords, veloc, below, above, neighbours, weights, mine, ghost_rows, later, new_coords, new_veloc, down, up, *scratch
+    coords, veloc, below, above, neighbours, weights, early, mine, ghost_rows, later,
+    new_coords, new_veloc, down, up, *scratch,
 ):
-    velocities = kicked(coords, veloc, below, above, neighbours, weights, mine, scratch)
+    velocities = kicked(coords, veloc, below, above, neighbours, weights, early, mine, scratch)
     moved = propagated(coords[...], velocities, later)
     finish_step(moved, new_coords, new_veloc, ghost_rows, down, up)
 
 
 def last_kernel(
-    coords, veloc, below, above, neighbours, weights, mine, ghost_rows, last,
+    coords, veloc, below, above, neighbours, weights, early, mine, ghost_rows, last,
     own, contracted, down, up, rows, *scratch,
 ):
-    velocities = kicked(coords, veloc, below, above, neighbours, weights, mine, scratch)
+    velocities = kicked(coords, veloc, below, above, neighbours, weights, early, mine, scratch)
     moved = propagated(coords[...], velocities, last)
     for x in range(3):
         part = moved[:, ATOMS * x : ATOMS * (x + 1)]
@@ -518,13 +537,12 @@
         out[8:16] = ghosts_of(lambda k: rows[which, :, 128 * k : 128 * k + 128], index)
 
 
-def early_end_kernel(own, contracted, neighbours, early):
+def early_end_kernel(contracted, neighbours, early):
     for a in range(CHUNKS):
         for g in range(SLOTS // 8):
-            for i in range(15):
-                source, row = (contracted, i) if i < 12 else (own, i - 12)
+            for i in range(12):
                 early[i, a, g] = own_lookup(
-                    lambda k: source[row : row + 1, 128 * k : 128 * k + 128], neighbours, g, a
+                    lambda k: contracted[i : i + 1, 128 * k : 128 * k + 128], neighbours, g, a
                 )
 
 
@@ -540,7 +558,11 @@
 
     def looked_at(i, a, g):
         index = neighbours[8 * g : 8 * g + 8, 128 * a : 128 * a + 128]
-        return with_ghosts(early[i, a, g], below[i : i + 1], above[i : i + 1], index)
+        if i < 12:
+            out = early[i, a, g]
+        else:
+            out = own_lookup(lambda k: own[i - 12 : i - 11, 128 * k : 128 * k + 128], neighbours, g, a)
+        return with_ghosts(out, below[i : i + 1], above[i : i + 1], index)
 
     learned_by_lanes(
         lambda c, x, a, g: looked_at(4 * x + c, a, g),
@@ -647,24 +669,27 @@
         ],
         (gathered, neighbours, weights, mine, ghosts, w_in, w_out, first, reduce_),
     )
+    early = lambda coords: call(
+        early_middle_kernel, [(3 * EARLY, CHUNKS, SLOTS // 8, 8, 128)], [], (coords, neighbours), cost=cost
+    )[0]
     big = [((3 * 72 + 8, 512), bf16), ((96, ATOMS), f32), ((24, 768), f32), ((24, 8, ATOMS), f32)]
     below, above = exchange(down, up)
     coords, veloc, down, up = call(
         middle_kernel,
         [(96, ATOMS), (96, ATOMS), (96, 128), (96, 128)],
         big,
-        (coords, veloc, below, above, neighbours, weights, mine, ghosts, later),
+        (coords, veloc, below, above, neighbours, weights, early(coords), mine, ghosts, later),
     )
     below, above = exchange(down, up)
     own, contracted, down, up = call(
         last_kernel,
         [(8, ATOMS), (16, ATOMS), (16, 128), (16, 128)],
         [((2, 8, ATOMS), f32)] + big,
-        (coords, veloc, below, above, neighbours, weights, mine, ghosts, last),
+        (coords, veloc, below, above, neighbours, weights, early(coords), mine, ghosts, last),
     )
     below, above = exchange(down, up)
     (early,) = call(
-        early_end_kernel, [(15, CHUNKS, SLOTS // 8, 8, 128)], [], (own, contracted, neighbours), cost=cost
+        early_end_kernel, [(12, CHUNKS, SLOTS // 8, 8, 128)], [], (contracted, neighbours), cost=cost
     )
     new_pos, new_mom = call(
         end_kernel,

time: 71.9 us -> 71.6 us (level)
  waiting for transfers between devices: 14.2 us -> 11.6 us
  Pallas kernels: 19.8 us -> 22.2 us
    pallas_call x9 -> x11, Pallas kernels: 19.8 us -> 22.2 us  [call(): pl.pallas_call(kernel, out_shape=shapes, in_specs=specs, out_specs=[pl.Bl...]
    ppermute x4, waiting for transfers between devices: 1.9 us -> 0.01 us  [exchange(): below = lax.ppermute(up, RING, ring(1))]
    ppermute x4, waiting for transfers between devices: 12.3 us -> 11.5 us  [exchange(): above = lax.ppermute(down, RING, ring(-1))]
  transfers between devices with their start and end apart: 8 -> 8, of which waited for: 6 -> 4; matrix products, arithmetic and copies ran while one was open for 0% -> 0% of each run, Pallas kernels for 4% -> 7%
where the time goes in v8:
time: 71.6 us; the launch traced here: 71.5 us
  blocking collectives  28.7 us (40%)
  Pallas kernels  22.2 us (31%)
  waiting for transfers between devices  11.6 us (16%)
  starting transfers between devices  8.21 us (11%)
  between operations  0.77 us (1%)
    pallas_call x11, Pallas kernels, call(): pl.pallas_call(kernel, out_shape=shapes, in_specs=specs, out_specs=[pl.Bl...  22.2 us
    all_to_all x1, blocking collectives, body(): lax.all_to_all(block, 'bead', 0, 0, axis_index_groups=groups, tiled=True)  16 us
    all_gather x1, blocking collectives, body(): pair = lax.all_gather(mine, 'bead', axis=0, axis_index_groups=halves)  12.7 us
    ppermute x4, waiting for transfers between devices, exchange(): above = lax.ppermute(down, RING, ring(-1))  11.5 us
    ppermute x4, starting transfers between devices, exchange(): below = lax.ppermute(up, RING, ring(1))  7.2 us
  transfers between devices with their start and end apart: 8, of which 4 were waited for; matrix products, arithmetic and copies ran while one was open for 0% of the time, Pallas kernels for 7%

profile of v8, /device:TPU:97, one launch (start us, length us, event | category | flops | bytes accessed | tf_op | source)
XLA Modules:
  0.0 71.5 jit_solution(15594833400986153295)
XLA Ops:
  0.6 0.0 copy-start
  0.6 0.9 %shard_map.149 = (f32[8,512]{1,0:T(8,128)S(1)}, s32[2,128]{1,0:T(2,128)S(1)}, bf16[16,384]{1,0:T(8,128)(2,1)S(1)}, f32[8,128]{1,0:T(8,128)S(1)}) custom-call(f32[3,1,512]{2,1,0:T(1,128)} %bitcast.13, f32[3,1,512]{2,1,0:T(1,128)} %bitcast.14, s32[1,512]{1,0:T(1,128)} %bitcast.15, s32[2,128]{1,0:T(2,128)} %bitcast.16, f32[2]{0:T(128)} %scale.1, f32[2]{0:T(128)} %mass_table.1, ...), custom_call_target="tpu_custom_call" | custom-call | tf_op jit(solution)/shard_map/pallas_call | solution.py:588
  1.5 12.7 %all-gather = f32[16,512]{1,0:T(8,128)S(1)} all-gather(f32[8,512]{1,0:T(8,128)S(1)} %get-tuple-element.25.mine), channel_id=2, replica_groups={{0,64},{16,80},{32,96},{48,112},{128,192},{144,208},{160,224},{176,240}..., dimensions={0}, use_global_device_ids=true | all-gather | bytes 49152 | tf_op jit(solution)/shard_map/all_gather | solution.py:646
  14.3 0.1 shard_map.151
  14.3 3.9 %collective-permute-start = (f32[8,128]{1,0:T(8,128)S(1)}, f32[8,128]{1,0:T(8,128)S(1)}, u32[]{:S(2)}, u32[]{:S(2)}) collective-permute-start(f32[8,128]{1,0:T(8,128)S(1)} %get-tuple-element.27), channel_id=1, source_target_pairs={{0,1},{1,2},{2,3},{3,4},{4,5},{5,6},{6,7},{7,8},{8,9},{9,10},{10,1... | collective-permute-start | bytes 12296 | tf_op jit(solution)/shard_map/ppermute | solution.py:613
  18.2 0.0 collective-permute-start.1
  18.2 0.0 copy-done
  18.2 0.9 %shard_map.150.early = f32[7,4,4,8,128]{4,3,2,1,0:T(8,128)S(1)} custom-call(f32[2,8,512]{2,1,0:T(8,128)S(1)} %bitcast.9, s32[32,512]{1,0:T(8,128)S(1)} %copy-done), custom_call_target="tpu_custom_call" | custom-call | flops 1000000000 | bytes 1000000 | tf_op jit(solution)/shard_map/pallas_call | solution.py:588
  19.1 0.0 copy-start.1
  19.1 0.0 copy-start.3
  19.1 0.0 copy-start.4
  19.1 0.0 copy-start.5
  19.1 0.0 collective-permute-done.below
  19.2 3.3 %collective-permute-done.1.above = f32[8,128]{1,0:T(8,128)S(1)} collective-permute-done((f32[8,128]{1,0:T(8,128)S(1)}, f32[8,128]{1,0:T(8,128)S(1)}, u32[]{:S(2)}, u32[]{:S(2)}) %collective-permute-start.1) | collective-permute-done | bytes 4128 | tf_op jit(solution)/shard_map/ppermute | solution.py:614
  22.4 0.5 shard_map.152
  23.0 16.0 %all_to_all.5.gathered = f32[16,64,128]{2,1,0:T(8,128)S(1)} all-to-all(f32[16,64,128]{2,1,0:T(8,128)S(1)} %get-tuple-element.29), channel_id=1, replica_groups={{0,16,32,48,128,144,160,176,256,272,288,304,384,400,416,432},{64,80,96,..., dimensions={0} | all-to-all | bytes 1048576 | tf_op jit(solution)/shard_map/all_to_all | solution.py:659
  38.9 0.0 copy-done.1
  39.0 0.0 copy-done.3
  39.0 0.0 copy-done.4
  39.0 0.0 copy-done.5
  39.0 3.2 %shard_map.153 = (f32[96,512]{1,0:T(8,128)S(1)}, f32[96,512]{1,0:T(8,128)S(1)}, f32[96,128]{1,0:T(8,128)S(1)}, f32[96,128]{1,0:T(8,128)S(1)}) custom-call(f32[16,64,128]{2,1,0:T(8,128)S(1)} %all_to_all.5.gathered, s32[32,512]{1,0:T(8,128)S(1)} %copy-done, f32[32,512]{1,0:T(8,128)S(1)} %get-tuple-element.30.weights, f32[8,512]{1,0:T(8,128)S(1)} %get-tuple-element.25.mine, ...), custom_call_target="tpu_custom_call" | custom-call | tf_op jit(solution)/shard_map/pallas_call | solution.py:588
  42.1 3.3 %collective-permute-start.2 = (f32[96,128]{1,0:T(8,128)S(1)}, f32[96,128]{1,0:T(8,128)S(1)}, u32[]{:S(2)}, u32[]{:S(2)}) collective-permute-start(f32[96,128]{1,0:T(8,128)S(1)} %get-tuple-element.33), channel_id=1, source_target_pairs={{0,1},{1,2},{2,3},{3,4},{4,5},{5,6},{6,7},{7,8},{8,9},{9,10},{10,1... | collective-permute-start | bytes 147464 | tf_op jit(solution)/shard_map/ppermute | solution.py:613
  45.5 0.0 collective-permute-start.3
  45.5 0.0 copy-start.2
  45.5 1.5 %shard_map.154.early = f32[12,4,4,8,128]{4,3,2,1,0:T(8,128)S(1)} custom-call(f32[96,512]{1,0:T(8,128)S(1)} %get-tuple-element.31.coords, s32[32,512]{1,0:T(8,128)S(1)} %copy-done), custom_call_target="tpu_custom_call" | custom-call | flops 1000000000 | bytes 1000000 | tf_op jit(solution)/shard_map/pallas_call | solution.py:588
  47.0 0.0 collective-permute-done.2.below
  47.0 3.2 %collective-permute-done.3.above = f32[96,128]{1,0:T(8,128)S(1)} collective-permute-done((f32[96,128]{1,0:T(8,128)S(1)}, f32[96,128]{1,0:T(8,128)S(1)}, u32[]{:S(2)}, u32[]{:S(2)}) %collective-permute-start.3) | collective-permute-done | bytes 49184 | tf_op jit(solution)/shard_map/ppermute | solution.py:614
  50.2 0.0 copy-done.2
  50.2 5.0 %shard_map.155 = (f32[96,512]{1,0:T(8,128)S(1)}, f32[96,512]{1,0:T(8,128)S(1)}, f32[96,128]{1,0:T(8,128)S(1)}, f32[96,128]{1,0:T(8,128)S(1)}) custom-call(f32[96,512]{1,0:T(8,128)S(1)} %get-tuple-element.31.coords, f32[96,512]{1,0:T(8,128)S(1)} %get-tuple-element.32.veloc, f32[96,128]{1,0:T(8,128)S(1)} %collective-permute-done.2.below, ...), custom_call_target="tpu_custom_call" | custom-call | tf_op jit(solution)/shard_map/pallas_call | solution.py:588
  55.2 0.0 collective-permute-start.4
  55.2 0.5 collective-permute-start.5
  55.7 1.5 %shard_map.156.early = f32[12,4,4,8,128]{4,3,2,1,0:T(8,128)S(1)} custom-call(f32[96,512]{1,0:T(8,128)S(1)} %get-tuple-element.35.coords, s32[32,512]{1,0:T(8,128)S(1)} %copy-done), custom_call_target="tpu_custom_call" | custom-call | flops 1000000000 | bytes 1000000 | tf_op jit(solution)/shard_map/pallas_call | solution.py:588
  57.2 0.0 collective-permute-done.4.below
  57.2 2.7 %collective-permute-done.5.above = f32[96,128]{1,0:T(8,128)S(1)} collective-permute-done((f32[96,128]{1,0:T(8,128)S(1)}, f32[96,128]{1,0:T(8,128)S(1)}, u32[]{:S(2)}, u32[]{:S(2)}) %collective-permute-start.5) | collective-permute-done | bytes 49184 | tf_op jit(solution)/shard_map/ppermute | solution.py:614
  60.0 5.0 %shard_map.157 = (f32[8,512]{1,0:T(8,128)S(1)}, f32[16,512]{1,0:T(8,128)S(1)}, f32[16,128]{1,0:T(8,128)S(1)}, f32[16,128]{1,0:T(8,128)S(1)}) custom-call(f32[96,512]{1,0:T(8,128)S(1)} %get-tuple-element.35.coords, f32[96,512]{1,0:T(8,128)S(1)} %get-tuple-element.36.veloc, f32[96,128]{1,0:T(8,128)S(1)} %collective-permute-done.4.below, ...), custom_call_target="tpu_custom_call" | custom-call | tf_op jit(solution)/shard_map/pallas_call | solution.py:588
  65.0 0.0 collective-permute-start.6
  65.0 0.5 collective-permute-start.7
  65.5 1.5 %shard_map.158.early = f32[12,4,4,8,128]{4,3,2,1,0:T(8,128)S(1)} custom-call(f32[16,512]{1,0:T(8,128)S(1)} %get-tuple-element.41.contracted, s32[32,512]{1,0:T(8,128)S(1)} %copy-done), custom_call_target="tpu_custom_call" | custom-call | flops 1000000000 | bytes 1000000 | tf_op jit(solution)/shard_map/pallas_call | solution.py:588
  67.0 0.0 collective-permute-done.6.below
  67.0 2.3 %collective-permute-done.7.above = f32[16,128]{1,0:T(8,128)S(1)} collective-permute-done((f32[16,128]{1,0:T(8,128)S(1)}, f32[16,128]{1,0:T(8,128)S(1)}, u32[]{:S(2)}, u32[]{:S(2)}) %collective-permute-start.7) | collective-permute-done | bytes 8224 | tf_op jit(solution)/shard_map/ppermute | solution.py:614
  69.3 2.2 %shard_map.159 = (f32[3,1,512]{2,1,0:T(1,128)}, f32[3,1,512]{2,1,0:T(1,128)}) custom-call(f32[8,128]{1,0:T(8,128)S(1)} %get-tuple-element.24.gains, f32[8,512]{1,0:T(8,128)S(1)} %get-tuple-element.40.own, f32[16,512]{1,0:T(8,128)S(1)} %get-tuple-element.41.contracted, f32[12,4,4,8,128]{4,3,2,1,0:T(8,128)S(1)} %shard_map.158.early, ...), custom_call_target="tpu_custom_call" | custom-call | tf_op jit(solution)/shard_map/pallas_call | solution.py:588
Async XLA Ops:
  0.6 17.6 %copy-start = (s32[32,512]{1,0:T(8,128)S(1)}, s32[32,512]{1,0:T(8,128)}, u32[]{:S(2)}) copy-start(s32[32,512]{1,0:T(8,128)} %neighbours.17) | copy-start | bytes 196612
  14.3 4.8 %collective-permute-start = (f32[8,128]{1,0:T(8,128)S(1)}, f32[8,128]{1,0:T(8,128)S(1)}, u32[]{:S(2)}, u32[]{:S(2)}) collective-permute-start(f32[8,128]{1,0:T(8,128)S(1)} %get-tuple-element.27), channel_id=1, source_target_pairs={{0,1},{1,2},{2,3},{3,4},{4,5},{5,6},{6,7},{7,8},{8,9},{9,10},{10,1... | collective-permute-start | bytes 12296 | tf_op jit(solution)/shard_map/ppermute | solution.py:613
  18.2 4.2 %collective-permute-start.1 = (f32[8,128]{1,0:T(8,128)S(1)}, f32[8,128]{1,0:T(8,128)S(1)}, u32[]{:S(2)}, u32[]{:S(2)}) collective-permute-start(f32[8,128]{1,0:T(8,128)S(1)} %get-tuple-element.28), channel_id=1, source_target_pairs={{0,79},{1,0},{2,1},{3,2},{4,3},{5,4},{6,5},{7,6},{8,7},{9,8},{10,9... | collective-permute-start | bytes 12296 | tf_op jit(solution)/shard_map/ppermute | solution.py:614
  19.1 19.9 %copy-start.1 = (bf16[64,480]{1,0:T(8,128)(2,1)S(1)}, bf16[64,480]{1,0:T(8,128)(2,1)}, u32[]{:S(2)}) copy-start(bf16[64,480]{1,0:T(8,128)(2,1)} %constant.10.clone.first) | copy-start | bytes 184324
  19.1 19.8 %copy-start.3 = (f32[128,8]{0,1:T(8,128)S(1)}, f32[128,8]{0,1:T(8,128)}, u32[]{:S(2)}) copy-start(f32[128,8]{0,1:T(8,128)} %param.21) | copy-start | bytes 12292
  19.1 19.8 %copy-start.4 = (f32[8,128]{1,0:T(8,128)S(1)}, f32[8,128]{1,0:T(8,128)}, u32[]{:S(2)}) copy-start(f32[8,128]{1,0:T(8,128)} %w_out.3) | copy-start | bytes 12292
  19.1 19.8 %copy-start.5 = (bf16[16,96]{1,0:T(8,128)(2,1)S(1)}, bf16[16,96]{1,0:T(8,128)(2,1)}, u32[]{:S(2)}) copy-start(bf16[16,96]{1,0:T(8,128)(2,1)} %constant.13.clone.reduce_) | copy-start | bytes 9220
  42.1 4.8 %collective-permute-start.2 = (f32[96,128]{1,0:T(8,128)S(1)}, f32[96,128]{1,0:T(8,128)S(1)}, u32[]{:S(2)}, u32[]{:S(2)}) collective-permute-start(f32[96,128]{1,0:T(8,128)S(1)} %get-tuple-element.33), channel_id=1, source_target_pairs={{0,1},{1,2},{2,3},{3,4},{4,5},{5,6},{6,7},{7,8},{8,9},{9,10},{10,1... | collective-permute-start | bytes 147464 | tf_op jit(solution)/shard_map/ppermute | solution.py:613
  45.5 4.7 %collective-permute-start.3 = (f32[96,128]{1,0:T(8,128)S(1)}, f32[96,128]{1,0:T(8,128)S(1)}, u32[]{:S(2)}, u32[]{:S(2)}) collective-permute-start(f32[96,128]{1,0:T(8,128)S(1)} %get-tuple-element.34), channel_id=1, source_target_pairs={{0,79},{1,0},{2,1},{3,2},{4,3},{5,4},{6,5},{7,6},{8,7},{9,8},{10,9... | collective-permute-start | bytes 147464 | tf_op jit(solution)/shard_map/ppermute | solution.py:614
  45.5 4.7 %copy-start.2 = (bf16[64,384]{1,0:T(8,128)(2,1)S(1)}, bf16[64,384]{1,0:T(8,128)(2,1)}, u32[]{:S(2)}) copy-start(bf16[64,384]{1,0:T(8,128)(2,1)} %constant.11.clone.later) | copy-start | bytes 147460
  55.2 2.0 %collective-permute-start.4 = (f32[96,128]{1,0:T(8,128)S(1)}, f32[96,128]{1,0:T(8,128)S(1)}, u32[]{:S(2)}, u32[]{:S(2)}) collective-permute-start(f32[96,128]{1,0:T(8,128)S(1)} %get-tuple-element.37), channel_id=1, source_target_pairs={{0,1},{1,2},{2,3},{3,4},{4,5},{5,6},{6,7},{7,8},{8,9},{9,10},{10,1... | collective-permute-start | bytes 147464 | tf_op jit(solution)/shard_map/ppermute | solution.py:613
  55.2 4.7 %collective-permute-start.5 = (f32[96,128]{1,0:T(8,128)S(1)}, f32[96,128]{1,0:T(8,128)S(1)}, u32[]{:S(2)}, u32[]{:S(2)}) collective-permute-start(f32[96,128]{1,0:T(8,128)S(1)} %get-tuple-element.38), channel_id=1, source_target_pairs={{0,79},{1,0},{2,1},{3,2},{4,3},{5,4},{6,5},{7,6},{8,7},{9,8},{10,9... | collective-permute-start | bytes 147464 | tf_op jit(solution)/shard_map/ppermute | solution.py:614
  65.0 2.0 %collective-permute-start.6 = (f32[16,128]{1,0:T(8,128)S(1)}, f32[16,128]{1,0:T(8,128)S(1)}, u32[]{:S(2)}, u32[]{:S(2)}) collective-permute-start(f32[16,128]{1,0:T(8,128)S(1)} %get-tuple-element.42), channel_id=1, source_target_pairs={{0,1},{1,2},{2,3},{3,4},{4,5},{5,6},{6,7},{7,8},{8,9},{9,10},{10,1... | collective-permute-start | bytes 24584 | tf_op jit(solution)/shard_map/ppermute | solution.py:613
  65.0 4.3 %collective-permute-start.7 = (f32[16,128]{1,0:T(8,128)S(1)}, f32[16,128]{1,0:T(8,128)S(1)}, u32[]{:S(2)}, u32[]{:S(2)}) collective-permute-start(f32[16,128]{1,0:T(8,128)S(1)} %get-tuple-element.43), channel_id=1, source_target_pairs={{0,79},{1,0},{2,1},{3,2},{4,3},{5,4},{6,5},{7,6},{8,7},{9,8},{10,9... | collective-permute-start | bytes 24584 | tf_op jit(solution)/shard_map/ppermute | solution.py:614

commit v9 on v8

--- a/solution.py
+++ b/solution.py
@@ -267,42 +267,46 @@
 EARLY = 4
 
 
-def cheap_of_all(coords, below, above, neighbours, weights, early, stacked, total, table, sums):
+def cheap_of_all(coords, below, above, neighbours, weights, early, stacked, total, table, sums, stacked_less):
     few = BEADS - 8
-    rows = 3 * few
-
-    def of_few(value):
-        return jnp.concatenate([value[BEADS * x : BEADS * x + few] for x in range(3)], axis=0)
-
-    own, low, high_ = of_few(coords), of_few(below), of_few(above)
-    stack = jnp.concatenate(
-        [
+    fewer = BEADS - 16
+
+    def prepared(count, target):
+        def of_few(value):
+            return jnp.concatenate([value[BEADS * x : BEADS * x + count] for x in range(3)], axis=0)
+
+        own, low, high_ = of_few(coords), of_few(below), of_few(above)
+        parts = [
             jnp.concatenate([low, own[:, 0:128]], axis=1),
             own[:, 128:384],
             jnp.concatenate([own[:, 384:512], high_], axis=1),
-            jnp.zeros((8, 256), f32),
-        ],
-        axis=0,
-    )
-    high = stack.astype(bf16)
-    stacked[:, 0:256] = high
-    stacked[:, 256:512] = (stack - high.astype(f32)).astype(bf16)
-    rounded = own.astype(bf16).astype(f32)
-    rounded = rounded + (own - rounded).astype(bf16).astype(f32)
+        ]
+        spare = target.shape[0] - 9 * count
+        if spare:
+            parts.append(jnp.zeros((spare, 256), f32))
+        stack = jnp.concatenate(parts, axis=0)
+        high = stack.astype(bf16)
+        target[:, 0:256] = high
+        target[:, 256:512] = (stack - high.astype(f32)).astype(bf16)
+        rounded = own.astype(bf16).astype(f32)
+        return rounded + (own - rounded).astype(bf16).astype(f32)
+
+    rounded_few, rounded_fewer = prepared(few, stacked), prepared(fewer, stacked_less)
     for x in range(3):
-        at = slice(BEADS * x + few, BEADS * (x + 1))
-        table[8 * x : 8 * x + 8, 0:128] = below[at]
-        table[8 * x : 8 * x + 8, 128:640] = coords[at]
-        table[8 * x : 8 * x + 8, 640:768] = above[at]
+        at = slice(BEADS * x + fewer, BEADS * (x + 1))
+        table[16 * x : 16 * x + 16, 0:128] = below[at]
+        table[16 * x : 16 * x + 16, 128:640] = coords[at]
+        table[16 * x : 16 * x + 16, 640:768] = above[at]
     total[...] = jnp.zeros_like(total)
     sums[...] = jnp.zeros_like(sums)
     place = lax.broadcasted_iota(jnp.int16, (256, ATOMS), 0)
 
-    def by_matmul(slot):
+    def by_matmul(slot, count, matrix, rounded):
+        rows = 3 * count
         index = neighbours[slot : slot + 1, :]
         column = jnp.broadcast_to(index & 255, (16, ATOMS)).astype(jnp.int16)
         chosen = jnp.where(place == jnp.tile(column, (16, 1)), bf16(1), bf16(0))
-        picked = jnp.dot(stacked[...], jnp.concatenate([chosen, chosen], axis=0), preferred_element_type=f32)
+        picked = jnp.dot(matrix[...], jnp.concatenate([chosen, chosen], axis=0), preferred_element_type=f32)
         part = index >> 8
         other = jnp.where(
             part == 0,
@@ -310,24 +314,24 @@
             jnp.where(part == 1, picked[rows : 2 * rows], picked[2 * rows : 3 * rows]),
         )
         offset = other - rounded
-        x, y, z = offset[0:few], offset[few : 2 * few], offset[2 * few :]
+        x, y, z = offset[0:count], offset[count : 2 * count], offset[2 * count :]
         w = weights[slot : slot + 1, :] * jnp.exp2(-LOG2E * (x * x + y * y + z * z))
-        total[0:few] += w * x
-        total[BEADS : BEADS + few] += w * y
-        total[2 * BEADS : 2 * BEADS + few] += w * z
-
-    def by_lanes(g, a):
+        total[0:count] += w * x
+        total[BEADS : BEADS + count] += w * y
+        total[2 * BEADS : 2 * BEADS + count] += w * z
+
+    def by_lanes(g, a, beads):
         at = slice(128 * a, 128 * a + 128)
         slots = slice(8 * g, 8 * g + 8)
         index = neighbours[slots, at]
         lane, masks = index & 127, [(index >> 7) == k for k in range(1, WINDOW)]
         weight = weights[slots, at]
-        for bead in range(8):
-            rows_of = lambda x, k: row8(table[8 * x + bead : 8 * x + bead + 1, 128 * k : 128 * k + 128])
+        for bead in beads:
+            rows_of = lambda x, k: row8(table[16 * x + bead : 16 * x + bead + 1, 128 * k : 128 * k + 128])
             offset = []
             for x in range(3):
-                if bead < EARLY:
-                    out = jnp.where(index >> 7 == 0, lanes(rows_of(x, 0), lane), early[EARLY * x + bead, a, g])
+                if 8 <= bead < 8 + EARLY:
+                    out = jnp.where(index >> 7 == 0, lanes(rows_of(x, 0), lane), early[EARLY * x + bead - 8, a, g])
                     out = jnp.where(masks[-1], lanes(rows_of(x, WINDOW - 1), lane), out)
                 else:
                     out = looked_up([rows_of(x, k) for k in range(WINDOW)], lane, masks)
@@ -335,17 +339,21 @@
             squared = offset[0] * offset[0] + offset[1] * offset[1] + offset[2] * offset[2]
             w = weight * jnp.exp2(-LOG2E * squared)
             for x in range(3):
-                sums[8 * x + bead, :, at] += w * offset[x]
+                sums[16 * x + bead, :, at] += w * offset[x]
 
     for g in range(SLOTS // 8):
+        less = g == SLOTS // 8 - 1
         for j in range(8):
-            by_matmul(g * 8 + j)
+            if less:
+                by_matmul(g * 8 + j, fewer, stacked_less, rounded_fewer)
+            else:
+                by_matmul(g * 8 + j, few, stacked, rounded_few)
             if j % 2:
-                by_lanes(g, j // 2)
+                by_lanes(g, j // 2, range(0 if less else 8, 16))
     for x in range(3):
-        for bead in range(8):
-            row = BEADS * x + few + bead
-            total[row : row + 1] = jnp.sum(sums[8 * x + bead], axis=0, keepdims=True)
+        for bead in range(16):
+            row = BEADS * x + fewer + bead
+            total[row : row + 1] += jnp.sum(sums[16 * x + bead], axis=0, keepdims=True)
 
 
 def propagated(coords, veloc, table, extra=None):
@@ -672,7 +680,7 @@
     early = lambda coords: call(
         early_middle_kernel, [(3 * EARLY, CHUNKS, SLOTS // 8, 8, 128)], [], (coords, neighbours), cost=cost
     )[0]
-    big = [((3 * 72 + 8, 512), bf16), ((96, ATOMS), f32), ((24, 768), f32), ((24, 8, ATOMS), f32)]
+    big = [((3 * 72 + 8, 512), bf16), ((96, ATOMS), f32), ((48, 768), f32), ((48, 8, ATOMS), f32), ((144, 512), bf16)]
     below, above = exchange(down, up)
     coords, veloc, down, up = call(
         middle_kernel,

time: 71.6 us -> 71.1 us (level)
  transfers between devices with their start and end apart: 8 -> 8, of which waited for: 4 -> 4; matrix products, arithmetic and copies ran while one was open for 0% -> 0% of each run, Pallas kernels for 7% -> 8%
where the time goes in v9:
time: 71.1 us; the launch traced here: 70.9 us
  blocking collectives  28.7 us (40%)
  Pallas kernels  21.6 us (30%)
  waiting for transfers between devices  11.6 us (16%)
  starting transfers between devices  8.21 us (12%)
  between operations  0.77 us (1%)
    pallas_call x11, Pallas kernels, call(): pl.pallas_call(kernel, out_shape=shapes, in_specs=specs, out_specs=[pl.Bl...  21.6 us
    all_to_all x1, blocking collectives, body(): lax.all_to_all(block, 'bead', 0, 0, axis_index_groups=groups, tiled=True)  16 us
    all_gather x1, blocking collectives, body(): pair = lax.all_gather(mine, 'bead', axis=0, axis_index_groups=halves)  12.7 us
    ppermute x4, waiting for transfers between devices, exchange(): above = lax.ppermute(down, RING, ring(-1))  11.5 us
    ppermute x4, starting transfers between devices, exchange(): below = lax.ppermute(up, RING, ring(1))  7.2 us
  transfers between devices with their start and end apart: 8, of which 4 were waited for; matrix products, arithmetic and copies ran while one was open for 0% of the time, Pallas kernels for 8%

profile of v9, /device:TPU:97, one launch (start us, length us, event | category | flops | bytes accessed | tf_op | source)
XLA Modules:
  0.0 70.9 jit_solution(993948972465273747)
XLA Ops:
  0.6 0.0 copy-start
  0.6 0.9 %shard_map.149 = (f32[8,512]{1,0:T(8,128)S(1)}, s32[2,128]{1,0:T(2,128)S(1)}, bf16[16,384]{1,0:T(8,128)(2,1)S(1)}, f32[8,128]{1,0:T(8,128)S(1)}) custom-call(f32[3,1,512]{2,1,0:T(1,128)} %bitcast.13, f32[3,1,512]{2,1,0:T(1,128)} %bitcast.14, s32[1,512]{1,0:T(1,128)} %bitcast.15, s32[2,128]{1,0:T(2,128)} %bitcast.16, f32[2]{0:T(128)} %scale.1, f32[2]{0:T(128)} %mass_table.1, ...), custom_call_target="tpu_custom_call" | custom-call | tf_op jit(solution)/shard_map/pallas_call | solution.py:596
  1.5 12.7 %all-gather = f32[16,512]{1,0:T(8,128)S(1)} all-gather(f32[8,512]{1,0:T(8,128)S(1)} %get-tuple-element.25.mine), channel_id=2, replica_groups={{0,64},{16,80},{32,96},{48,112},{128,192},{144,208},{160,224},{176,240}..., dimensions={0}, use_global_device_ids=true | all-gather | bytes 49152 | tf_op jit(solution)/shard_map/all_gather | solution.py:654
  14.3 0.1 shard_map.151
  14.3 3.9 %collective-permute-start = (f32[8,128]{1,0:T(8,128)S(1)}, f32[8,128]{1,0:T(8,128)S(1)}, u32[]{:S(2)}, u32[]{:S(2)}) collective-permute-start(f32[8,128]{1,0:T(8,128)S(1)} %get-tuple-element.27), channel_id=1, source_target_pairs={{0,1},{1,2},{2,3},{3,4},{4,5},{5,6},{6,7},{7,8},{8,9},{9,10},{10,1... | collective-permute-start | bytes 12296 | tf_op jit(solution)/shard_map/ppermute | solution.py:621
  18.2 0.0 collective-permute-start.1
  18.2 0.0 copy-done
  18.2 0.9 %shard_map.150.early = f32[7,4,4,8,128]{4,3,2,1,0:T(8,128)S(1)} custom-call(f32[2,8,512]{2,1,0:T(8,128)S(1)} %bitcast.9, s32[32,512]{1,0:T(8,128)S(1)} %copy-done), custom_call_target="tpu_custom_call" | custom-call | flops 1000000000 | bytes 1000000 | tf_op jit(solution)/shard_map/pallas_call | solution.py:596
  19.1 0.0 copy-start.1
  19.1 0.0 copy-start.3
  19.1 0.0 copy-start.4
  19.1 0.0 copy-start.5
  19.1 0.0 collective-permute-done.below
  19.2 3.3 %collective-permute-done.1.above = f32[8,128]{1,0:T(8,128)S(1)} collective-permute-done((f32[8,128]{1,0:T(8,128)S(1)}, f32[8,128]{1,0:T(8,128)S(1)}, u32[]{:S(2)}, u32[]{:S(2)}) %collective-permute-start.1) | collective-permute-done | bytes 4128 | tf_op jit(solution)/shard_map/ppermute | solution.py:622
  22.4 0.5 shard_map.152
  23.0 16.0 %all_to_all.5.gathered = f32[16,64,128]{2,1,0:T(8,128)S(1)} all-to-all(f32[16,64,128]{2,1,0:T(8,128)S(1)} %get-tuple-element.29), channel_id=1, replica_groups={{0,16,32,48,128,144,160,176,256,272,288,304,384,400,416,432},{64,80,96,..., dimensions={0} | all-to-all | bytes 1048576 | tf_op jit(solution)/shard_map/all_to_all | solution.py:667
  38.9 0.0 copy-done.1
  39.0 0.0 copy-done.3
  39.0 0.0 copy-done.4
  39.0 0.0 copy-done.5
  39.0 3.2 %shard_map.153 = (f32[96,512]{1,0:T(8,128)S(1)}, f32[96,512]{1,0:T(8,128)S(1)}, f32[96,128]{1,0:T(8,128)S(1)}, f32[96,128]{1,0:T(8,128)S(1)}) custom-call(f32[16,64,128]{2,1,0:T(8,128)S(1)} %all_to_all.5.gathered, s32[32,512]{1,0:T(8,128)S(1)} %copy-done, f32[32,512]{1,0:T(8,128)S(1)} %get-tuple-element.30.weights, f32[8,512]{1,0:T(8,128)S(1)} %get-tuple-element.25.mine, ...), custom_call_target="tpu_custom_call" | custom-call | tf_op jit(solution)/shard_map/pallas_call | solution.py:596
  42.1 3.3 %collective-permute-start.2 = (f32[96,128]{1,0:T(8,128)S(1)}, f32[96,128]{1,0:T(8,128)S(1)}, u32[]{:S(2)}, u32[]{:S(2)}) collective-permute-start(f32[96,128]{1,0:T(8,128)S(1)} %get-tuple-element.33), channel_id=1, source_target_pairs={{0,1},{1,2},{2,3},{3,4},{4,5},{5,6},{6,7},{7,8},{8,9},{9,10},{10,1... | collective-permute-start | bytes 147464 | tf_op jit(solution)/shard_map/ppermute | solution.py:621
  45.5 0.0 collective-permute-start.3
  45.5 0.0 copy-start.2
  45.5 1.5 %shard_map.154.early = f32[12,4,4,8,128]{4,3,2,1,0:T(8,128)S(1)} custom-call(f32[96,512]{1,0:T(8,128)S(1)} %get-tuple-element.31.coords, s32[32,512]{1,0:T(8,128)S(1)} %copy-done), custom_call_target="tpu_custom_call" | custom-call | flops 1000000000 | bytes 1000000 | tf_op jit(solution)/shard_map/pallas_call | solution.py:596
  47.0 0.0 collective-permute-done.2.below
  47.0 3.2 %collective-permute-done.3.above = f32[96,128]{1,0:T(8,128)S(1)} collective-permute-done((f32[96,128]{1,0:T(8,128)S(1)}, f32[96,128]{1,0:T(8,128)S(1)}, u32[]{:S(2)}, u32[]{:S(2)}) %collective-permute-start.3) | collective-permute-done | bytes 49184 | tf_op jit(solution)/shard_map/ppermute | solution.py:622
  50.2 0.0 copy-done.2
  50.2 4.7 %shard_map.155 = (f32[96,512]{1,0:T(8,128)S(1)}, f32[96,512]{1,0:T(8,128)S(1)}, f32[96,128]{1,0:T(8,128)S(1)}, f32[96,128]{1,0:T(8,128)S(1)}) custom-call(f32[96,512]{1,0:T(8,128)S(1)} %get-tuple-element.31.coords, f32[96,512]{1,0:T(8,128)S(1)} %get-tuple-element.32.veloc, f32[96,128]{1,0:T(8,128)S(1)} %collective-permute-done.2.below, ...), custom_call_target="tpu_custom_call" | custom-call | tf_op jit(solution)/shard_map/pallas_call | solution.py:596
  54.9 0.0 collective-permute-start.4
  54.9 0.5 collective-permute-start.5
  55.4 1.5 %shard_map.156.early = f32[12,4,4,8,128]{4,3,2,1,0:T(8,128)S(1)} custom-call(f32[96,512]{1,0:T(8,128)S(1)} %get-tuple-element.35.coords, s32[32,512]{1,0:T(8,128)S(1)} %copy-done), custom_call_target="tpu_custom_call" | custom-call | flops 1000000000 | bytes 1000000 | tf_op jit(solution)/shard_map/pallas_call | solution.py:596
  56.9 0.0 collective-permute-done.4.below
  56.9 2.7 %collective-permute-done.5.above = f32[96,128]{1,0:T(8,128)S(1)} collective-permute-done((f32[96,128]{1,0:T(8,128)S(1)}, f32[96,128]{1,0:T(8,128)S(1)}, u32[]{:S(2)}, u32[]{:S(2)}) %collective-permute-start.5) | collective-permute-done | bytes 49184 | tf_op jit(solution)/shard_map/ppermute | solution.py:622
  59.7 4.7 %shard_map.157 = (f32[8,512]{1,0:T(8,128)S(1)}, f32[16,512]{1,0:T(8,128)S(1)}, f32[16,128]{1,0:T(8,128)S(1)}, f32[16,128]{1,0:T(8,128)S(1)}) custom-call(f32[96,512]{1,0:T(8,128)S(1)} %get-tuple-element.35.coords, f32[96,512]{1,0:T(8,128)S(1)} %get-tuple-element.36.veloc, f32[96,128]{1,0:T(8,128)S(1)} %collective-permute-done.4.below, ...), custom_call_target="tpu_custom_call" | custom-call | tf_op jit(solution)/shard_map/pallas_call | solution.py:596
  64.4 0.0 collective-permute-start.6
  64.4 0.5 collective-permute-start.7
  64.9 1.5 %shard_map.158.early = f32[12,4,4,8,128]{4,3,2,1,0:T(8,128)S(1)} custom-call(f32[16,512]{1,0:T(8,128)S(1)} %get-tuple-element.41.contracted, s32[32,512]{1,0:T(8,128)S(1)} %copy-done), custom_call_target="tpu_custom_call" | custom-call | flops 1000000000 | bytes 1000000 | tf_op jit(solution)/shard_map/pallas_call | solution.py:596
  66.4 0.0 collective-permute-done.6.below
  66.4 2.3 %collective-permute-done.7.above = f32[16,128]{1,0:T(8,128)S(1)} collective-permute-done((f32[16,128]{1,0:T(8,128)S(1)}, f32[16,128]{1,0:T(8,128)S(1)}, u32[]{:S(2)}, u32[]{:S(2)}) %collective-permute-start.7) | collective-permute-done | bytes 8224 | tf_op jit(solution)/shard_map/ppermute | solution.py:622
  68.7 2.2 %shard_map.159 = (f32[3,1,512]{2,1,0:T(1,128)}, f32[3,1,512]{2,1,0:T(1,128)}) custom-call(f32[8,128]{1,0:T(8,128)S(1)} %get-tuple-element.24.gains, f32[8,512]{1,0:T(8,128)S(1)} %get-tuple-element.40.own, f32[16,512]{1,0:T(8,128)S(1)} %get-tuple-element.41.contracted, f32[12,4,4,8,128]{4,3,2,1,0:T(8,128)S(1)} %shard_map.158.early, ...), custom_call_target="tpu_custom_call" | custom-call | tf_op jit(solution)/shard_map/pallas_call | solution.py:596
Async XLA Ops:
  0.6 17.6 %copy-start = (s32[32,512]{1,0:T(8,128)S(1)}, s32[32,512]{1,0:T(8,128)}, u32[]{:S(2)}) copy-start(s32[32,512]{1,0:T(8,128)} %neighbours.17) | copy-start | bytes 196612
  14.3 4.8 %collective-permute-start = (f32[8,128]{1,0:T(8,128)S(1)}, f32[8,128]{1,0:T(8,128)S(1)}, u32[]{:S(2)}, u32[]{:S(2)}) collective-permute-start(f32[8,128]{1,0:T(8,128)S(1)} %get-tuple-element.27), channel_id=1, source_target_pairs={{0,1},{1,2},{2,3},{3,4},{4,5},{5,6},{6,7},{7,8},{8,9},{9,10},{10,1... | collective-permute-start | bytes 12296 | tf_op jit(solution)/shard_map/ppermute | solution.py:621
  18.2 4.2 %collective-permute-start.1 = (f32[8,128]{1,0:T(8,128)S(1)}, f32[8,128]{1,0:T(8,128)S(1)}, u32[]{:S(2)}, u32[]{:S(2)}) collective-permute-start(f32[8,128]{1,0:T(8,128)S(1)} %get-tuple-element.28), channel_id=1, source_target_pairs={{0,79},{1,0},{2,1},{3,2},{4,3},{5,4},{6,5},{7,6},{8,7},{9,8},{10,9... | collective-permute-start | bytes 12296 | tf_op jit(solution)/shard_map/ppermute | solution.py:622
  19.1 19.9 %copy-start.1 = (bf16[64,480]{1,0:T(8,128)(2,1)S(1)}, bf16[64,480]{1,0:T(8,128)(2,1)}, u32[]{:S(2)}) copy-start(bf16[64,480]{1,0:T(8,128)(2,1)} %constant.10.clone.first) | copy-start | bytes 184324
  19.1 19.8 %copy-start.3 = (f32[128,8]{0,1:T(8,128)S(1)}, f32[128,8]{0,1:T(8,128)}, u32[]{:S(2)}) copy-start(f32[128,8]{0,1:T(8,128)} %param.21) | copy-start | bytes 12292
  19.1 19.8 %copy-start.4 = (f32[8,128]{1,0:T(8,128)S(1)}, f32[8,128]{1,0:T(8,128)}, u32[]{:S(2)}) copy-start(f32[8,128]{1,0:T(8,128)} %w_out.3) | copy-start | bytes 12292
  19.1 19.8 %copy-start.5 = (bf16[16,96]{1,0:T(8,128)(2,1)S(1)}, bf16[16,96]{1,0:T(8,128)(2,1)}, u32[]{:S(2)}) copy-start(bf16[16,96]{1,0:T(8,128)(2,1)} %constant.13.clone.reduce_) | copy-start | bytes 9220
  42.1 4.8 %collective-permute-start.2 = (f32[96,128]{1,0:T(8,128)S(1)}, f32[96,128]{1,0:T(8,128)S(1)}, u32[]{:S(2)}, u32[]{:S(2)}) collective-permute-start(f32[96,128]{1,0:T(8,128)S(1)} %get-tuple-element.33), channel_id=1, source_target_pairs={{0,1},{1,2},{2,3},{3,4},{4,5},{5,6},{6,7},{7,8},{8,9},{9,10},{10,1... | collective-permute-start | bytes 147464 | tf_op jit(solution)/shard_map/ppermute | solution.py:621
  45.5 4.7 %collective-permute-start.3 = (f32[96,128]{1,0:T(8,128)S(1)}, f32[96,128]{1,0:T(8,128)S(1)}, u32[]{:S(2)}, u32[]{:S(2)}) collective-permute-start(f32[96,128]{1,0:T(8,128)S(1)} %get-tuple-element.34), channel_id=1, source_target_pairs={{0,79},{1,0},{2,1},{3,2},{4,3},{5,4},{6,5},{7,6},{8,7},{9,8},{10,9... | collective-permute-start | bytes 147464 | tf_op jit(solution)/shard_map/ppermute | solution.py:622
  45.5 4.7 %copy-start.2 = (bf16[64,384]{1,0:T(8,128)(2,1)S(1)}, bf16[64,384]{1,0:T(8,128)(2,1)}, u32[]{:S(2)}) copy-start(bf16[64,384]{1,0:T(8,128)(2,1)} %constant.11.clone.later) | copy-start | bytes 147460
  54.9 2.0 %collective-permute-start.4 = (f32[96,128]{1,0:T(8,128)S(1)}, f32[96,128]{1,0:T(8,128)S(1)}, u32[]{:S(2)}, u32[]{:S(2)}) collective-permute-start(f32[96,128]{1,0:T(8,128)S(1)} %get-tuple-element.37), channel_id=1, source_target_pairs={{0,1},{1,2},{2,3},{3,4},{4,5},{5,6},{6,7},{7,8},{8,9},{9,10},{10,1... | collective-permute-start | bytes 147464 | tf_op jit(solution)/shard_map/ppermute | solution.py:621
  54.9 4.7 %collective-permute-start.5 = (f32[96,128]{1,0:T(8,128)S(1)}, f32[96,128]{1,0:T(8,128)S(1)}, u32[]{:S(2)}, u32[]{:S(2)}) collective-permute-start(f32[96,128]{1,0:T(8,128)S(1)} %get-tuple-element.38), channel_id=1, source_target_pairs={{0,79},{1,0},{2,1},{3,2},{4,3},{5,4},{6,5},{7,6},{8,7},{9,8},{10,9... | collective-permute-start | bytes 147464 | tf_op jit(solution)/shard_map/ppermute | solution.py:622
  64.4 2.0 %collective-permute-start.6 = (f32[16,128]{1,0:T(8,128)S(1)}, f32[16,128]{1,0:T(8,128)S(1)}, u32[]{:S(2)}, u32[]{:S(2)}) collective-permute-start(f32[16,128]{1,0:T(8,128)S(1)} %get-tuple-element.42), channel_id=1, source_target_pairs={{0,1},{1,2},{2,3},{3,4},{4,5},{5,6},{6,7},{7,8},{8,9},{9,10},{10,1... | collective-permute-start | bytes 24584 | tf_op jit(solution)/shard_map/ppermute | solution.py:621
  64.4 4.3 %collective-permute-start.7 = (f32[16,128]{1,0:T(8,128)S(1)}, f32[16,128]{1,0:T(8,128)S(1)}, u32[]{:S(2)}, u32[]{:S(2)}) collective-permute-start(f32[16,128]{1,0:T(8,128)S(1)} %get-tuple-element.43), channel_id=1, source_target_pairs={{0,79},{1,0},{2,1},{3,2},{4,3},{5,4},{6,5},{7,6},{8,7},{9,8},{10,9... | collective-permute-start | bytes 24584 | tf_op jit(solution)/shard_map/ppermute | solution.py:622
